TPU v7x, 32 devices: a whole 2x2x4 slice. The times are simulated.
32 devices in a mesh: fsdp: 4 (over y, x), expert: 8 (over z, core).
Axes of the slice: x: 2, y: 2, z: 4, core: 2. Of those that a mesh axis runs over, the one named last changes fastest.
Arguments:
- patches: bfloat16 [64, 197, 768], P(('fsdp', 'expert')), may hold values from -6 to 6
- dense_gains: bfloat16 [2, 768], P(None, ('fsdp', 'expert')), may hold values from 0.25 to 1.75
- dense_shifts: bfloat16 [6, 768], P(None, ('fsdp', 'expert')), may hold values from -1.796875 to 1.796875
- dense_qkv: bfloat16 [768, 2304], P(('fsdp', 'expert')), may hold values from -0.3125 to 0.3125
- dense_proj: bfloat16 [768, 768], P(('fsdp', 'expert')), may hold values from -0.75 to 0.75
- dense_fc_in: bfloat16 [768, 3072], P(('fsdp', 'expert')), may hold values from -0.21875 to 0.21875
- dense_fc_bias: bfloat16 [3072], P(('fsdp', 'expert')), may hold values from -1.796875 to 1.796875
- dense_fc_out: bfloat16 [3072, 768], P(('fsdp', 'expert')), may hold values from -0.15625 to 0.15625
- moe_gains: bfloat16 [2, 768], P(None, ('fsdp', 'expert')), may hold values from 0.25 to 1.75
- moe_shifts: bfloat16 [5, 768], P(None, ('fsdp', 'expert')), may hold values from -1.796875 to 1.796875
- moe_qkv: bfloat16 [768, 2304], P(('fsdp', 'expert')), may hold values from -0.3125 to 0.3125
- moe_proj: bfloat16 [768, 768], P(('fsdp', 'expert')), may hold values from -0.75 to 0.75
- router: bfloat16 [768, 8], P(('fsdp', 'expert')), may hold values from -0.15625 to 0.15625
- expert_in: bfloat16 [8, 768, 3072], P('expert', 'fsdp'), may hold values from -0.21875 to 0.21875
- expert_in_bias: bfloat16 [8, 3072], P('expert', 'fsdp'), may hold values from -1.1953125 to 1.1953125
- expert_out: bfloat16 [8, 3072, 768], P('expert', 'fsdp'), may hold values from -0.4375 to 0.4375
- expert_out_bias: bfloat16 [8, 768], P('expert', 'fsdp'), may hold values from -1.796875 to 1.796875
- routes: int32 [64, 197, 2], P(('fsdp', 'expert')), may hold values from 0 to 7, as said below
- slot_pos: int32 [64, 197, 2], P(('fsdp', 'expert')), may hold values from -1 to 93, as said below
- image_counts: int32 [32], P(('fsdp', 'expert')), may hold values from 1 to 2, as said below
- cotangent: bfloat16 [64, 197, 768], P(('fsdp', 'expert')), may hold values from -6 to 6
Outputs:
- output_tokens: bfloat16 [64, 197, 768], P(('fsdp', 'expert'))
- patches_grad: float32 [64, 197, 768], P(('fsdp', 'expert'))
- dense_gains_grad: float32 [2, 768], P(None, ('fsdp', 'expert'))
- dense_shifts_grad: float32 [6, 768], P(None, ('fsdp', 'expert'))
- dense_qkv_grad: float32 [768, 2304], P(('fsdp', 'expert'))
- dense_proj_grad: float32 [768, 768], P(('fsdp', 'expert'))
- dense_fc_in_grad: float32 [768, 3072], P(('fsdp', 'expert'))
- dense_fc_bias_grad: float32 [3072], P(('fsdp', 'expert'))
- dense_fc_out_grad: float32 [3072, 768], P(('fsdp', 'expert'))
- moe_gains_grad: float32 [2, 768], P(None, ('fsdp', 'expert'))
- moe_shifts_grad: float32 [5, 768], P(None, ('fsdp', 'expert'))
- moe_qkv_grad: float32 [768, 2304], P(('fsdp', 'expert'))
- moe_proj_grad: float32 [768, 768], P(('fsdp', 'expert'))
- router_grad: float32 [768, 8], P(('fsdp', 'expert'))
- expert_in_grad: float32 [8, 768, 3072], P('expert', 'fsdp')
- expert_in_bias_grad: float32 [8, 3072], P('expert', 'fsdp')
- expert_out_grad: float32 [8, 3072, 768], P('expert', 'fsdp')
- expert_out_bias_grad: float32 [8, 768], P('expert', 'fsdp')
Inputs may be any that keep to these rules, and one draw needn't show every extreme that they name: `routes`: each token names two different experts. `slot_pos`: within one block of 2 images, the placed entries that name one expert hold distinct slots; entries of images beyond the block's live count are -1, and some live entries are -1 where an expert's slots run out. In every block some expert has all 94 slots filled. A device's live images are its first image_counts image slots.
All inputs are finite; a program needn't handle non-finite values.
Results may differ from a plain program's by a relative error of at most 0.02.
Values may be sent and summed in bfloat16 or wider, within the bound.
No kernel may reach another device: no remote copies, remote signals or barrier semaphores. Data moves between devices by JAX's collectives and lax.ppermute only.
A program may use at most 256 MiB of HBM per device.

v0:
```python
from functools import partial

import jax
import jax.numpy as jnp
from jax import lax
from jax.experimental import pallas as pl
from jax.experimental.pallas import tpu as pltpu
from jax.sharding import PartitionSpec as P

TILE = 256
LOW = jnp.bfloat16
FULL = jnp.float32
eps_norm = 1e-06


def fit(count, step):
    return -(-count // step) * step


def whole(shape):
    return pl.BlockSpec(shape, lambda *at: (0,) * len(shape))


def shape_of(rows, cols, kind):
    return jax.ShapeDtypeStruct((rows, cols), kind)


def run_kernel(kernel, outs, arrays, micros, scalars=(), scratch=(), far=(), grid=None, in_blocks=None, out_blocks=None, ahead=False):
    nbytes = sum(a.size * a.dtype.itemsize for a in list(arrays) + list(far))
    nbytes += sum(o.size * o.dtype.itemsize for o in outs)
    if grid is None:
        in_blocks = [pl.BlockSpec(memory_space=pltpu.VMEM)] * len(arrays)
        out_blocks = [pl.BlockSpec(memory_space=pltpu.VMEM)] * len(outs)
    in_specs = [pl.BlockSpec(memory_space=pltpu.SMEM)] * len(scalars)
    in_specs += list(in_blocks) + [pl.BlockSpec(memory_space=pl.ANY)] * len(far)
    if ahead:
        more = {
            "grid_spec": pltpu.PrefetchScalarGridSpec(
                num_scalar_prefetch=len(scalars),
                grid=grid,
                in_specs=in_specs[len(scalars) :],
                out_specs=list(out_blocks),
                scratch_shapes=list(scratch),
            )
        }
    else:
        more = {
            "in_specs": in_specs,
            "out_specs": list(out_blocks),
            "scratch_shapes": list(scratch),
        }
        if grid is not None:
            more["grid"] = grid
    return pl.pallas_call(
        kernel,
        out_shape=list(outs),
        compiler_params=pltpu.CompilerParams(vmem_limit_bytes=56 * 1024 * 1024),
        cost_estimate=pl.CostEstimate(
            flops=int(micros * 1.15e9), bytes_accessed=nbytes, transcendentals=0
        ),
        **more,
    )(*scalars, *arrays, *far)


def mul(left, right):
    return jnp.dot(left, right, preferred_element_type=FULL)


def mul_turned(left, right):
    return lax.dot_general(left, right, (((1,), (1,)), ((), ())), preferred_element_type=FULL)


def turned_mul(left, right):
    return lax.dot_general(left, right, (((0,), (0,)), ((), ())), preferred_element_type=FULL)


def span(at, size):
    if isinstance(at, int):
        return slice(at * size, (at + 1) * size)
    return pl.ds(pl.multiple_of(at * size, size), size)


def norm_parts(values):
    center = values - jnp.mean(values, axis=-1, keepdims=True)
    spread = jnp.mean(center * center, axis=-1, keepdims=True)
    return center, lax.rsqrt(spread + eps_norm)


def norm_low(values, gain, shift):
    center, scale = norm_parts(values)
    return (center * scale * gain + shift).astype(LOW)


def norm_back(values, gain, upstream):
    center, scale = norm_parts(values)
    unit = center * scale
    inner = upstream * gain
    grad = scale * (
        inner
        - jnp.mean(inner, axis=-1, keepdims=True)
        - unit * jnp.mean(inner * unit, axis=-1, keepdims=True)
    )
    return (
        grad,
        jnp.sum(upstream * unit, axis=0, keepdims=True),
        jnp.sum(upstream, axis=0, keepdims=True),
    )


def gelu_parts(values):
    rate = 0.7978845608028654
    square = values * values
    bend = jnp.tanh(values * (rate + (rate * 0.044715) * square))
    half = 0.5 + 0.5 * bend
    slope = half + (values * (1.0 - bend * bend)) * (0.5 * rate + (1.5 * rate * 0.044715) * square)
    return (values * half).astype(LOW), slope.astype(LOW)


def split_low(values):
    high = values.astype(LOW)
    return high, (values - high.astype(FULL)).astype(LOW)


def head_masks():
    lane = lax.broadcasted_iota(jnp.int32, (1, 128), 1)
    first = (lane < 64).astype(FULL)
    return first, 1.0 - first


def near_copies(place_ref, own_ref, other_ref, target, sems):
    plane, side = place_ref[0], place_ref[1]
    count = sems.shape[0] // 2
    half_cols = own_ref.shape[1]
    lines = own_ref.shape[0] // count
    copies = []
    for core, source in enumerate((own_ref, other_ref)):
        cols = pl.ds(pl.multiple_of((side if core == 0 else 1 - side) * half_cols, 128), half_cols)
        for mask in range(count):
            start = pl.multiple_of((plane ^ mask) * lines, lines)
            copies.append(
                pltpu.make_async_copy(
                    source.at[pl.ds(mask * lines, lines), :],
                    target.at[pl.ds(start, lines), cols],
                    sems.at[core * count + mask],
                )
            )
    return copies


def pack_copies(pack_ref, target, sems):
    groups, cores, lines, wide = pack_ref.shape
    half_cols = target.shape[1] // cores
    return [
        pltpu.make_async_copy(
            pack_ref.at[group, core, :, wide - half_cols : wide],
            target.at[span(group, lines), span(core, half_cols)],
            sems.at[group * cores + core],
        )
        for group in range(groups)
        for core in range(cores)
    ]


def score_parts(query, key, mask, keep):
    scores = mul_turned(query * (0.125 * mask).astype(LOW), key)
    scores = jnp.where(keep, scores, -1e30)
    raised = jnp.exp(scores - jnp.max(scores, axis=-1, keepdims=True))
    return raised * (1.0 / jnp.sum(raised, axis=-1, keepdims=True))


def attend_forward_kernel(length, images, lines_of, own, experts, *refs):
    if own:
        (
            place_ref, x_ref, near_ref, other_ref,
            an_ref, qkv_ref, o_ref, out_ref, vec_ref, wide_ref, router_ref, w_ref, sems,
        ) = refs
        copies = near_copies(place_ref, near_ref, other_ref, w_ref, sems)
    else:
        place_ref, x_ref, vec_ref, pack_ref, an_ref, qkv_ref, o_ref, out_ref, w_ref, sems = refs
        copies = pack_copies(pack_ref, w_ref, sems)
    gain, shift, q_line, v_line, o_line = lines_of
    for copy in copies:
        copy.start()
    rows, width = x_ref.shape
    block = rows // images
    pairs = width // 128
    for copy in copies:
        copy.wait()
    if own:
        small = w_ref[:, 4 * width : 4 * width + 128]
        turned = small.astype(FULL).T
        vec_ref[...] = turned[0:32, :]
        spot = lax.broadcasted_iota(jnp.int32, (128, 128), 0) - lax.broadcasted_iota(
            jnp.int32, (128, 128), 1
        )
        lane = lax.broadcasted_iota(jnp.int32, (128, 128), 1)
        pick = jnp.where((spot == 15) & (lane < experts), 1.0, 0.0).astype(LOW)
        router_ref[...] = mul(small, pick).astype(LOW)
        depth = wide_ref.shape[1] // width
        near = lax.broadcasted_iota(jnp.int32, (128, 128 * depth), 0)
        place = lax.broadcasted_iota(jnp.int32, (128, 128 * depth), 1)
        spread = jnp.where(place // depth == near, 1.0, 0.0).astype(LOW)
        line = lax.broadcasted_iota(jnp.int32, (128, 128 * depth), 0)
        for at in range(width // 128):
            many = mul(turned[:, span(at, 128)].astype(LOW), spread)
            keep_line = line == place % depth + 15 + experts
            wide_ref[:, span(at, 128 * depth)] = jnp.sum(
                jnp.where(keep_line, many, 0.0), axis=0, keepdims=True
            )
    an_ref[...] = norm_low(x_ref[...], vec_ref[gain : gain + 1, :], vec_ref[shift : shift + 1, :])
    for at in range(3 * width // TILE):
        part = mul(an_ref[...], w_ref[:, span(at, TILE)])
        here = (at * TILE) % width
        if at * TILE < width:
            part = part + vec_ref[q_line : q_line + 1, here : here + TILE]
        elif at * TILE >= 2 * width:
            part = part + vec_ref[v_line : v_line + 1, here : here + TILE]
        qkv_ref[:, span(at, TILE)] = part.astype(LOW)

    first, second = head_masks()
    keep = lax.broadcasted_iota(jnp.int32, (1, block), 1) < length
    for image in range(images):
        for pair in range(pairs):
            lines = span(image, block)
            query = qkv_ref[lines, span(pair, 128)]
            key = qkv_ref[lines, span(pair + pairs, 128)]
            value = qkv_ref[lines, span(pair + 2 * pairs, 128)]
            mixed = [
                mul(score_parts(query, key, mask, keep).astype(LOW), value)
                for mask in (first, second)
            ]
            o_ref[lines, span(pair, 128)] = (mixed[0] * first + mixed[1] * second).astype(LOW)

    for at in range(width // TILE):
        cols = span(at, TILE)
        weight = w_ref[:, 3 * width + at * TILE : 3 * width + (at + 1) * TILE]
        out_ref[:, cols] = x_ref[:, cols] + (
            mul(o_ref[...], weight) + vec_ref[o_line : o_line + 1, cols]
        )


def weight_scratch(width, pieces, planes):
    if len(pieces) == 2:
        cols, count = 2 * pieces[0].shape[1], 2 * planes
    else:
        cols, count = 4 * width, pieces[0].shape[0] * pieces[0].shape[1]
    return [pltpu.VMEM((width, cols), LOW), pltpu.SemaphoreType.DMA((count,))]


def attend_forward(place, x, vec, pieces, planes, lines_of, length, images, experts, inner):
    rows, width = x.shape
    outs = [
        shape_of(rows, width, LOW),
        shape_of(rows, 3 * width, LOW),
        shape_of(rows, width, LOW),
        shape_of(rows, width, FULL),
    ]
    own = vec is None
    if own:
        outs += [shape_of(32, width, FULL), shape_of(1, inner, FULL), shape_of(width, 128, LOW)]
    return run_kernel(
        partial(attend_forward_kernel, length, images, lines_of, own, experts),
        outs,
        [x] if own else [x, vec],
        11,
        scalars=[place],
        far=pieces,
        scratch=weight_scratch(width, pieces, planes),
    )


def attend_backward_kernel(length, images, lines_of, own, experts, place_ref, up_ref, x_ref, vec_ref, qkv_ref, *refs):
    gain = lines_of[0]
    if own:
        (
            feed_ref, moe_ref, gate_ref, wide_ref, router_ref, near_ref, other_ref,
            din_ref, mine_ref, away_ref, low_mine_ref, low_away_ref, small_ref,
            dol_ref, mix_ref, grad_ref, sums_ref, w_ref, sems,
        ) = refs
        copies = near_copies(place_ref, near_ref, other_ref, w_ref, sems)
    else:
        (
            pack_ref, din_ref, mine_ref, away_ref, low_mine_ref, low_away_ref, sums_ref,
            dol_ref, mix_ref, grad_ref, w_ref, sems,
        ) = refs
        copies = pack_copies(pack_ref, w_ref, sems)
    for copy in copies:
        copy.start()
    rows, width = x_ref.shape
    block = rows // images
    pairs = width // 128
    side = place_ref[1]
    dol_ref[...] = up_ref[...].astype(LOW)
    for copy in copies:
        copy.wait()
    for at in range(width // TILE):
        cols = span(at, TILE)
        mix_ref[:, cols] = mul_turned(dol_ref[...], w_ref[cols, 3 * width : 4 * width]).astype(LOW)

    first, second = head_masks()
    keep = lax.broadcasted_iota(jnp.int32, (block, 1), 0) < length
    for image in range(images):
        for pair in range(pairs):
            lines = span(image, block)
            query = qkv_ref[lines, span(pair, 128)]
            key = qkv_ref[lines, span(pair + pairs, 128)]
            value = qkv_ref[lines, span(pair + 2 * pairs, 128)]
            mix = mix_ref[lines, span(pair, 128)]
            grads = []
            for mask in (first, second):
                scores = mul_turned(key * (0.125 * mask).astype(LOW), query)
                scores = jnp.where(keep, scores, -1e30)
                raised = jnp.exp(scores - jnp.max(scores, axis=0, keepdims=True))
                prob = raised * (1.0 / jnp.sum(raised, axis=0, keepdims=True))
                slope = mul_turned(value * mask.astype(LOW), mix)
                inner = jnp.sum(slope * prob, axis=0, keepdims=True)
                change = (prob * (slope - inner)).astype(LOW)
                grads.append(
                    (turned_mul(change, key), mul(change, query), mul(prob.astype(LOW), mix))
                )
            for part, rate in ((0, 0.125), (1, 0.125), (2, 1.0)):
                both = grads[0][part] * (rate * first) + grads[1][part] * (rate * second)
                grad_ref[lines, span(pair + part * pairs, 128)] = both.astype(LOW)

    for at in range(width // TILE):
        cols = span(at, TILE)
        din_ref[:, cols] = mul_turned(grad_ref[...], w_ref[cols, 0 : 3 * width])

    grad, gain_sum, shift_sum = norm_back(x_ref[...], vec_ref[gain : gain + 1, :], din_ref[...])
    din_ref[...] = up_ref[...] + grad
    sums_ref[0:1, :] = gain_sum
    sums_ref[1:2, :] = shift_sum
    sums_ref[2:3, :] = jnp.sum(grad_ref[:, 0:width].astype(FULL), axis=0, keepdims=True)
    sums_ref[3:4, :] = jnp.sum(
        grad_ref[:, 2 * width : 3 * width].astype(FULL), axis=0, keepdims=True
    )
    sums_ref[4:5, :] = jnp.sum(dol_ref[...].astype(FULL), axis=0, keepdims=True)
    sums_ref[5:8, :] = jnp.zeros((3, width), FULL)
    mine_ref[...] = grad_ref[:, span(side, 3 * width // 2)]
    away_ref[...] = grad_ref[:, span(1 - side, 3 * width // 2)]
    low_mine_ref[...] = dol_ref[:, span(side, width // 2)]
    low_away_ref[...] = dol_ref[:, span(1 - side, width // 2)]
    if not own:
        return
    depth = wide_ref.shape[1] // width
    line = lax.broadcasted_iota(jnp.int32, (8, 128 * depth), 0)
    place = lax.broadcasted_iota(jnp.int32, (8, 128 * depth), 1)
    near = lax.broadcasted_iota(jnp.int32, (128 * depth, 128), 1)
    spot = lax.broadcasted_iota(jnp.int32, (128 * depth, 128), 0)
    collect = jnp.where(spot // depth == near, 1.0, 0.0).astype(LOW)
    pieces = []
    for at in range(width // 128):
        many = jnp.where(place % depth == line, wide_ref[:, span(at, 128 * depth)], 0.0)
        high, rest = split_low(many)
        pieces.append(mul(high, collect) + mul(rest, collect))
    wide_rows = jnp.concatenate(pieces, axis=1)
    order = (
        (sums_ref, 0), (feed_ref, 0), (sums_ref, 1), (feed_ref, 1), (sums_ref, 2), (sums_ref, 3),
        (sums_ref, 4), (feed_ref, 2), (moe_ref, 0), (gate_ref, 0), (moe_ref, 1), (gate_ref, 1),
        (moe_ref, 2), (moe_ref, 3), (moe_ref, 4),
    )
    row = lax.broadcasted_iota(jnp.int32, (128, 1), 0)
    total = jnp.zeros((128, width), FULL)
    for at, (source, spot_line) in enumerate(order):
        total = jnp.where(row == at, source[spot_line : spot_line + 1, :], total)
    for at in range(depth):
        total = jnp.where(row == 15 + experts + at, wide_rows[at : at + 1, :], total)
    small_ref[...] = total.T + router_ref[...]


def attend_backward(place, up, x, vec, qkv, pieces, planes, gain, length, images, experts=0, more=()):
    rows, width = x.shape
    own = len(more) > 0
    return run_kernel(
        partial(attend_backward_kernel, length, images, (gain,), own, experts),
        [
            shape_of(rows, width, FULL),
            shape_of(rows, 3 * width // 2, LOW),
            shape_of(rows, 3 * width // 2, LOW),
            shape_of(rows, width // 2, LOW),
            shape_of(rows, width // 2, LOW),
            shape_of(width, 128, FULL) if own else shape_of(8, width, FULL),
        ],
        [up, x, vec, qkv] + list(more),
        19,
        scalars=[place],
        far=pieces,
        scratch=[
            pltpu.VMEM((rows, width), LOW),
            pltpu.VMEM((rows, width), LOW),
            pltpu.VMEM((rows, 3 * width), LOW),
        ]
        + ([pltpu.VMEM((8, width), FULL)] if own else [])
        + weight_scratch(width, pieces, planes),
    )


def unfold(source, target):
    groups, _, lines, wide = source.shape
    width = target.shape[1]
    fold = wide // width
    for group in range(groups):
        for at in range(fold):
            start = (group * fold + at) * lines
            target[start : start + lines, :] = source[group, 0, :, span(at, width)]


def feed_forward_kernel(
    lines_of, x_ref, vec_ref, bias_ref, in_ref, pack_ref, hn_ref, act_ref, slope_ref, out_ref, out_w_ref
):
    gain, shift, last = lines_of
    step = pl.program_id(0)

    @pl.when(step == 0)
    def _():
        hn_ref[...] = norm_low(
            x_ref[...], vec_ref[gain : gain + 1, :], vec_ref[shift : shift + 1, :]
        )
        out_ref[...] = x_ref[...] + vec_ref[last : last + 1, :]

    unfold(pack_ref, out_w_ref)
    for at in range(act_ref.shape[1] // TILE):
        cols = span(at, TILE)
        weight = in_ref[:, 0, :, cols].reshape(x_ref.shape[1], TILE)
        act, slope = gelu_parts(mul(hn_ref[...], weight) + bias_ref[:, cols])
        act_ref[:, cols] = act
        slope_ref[:, cols] = slope
    for at in range(out_ref.shape[1] // TILE):
        cols = span(at, TILE)
        out_ref[:, cols] += mul(act_ref[...], out_w_ref[:, cols])


def pack_blocks(pack, part, inner):
    groups, _, lines, _ = pack.shape
    return [
        pl.BlockSpec((groups, 1, lines, part), lambda at: (0, 0, 0, at)),
        pl.BlockSpec((part * groups // inner, 1, lines, inner), lambda at: (at, 1, 0, 0)),
    ]


def feed_forward(x, vec, bias, pack, lines_of):
    rows, width = x.shape
    inner = bias.shape[1]
    part = 768
    return run_kernel(
        partial(feed_forward_kernel, lines_of),
        [
            shape_of(rows, width, LOW),
            shape_of(rows, inner, LOW),
            shape_of(rows, inner, LOW),
            shape_of(rows, width, FULL),
        ],
        [x, vec, bias, pack, pack],
        11,
        scratch=[pltpu.VMEM((part, width), LOW)],
        grid=(inner // part,),
        in_blocks=[
            whole((rows, width)),
            whole(vec.shape),
            pl.BlockSpec((1, part), lambda at: (0, at)),
        ]
        + pack_blocks(pack, part, inner),
        out_blocks=[
            whole((rows, width)),
            pl.BlockSpec((rows, part), lambda at: (0, at)),
            pl.BlockSpec((rows, part), lambda at: (0, at)),
            whole((rows, width)),
        ],
    )


def feed_backward_kernel(
    gain, place_ref, up_ref, x_ref, vec_ref, slope_ref, in_ref, pack_ref,
    down_ref, mine_ref, away_ref, low_mine_ref, low_away_ref, sums_ref, bias_ref,
    dml_ref, du_ref, out_w_ref,
):
    step = pl.program_id(0)
    last = pl.num_programs(0) - 1
    width = x_ref.shape[1]
    part_cols = slope_ref.shape[1]

    @pl.when(step == 0)
    def _():
        dml_ref[...] = up_ref[...].astype(LOW)
        down_ref[...] = jnp.zeros(down_ref.shape, FULL)

    unfold(pack_ref, out_w_ref)
    for at in range(part_cols // TILE):
        cols = span(at, TILE)
        part = (
            mul_turned(dml_ref[...], out_w_ref[cols, :]) * slope_ref[:, cols].astype(FULL)
        ).astype(LOW)
        du_ref[step, :, cols] = part
        bias_ref[:, cols] = jnp.sum(part.astype(FULL), axis=0, keepdims=True)
    groups = in_ref.shape[0] // 2
    for at in range(2):
        weight = in_ref[span(at, groups), 0, :, :].reshape(width // 2, part_cols)
        down_ref[:, span(at, width // 2)] += mul_turned(du_ref[step, :, :], weight)

    @pl.when(step == last)
    def _():
        side = place_ref[1]
        grad, gain_sum, shift_sum = norm_back(x_ref[...], vec_ref[gain : gain + 1, :], down_ref[...])
        down_ref[...] = up_ref[...] + grad
        sums_ref[0:1, :] = gain_sum
        sums_ref[1:2, :] = shift_sum
        sums_ref[2:3, :] = jnp.sum(dml_ref[...].astype(FULL), axis=0, keepdims=True)
        sums_ref[3:8, :] = jnp.zeros((5, width), FULL)
        half = du_ref.shape[0] // 2
        for at in range(half):
            mine_ref[:, span(at, part_cols)] = du_ref[side * half + at, :, :]
            away_ref[:, span(at, part_cols)] = du_ref[(1 - side) * half + at, :, :]
        low_mine_ref[...] = dml_ref[:, span(side, width // 2)]
        low_away_ref[...] = dml_ref[:, span(1 - side, width // 2)]


def feed_backward(place, up, x, vec, slope, pack, gain):
    rows, width = x.shape
    inner = slope.shape[1]
    part = 768
    return run_kernel(
        partial(feed_backward_kernel, gain),
        [
            shape_of(rows, width, FULL),
            shape_of(rows, inner // 2, LOW),
            shape_of(rows, inner // 2, LOW),
            shape_of(rows, width // 2, LOW),
            shape_of(rows, width // 2, LOW),
            shape_of(8, width, FULL),
            shape_of(1, inner, FULL),
        ],
        [up, x, vec, slope, pack, pack],
        13,
        scalars=[place],
        scratch=[
            pltpu.VMEM((rows, width), LOW),
            pltpu.VMEM((inner // part, rows, part), LOW),
            pltpu.VMEM((part, width), LOW),
        ],
        grid=(inner // part,),
        in_blocks=[
            whole((rows, width)),
            whole((rows, width)),
            whole(vec.shape),
            pl.BlockSpec((rows, part), lambda at: (0, at)),
        ]
        + pack_blocks(pack, part, inner),
        out_blocks=[
            whole((rows, width)),
            whole((rows, inner // 2)),
            whole((rows, inner // 2)),
            whole((rows, width // 2)),
            whole((rows, width // 2)),
            whole((8, width)),
            pl.BlockSpec((1, part), lambda at: (0, at)),
        ],
    )


def product_kernel(counts, *refs):
    out_ref = refs[-1]
    start = 0
    at_ref = 0
    for count in counts:
        size = refs[at_ref + 1].shape[1]
        total = turned_mul(refs[at_ref][...], refs[at_ref + 1][...])
        for more in range(1, count):
            total += turned_mul(refs[at_ref + 2 * more][...], refs[at_ref + 2 * more + 1][...])
        out_ref[:, start : start + size] = total.astype(LOW)
        start += size
        at_ref += 2 * count
    if at_ref < len(refs) - 1:
        extra = refs[at_ref]
        out_ref[:, start : start + extra.shape[1]] = extra[...].astype(LOW)


def products(groups, extra=None, part=256):
    counts = [len(group) for group in groups]
    arrays = [array for group in groups for pair in group for array in pair]
    blocks = []
    for group in groups:
        for left, right in group:
            blocks += [pl.BlockSpec((left.shape[0], part), lambda at: (0, at)), whole(right.shape)]
    cols = sum(group[0][1].shape[1] for group in groups)
    if extra is not None:
        arrays.append(extra)
        blocks.append(pl.BlockSpec((part, extra.shape[1]), lambda at: (at, 0)))
        cols += extra.shape[1]
    lines = groups[0][0][0].shape[1]
    return run_kernel(
        partial(product_kernel, counts),
        [shape_of(lines, cols, LOW)],
        arrays,
        7,
        grid=(lines // part,),
        in_blocks=blocks,
        out_blocks=[pl.BlockSpec((part, cols), lambda at: (at, 0))],
    )[0]


def one_hot_rows(target, slots):
    hit = lax.broadcasted_iota(jnp.int32, (slots, target.shape[1]), 0) == target
    return jnp.where(hit, 1.0, 0.0).astype(LOW)


def one_hot_cols(target, slots):
    hit = lax.broadcasted_iota(jnp.int32, (target.shape[0], slots), 1) == target
    return jnp.where(hit, 1.0, 0.0).astype(LOW)


def dispatch_kernel(
    experts, lines_of, x_ref, vec_ref, router_ref, route_ref, target_ref, up_ref,
    mn_ref, gate_ref, pick_ref, out_ref, grad_ref, spot_ref, low_ref,
):
    gain, shift = lines_of
    slots = out_ref.shape[0]
    mn_ref[...] = norm_low(x_ref[...], vec_ref[gain : gain + 1, :], vec_ref[shift : shift + 1, :])
    logits = mul(mn_ref[...], router_ref[...])
    lane = lax.broadcasted_iota(jnp.int32, logits.shape, 1)
    logits = jnp.where(lane < experts, logits, -1e30)
    raised = jnp.exp(logits - jnp.max(logits, axis=-1, keepdims=True))
    gate = raised / jnp.sum(raised, axis=-1, keepdims=True)
    gate_ref[...] = gate
    picks = [
        jnp.sum(jnp.where(lane == route_ref[:, k : k + 1], gate, 0.0), axis=-1, keepdims=True)
        for k in range(2)
    ]
    pick_ref[...] = jnp.where(lane == 0, picks[0], jnp.where(lane == 1, picks[1], 0.0))
    spots = [one_hot_rows(target_ref[k : k + 1, :], slots) for k in range(2)]
    spot_ref[0, :, :] = spots[0]
    spot_ref[1, :, :] = spots[1]
    low_ref[0, :, :] = (picks[0] * up_ref[...].astype(FULL)).astype(LOW)
    low_ref[1, :, :] = (picks[1] * up_ref[...].astype(FULL)).astype(LOW)
    for at in range(out_ref.shape[1] // TILE):
        cols = span(at, TILE)
        out_ref[:, cols] = mul(spot_ref[0, :, :] + spot_ref[1, :, :], mn_ref[:, cols]).astype(LOW)
        grad_ref[:, cols] = (
            mul(spot_ref[0, :, :], low_ref[0, :, cols]) + mul(spot_ref[1, :, :], low_ref[1, :, cols])
        ).astype(LOW)


def dispatch(x, vec, router, routes, targets, up, experts, slots, lines_of):
    rows, width = x.shape
    return run_kernel(
        partial(dispatch_kernel, experts, lines_of),
        [
            shape_of(rows, width, LOW),
            shape_of(rows, 128, FULL),
            shape_of(rows, 128, FULL),
            shape_of(slots, width, LOW),
            shape_of(slots, width, LOW),
        ],
        [x, vec, router, routes, targets, up],
        6,
        scratch=[pltpu.VMEM((2, slots, rows), LOW), pltpu.VMEM((2, rows, width), LOW)],
    )


def restore(place_ref, source, target):
    planes, lines, _ = target.shape
    for mask in range(planes):
        target[place_ref[0] ^ mask, :, :] = source[mask * lines : (mask + 1) * lines, :]


def unfold_lines(place_ref, source, target, lines):
    width = target.shape[1]
    fold = source.shape[1] // width
    many = source.shape[0] // lines
    for mask in range(many):
        group = mask ^ (place_ref[0] % many)
        for at in range(fold):
            start = pl.multiple_of((group * fold + at) * lines, lines)
            target[pl.ds(start, lines), :] = source[
                mask * lines : (mask + 1) * lines, span(at, width)
            ]


def hidden_kernel(place_ref, x_ref, bias_ref, pack_ref, act_ref, slope_ref, w_ref):
    restore(place_ref, pack_ref, w_ref)
    for at in range(act_ref.shape[1] // TILE):
        cols = span(at, TILE)
        weight = w_ref[:, :, cols].reshape(x_ref.shape[1], TILE)
        act, slope = gelu_parts(mul(x_ref[...], weight) + bias_ref[:, cols])
        act_ref[:, cols] = act
        slope_ref[:, cols] = slope


def hidden_forward(place, x, bias, weight, planes):
    rows, width = x.shape
    inner = bias.shape[1]
    part = 768
    return run_kernel(
        hidden_kernel,
        [shape_of(rows, inner, LOW), shape_of(rows, inner, LOW)],
        [x, bias, weight],
        11,
        scalars=[place],
        scratch=[pltpu.VMEM((planes, width // planes, part), LOW)],
        grid=(inner // part,),
        in_blocks=[
            whole(x.shape),
            pl.BlockSpec((1, part), lambda at: (0, at)),
            pl.BlockSpec((width, part), lambda at: (0, at)),
        ],
        out_blocks=[pl.BlockSpec((rows, part), lambda at: (0, at))] * 2,
    )


def expert_out_kernel(lines, place_ref, act_ref, bias_ref, pack_ref, out_ref, sum_ref, w_ref):
    step = pl.program_id(0)
    unfold_lines(place_ref, pack_ref, w_ref, lines)

    @pl.when(step == 0)
    def _():
        sum_ref[...] = jnp.zeros(sum_ref.shape, FULL) + bias_ref[...]

    for at in range(w_ref.shape[1] // TILE):
        cols = span(at, TILE)
        sum_ref[:, cols] += mul(act_ref[...], w_ref[:, cols])

    @pl.when(step == pl.num_programs(0) - 1)
    def _():
        out_ref[...] = sum_ref[...].astype(LOW)


def expert_out_forward(place, act, bias, weight, lines):
    rows, width = act.shape[0], weight.shape[0]
    inner = act.shape[1]
    part = 768
    many = part * width // (inner * lines)
    return run_kernel(
        partial(expert_out_kernel, lines),
        [shape_of(rows, width, LOW)],
        [act, bias, weight],
        8,
        scalars=[place],
        scratch=[pltpu.VMEM((rows, width), FULL), pltpu.VMEM((part, width), LOW)],
        grid=(inner // part,),
        in_blocks=[
            pl.BlockSpec((rows, part), lambda at, place: (0, at ^ (place[0] // many))),
            pl.BlockSpec(bias.shape, lambda at, place: (0, 0)),
            pl.BlockSpec((many * lines, inner), lambda at, place: (at, 1)),
        ],
        out_blocks=[pl.BlockSpec((rows, width), lambda at, place: (0, 0))],
        ahead=True,
    )[0]


def expert_backward_kernel(
    lines, place_ref, dy_ref, slope_ref, pack_ref, in_ref,
    dh_ref, bias_ref, last_ref, back_ref, sum_ref, out_w_ref, in_w_ref,
):
    step = pl.program_id(0)
    unfold_lines(place_ref, pack_ref, out_w_ref, lines)
    restore(place_ref, in_ref, in_w_ref)

    @pl.when(step == 0)
    def _():
        sum_ref[...] = jnp.zeros(sum_ref.shape, FULL)
        last_ref[...] = jnp.sum(dy_ref[...].astype(FULL), axis=0, keepdims=True)

    for at in range(slope_ref.shape[1] // TILE):
        cols = span(at, TILE)
        part = (
            mul_turned(dy_ref[...], out_w_ref[cols, :]) * slope_ref[:, cols].astype(FULL)
        ).astype(LOW)
        dh_ref[:, cols] = part
        bias_ref[:, cols] = jnp.sum(part.astype(FULL), axis=0, keepdims=True)
    planes, lines, part_cols = in_w_ref.shape
    for at in range(2):
        weight = in_w_ref[span(at, planes // 2), :, :].reshape(planes * lines // 2, part_cols)
        sum_ref[:, span(at, planes * lines // 2)] += mul_turned(dh_ref[...], weight)

    @pl.when(step == pl.num_programs(0) - 1)
    def _():
        back_ref[...] = sum_ref[...].astype(LOW)


def expert_backward(place, dy, slope, weight, lines):
    rows, width = dy.shape
    inner = slope.shape[1]
    part = 768
    many = part * width // (inner * lines)

    def moved(at, place):
        return (0, at ^ (place[0] // many))

    def fixed(at, place):
        return (0, 0)

    return run_kernel(
        partial(expert_backward_kernel, lines),
        [
            shape_of(rows, inner, LOW),
            shape_of(1, inner, FULL),
            shape_of(1, width, FULL),
            shape_of(rows, width, LOW),
        ],
        [dy, slope, weight, weight],
        14,
        scalars=[place],
        scratch=[
            pltpu.VMEM((rows, width), FULL),
            pltpu.VMEM((part, width), LOW),
            pltpu.VMEM((width // lines, lines, part), LOW),
        ],
        grid=(inner // part,),
        in_blocks=[
            pl.BlockSpec(dy.shape, fixed),
            pl.BlockSpec((rows, part), moved),
            pl.BlockSpec((many * lines, inner), lambda at, place: (at, 1)),
            pl.BlockSpec((width, part), moved),
        ],
        out_blocks=[
            pl.BlockSpec((rows, part), moved),
            pl.BlockSpec((1, part), moved),
            pl.BlockSpec((1, width), fixed),
            pl.BlockSpec((rows, width), fixed),
        ],
        ahead=True,
    )


def combine_kernel(
    x_ref, home_ref, gate_ref, pick_ref, route_ref, target_ref, up_ref, live_ref, mn_ref, router_ref,
    out_ref, part_ref, router_grad_ref, spot_ref, dot_ref,
):
    rows, width = x_ref.shape
    slots = home_ref.shape[0]
    for k in range(2):
        spot_ref[k, :, :] = one_hot_cols(target_ref[:, k : k + 1], slots)
    lane = lax.broadcasted_iota(jnp.int32, (rows, 128), 1)
    dot_ref[...] = jnp.zeros((rows, 128), FULL)

    @pl.loop(0, width // TILE)
    def _(at):
        cols = span(at, TILE)
        up = up_ref[:, cols].astype(FULL)
        total = x_ref[:, cols]
        for k in range(2):
            fetched = mul(spot_ref[k, :, :], home_ref[:, cols])
            total += pick_ref[:, k : k + 1] * fetched
            dot_ref[...] += jnp.where(lane == k, jnp.sum(up * fetched, axis=-1, keepdims=True), 0.0)
        out_ref[:, cols] = (total * live_ref[...]).astype(LOW)

    gate = gate_ref[...]
    spread = jnp.zeros((rows, 128), FULL)
    for k in range(2):
        spread += jnp.where(lane == route_ref[:, k : k + 1], dot_ref[:, k : k + 1], 0.0)
    logit = gate * (spread - jnp.sum(gate * spread, axis=-1, keepdims=True))
    high, rest = split_low(pltpu.roll(logit, 15, 1))
    router_grad_ref[...] = turned_mul(mn_ref[...], high) + turned_mul(mn_ref[...], rest)
    high, rest = split_low(logit)
    part_ref[...] = mul_turned(high, router_ref[...]) + mul_turned(rest, router_ref[...])


def combine(x, home, gate, pick, routes, targets, up, live, mn, router):
    rows, width = x.shape
    slots = home.shape[0]
    return run_kernel(
        combine_kernel,
        [shape_of(rows, width, LOW), shape_of(rows, width, FULL), shape_of(width, 128, FULL)],
        [x, home, gate, pick, routes, targets, up, live, mn, router],
        8,
        scratch=[pltpu.VMEM((2, rows, slots), LOW), pltpu.VMEM((rows, 128), FULL)],
    )


def return_kernel(gain, x_ref, vec_ref, part_ref, home_ref, target_ref, up_ref, out_ref, sums_ref, spot_ref):
    width = x_ref.shape[1]
    slots = home_ref.shape[0]
    spot_ref[...] = one_hot_cols(target_ref[:, 0:1], slots) + one_hot_cols(target_ref[:, 1:2], slots)
    for at in range(width // TILE):
        cols = span(at, TILE)
        out_ref[:, cols] = part_ref[:, cols] + mul(spot_ref[...], home_ref[:, cols])

    grad, gain_sum, shift_sum = norm_back(x_ref[...], vec_ref[gain : gain + 1, :], out_ref[...])
    out_ref[...] = up_ref[...].astype(FULL) + grad
    sums_ref[0:1, :] = gain_sum
    sums_ref[1:2, :] = shift_sum
    sums_ref[2:8, :] = jnp.zeros((6, width), FULL)


def return_grad(x, vec, part, home, targets, up, gain):
    rows, width = x.shape
    slots = home.shape[0]
    return run_kernel(
        partial(return_kernel, gain),
        [shape_of(rows, width, FULL), shape_of(8, width, FULL)],
        [x, vec, part, home, targets, up],
        5,
        scratch=[pltpu.VMEM((rows, slots), LOW)],
    )


def feed_products_kernel(lines, fold, hn_ref, hn_far_ref, du_ref, du_far_ref, act_ref, act_far_ref, low_ref, low_far_ref, out_ref):
    cols = du_ref.shape[1] // fold
    tall = 2 * fold * lines
    tile = hn_ref.shape[1]
    for at in range(fold):
        part = turned_mul(hn_ref[...], du_ref[:, span(at, cols)])
        part += turned_mul(hn_far_ref[...], du_far_ref[:, span(at, cols)])
        part = part.astype(LOW)
        for spot in range(tile // lines):
            start = spot * tall + at * lines
            out_ref[start : start + lines, :] = part[spot * lines : (spot + 1) * lines, :]
    for at in range(act_ref.shape[1] // tile):
        part = turned_mul(act_ref[:, span(at, tile)], low_ref[...])
        part += turned_mul(act_far_ref[:, span(at, tile)], low_far_ref[...])
        part = part.astype(LOW)
        size = fold * lines
        for spot in range(tile // size):
            start = (at * (tile // size) + spot) * tall + size
            out_ref[start : start + size, :] = part[spot * size : (spot + 1) * size, :]


def feed_products(hn, hn_far, du, du_far, act, act_far, low, low_far, blocks, fold):
    rows, width = hn.shape
    lines = width // blocks
    tall = 2 * fold * lines
    steps = 2
    left = pl.BlockSpec((rows, width // steps), lambda at: (0, at))
    wide = pl.BlockSpec((rows, fold * width // steps), lambda at: (0, at))
    return run_kernel(
        partial(feed_products_kernel, lines, fold),
        [shape_of(blocks * tall, low.shape[1], LOW)],
        [hn, hn_far, du, du_far, act, act_far, low, low_far],
        11,
        grid=(steps,),
        in_blocks=[left, left, whole(du.shape), whole(du.shape), wide, wide, whole(low.shape), whole(low.shape)],
        out_blocks=[pl.BlockSpec((blocks * tall // steps, low.shape[1]), lambda at: (at, 0))],
    )[0]


def expert_products_kernel(lines, fold, x_ref, dh_ref, act_ref, dy_ref, out_ref):
    width = dy_ref.shape[1]
    tile = x_ref.shape[1]
    for at in range(fold):
        part = turned_mul(x_ref[...], dh_ref[:, span(at, width)]).astype(LOW)
        for spot in range(tile // lines):
            start = 2 * spot * lines
            out_ref[start : start + lines, span(at, width)] = part[spot * lines : (spot + 1) * lines, :]
    for at in range(fold):
        part = turned_mul(act_ref[:, span(at, tile)], dy_ref[...]).astype(LOW)
        for spot in range(tile // lines):
            group = at * (tile // lines) + spot
            start = (2 * (group // fold) + 1) * lines
            out_ref[start : start + lines, span(group % fold, width)] = part[
                spot * lines : (spot + 1) * lines, :
            ]


def expert_products(x, dh, act, dy, planes):
    slots, width = x.shape
    fold = dh.shape[1] // width
    steps = 2
    return run_kernel(
        partial(expert_products_kernel, width // planes, fold),
        [shape_of(2 * width, fold * width, LOW)],
        [x, dh, act, dy],
        14,
        grid=(steps,),
        in_blocks=[
            pl.BlockSpec((slots, width // steps), lambda at: (0, at)),
            whole(dh.shape),
            pl.BlockSpec((slots, fold * width // steps), lambda at: (0, at)),
            whole(dy.shape),
        ],
        out_blocks=[pl.BlockSpec((2 * width // steps, fold * width), lambda at: (at, 0))],
    )[0]


tie = lax.optimization_barrier


def trade(value, axis_name, mask):
    count = lax.axis_size(axis_name)
    return lax.ppermute(value, axis_name, [(place, place ^ mask) for place in range(count)])


def in_order(pieces, place):
    level = 0
    while len(pieces) > 1:
        flip = ((place >> level) & 1) == 1
        pieces = [
            jnp.where(
                flip,
                jnp.concatenate([pieces[at + 1], pieces[at]], axis=0),
                jnp.concatenate([pieces[at], pieces[at + 1]], axis=0),
            )
            for at in range(0, len(pieces), 2)
        ]
        level += 1
    return pieces[0]


def core_side():
    return lax.axis_index("expert") % 2


def core_half(shard):
    side = core_side()
    half = shard.shape[1] // 2
    mine = lax.dynamic_slice_in_dim(shard, side * half, half, 1)
    away = lax.dynamic_slice_in_dim(shard, (1 - side) * half, half, 1)
    return in_order([mine, trade(away, "expert", 1)], side)


def layer_gather(shard):
    layers = lax.axis_size("expert") // 2
    stacked = [shard] + [trade(shard, "expert", 2 * mask) for mask in range(1, layers)]
    return in_order(stacked, lax.axis_index("expert") // 2)


def plane_near(piece):
    count = lax.axis_size("fsdp")
    masks = (1, 2) if count == 4 else range(1, count)
    return [trade(piece, "fsdp", mask) for mask in masks]


def plane_far(near):
    if lax.axis_size("fsdp") != 4:
        return []
    half = near[0].shape[0] // 2
    return [trade(near[1][:half], "fsdp", 1), trade(near[0][half:], "fsdp", 2)]


def both_cores(own, near, far):
    held = jnp.concatenate([own] + near + far, axis=0)
    return held, trade(held, "expert", 1)


def sum_first(blocks):
    count = lax.axis_size("fsdp")
    place = lax.axis_index("fsdp")
    parts = [
        lax.dynamic_index_in_dim(blocks, place ^ mask, 0, keepdims=False) for mask in range(count)
    ]
    if count != 4:
        return parts, []
    half = blocks.shape[1] // 2
    return parts[:3], [
        trade(parts[3][:half], "fsdp", 1),
        trade(parts[3][half:], "fsdp", 2),
    ]


def added(left, right):
    return (left.astype(FULL) + right.astype(FULL)).astype(LOW)


def sum_second(parts, got):
    if not got:
        return [trade(part, "fsdp", mask) for mask, part in enumerate(parts) if mask > 0]
    half = parts[1].shape[0] // 2
    send_x = jnp.concatenate([parts[1][:half], added(parts[1][half:], got[1])], axis=0)
    send_y = jnp.concatenate([added(parts[2][:half], got[0]), parts[2][half:]], axis=0)
    return [trade(send_x, "fsdp", 1), trade(send_y, "fsdp", 2)]


def sum_total(own, arrived):
    total = own.astype(FULL)
    for term in arrived:
        total = total + term.astype(FULL)
    return total


def layer_first(held):
    layer = lax.axis_index("expert") // 2
    layers = lax.axis_size("expert") // 2
    parts = [
        lax.dynamic_index_in_dim(held, layer ^ mask, 0, keepdims=False) for mask in range(layers)
    ]
    return parts[0], [trade(parts[mask], "expert", 2 * mask) for mask in range(1, layers)]


def core_last(total):
    side = core_side()
    rows = total.shape[0] // 2
    mine = lax.dynamic_slice_in_dim(total, side * rows, rows, 0)
    away = lax.dynamic_slice_in_dim(total, (1 - side) * rows, rows, 0).astype(LOW)
    came = trade(away, "expert", 1).astype(FULL)
    return jnp.where(side == 0, mine, came), jnp.where(side == 0, came, mine)


def feed_half(fc_in, fc_out):
    side = core_side()
    lines, inner = fc_in.shape
    fold = inner // fc_out.shape[1]
    blocks = [fc_out[at * lines : (at + 1) * lines] for at in range(fold)]
    folded = jnp.concatenate(blocks, axis=1)
    came = trade(jnp.where(side == 0, folded, fc_in), "expert", 1)
    width = fc_out.shape[1]
    rows_came = [came[:, at * width : (at + 1) * width] for at in range(fold)]
    stacked = [
        jnp.concatenate([group[at], group[at + 1]], axis=0)
        for group in (rows_came, blocks)
        for at in range(0, fold, 2)
    ]
    return jnp.where(
        side == 0, jnp.concatenate([fc_in, came], axis=0), jnp.concatenate(stacked, axis=1)
    )


def feed_last(total, fold):
    side = core_side()
    cols = total.shape[1]
    size = total.shape[0] // 2
    inside = total[:size].reshape(fold, 2, -1, cols)
    outside = total[size:].reshape(2, -1, cols)

    def part(core):
        return jnp.concatenate(
            [
                lax.dynamic_index_in_dim(inside, core, 1, keepdims=False).reshape(-1, cols),
                lax.dynamic_index_in_dim(outside, core, 0, keepdims=False),
            ],
            axis=0,
        )

    mine = part(side)
    came = trade(part(1 - side).astype(LOW), "expert", 1).astype(FULL)
    return jnp.where(side == 0, mine, came), jnp.where(side == 0, came, mine)


def in_blocks(half_grad):
    planes = lax.axis_size("fsdp")
    layers = lax.axis_size("expert") // 2
    return half_grad.reshape(planes, layers, -1, half_grad.shape[-1])


def per_device(
    patches,
    dense_gains,
    dense_shifts,
    dense_qkv,
    dense_proj,
    dense_fc_in,
    dense_fc_bias,
    dense_fc_out,
    moe_gains,
    moe_shifts,
    moe_qkv,
    moe_proj,
    router,
    expert_in,
    expert_in_bias,
    expert_out,
    expert_out_bias,
    routes,
    slot_pos,
    image_counts,
    cotangent,
):
    images, length, width = patches.shape
    shard_rows = dense_qkv.shape[0]
    inner = dense_fc_in.shape[1]
    local_experts = expert_in.shape[0]
    experts = local_experts * lax.axis_size("expert")
    planes = lax.axis_size("fsdp")
    plane = lax.axis_index("fsdp")
    place = jnp.stack([plane, core_side()]).astype(jnp.int32)
    block = fit(length, 16)
    rows = images * block
    lowest = (images + 1) // 2
    capacity = fit(5 * (images + lowest) * length // (4 * experts) + 2, 16)
    slots = experts * capacity

    def padded(array, fill=0):
        return jnp.pad(
            array, ((0, 0), (0, block - length), (0, 0)), constant_values=fill
        ).reshape(rows, array.shape[-1])

    def trimmed(array):
        return array.reshape(images, block, array.shape[-1])[:, :length]

    def far(array):
        return trade(array, "expert", 1)

    layers = lax.axis_size("expert") // 2
    fold = inner // width
    small_rows = jnp.concatenate(
        [
            dense_gains.T,
            dense_shifts.T,
            moe_gains.T,
            moe_shifts.T,
            router,
            dense_fc_bias.reshape(shard_rows, -1),
        ],
        axis=1,
    )
    small_cols = small_rows.shape[1]
    small_rows = jnp.pad(small_rows, ((0, 0), (0, 256 - small_cols)))
    first_half = core_half(jnp.concatenate([dense_qkv, dense_proj, small_rows], axis=1))
    moe_rows = jnp.concatenate([moe_qkv, moe_proj], axis=1)
    if (2 * shard_rows) % 16 == 0:
        later = jnp.concatenate([feed_half(dense_fc_in, dense_fc_out), core_half(moe_rows)], axis=1)
        pack = lax.all_gather(later, ("fsdp", "expert"), axis=0, tiled=True)
        pack = pack.reshape(planes * layers, 2, 2 * shard_rows, later.shape[1])
    else:
        groups = width // 48
        whole_in = lax.all_gather(dense_fc_in, ("fsdp", "expert"), axis=0, tiled=True)
        whole_out = lax.all_gather(dense_fc_out, ("fsdp", "expert"), axis=0, tiled=True)
        whole_moe = lax.all_gather(moe_rows, ("fsdp", "expert"), axis=0, tiled=True)
        folded = whole_out.reshape(groups, fold, 48, width).swapaxes(1, 2).reshape(groups, 48, inner)
        pack = jnp.concatenate(
            [
                jnp.stack([whole_in.reshape(groups, 48, inner), folded], axis=1),
                whole_moe.reshape(groups, 48, 2, 2 * width).swapaxes(1, 2),
            ],
            axis=3,
        )
    dense_own = layer_gather(first_half)
    dense_near = plane_near(dense_own)
    expert_rows = width // planes
    expert_own = jnp.concatenate(
        [expert_in[0]]
        + [expert_out[0, at * expert_rows : (at + 1) * expert_rows] for at in range(fold)],
        axis=1,
    )
    dense_pieces = both_cores(dense_own, dense_near, plane_far(dense_near))

    live_images = jnp.arange(images) < image_counts[0]
    live_rows = jnp.repeat(live_images, block).astype(FULL)[:, None]
    up = padded(jnp.where(live_images[:, None, None], cotangent, jnp.zeros_like(cotangent)))
    route_cols = padded(routes)
    target_cols = padded(jnp.where(slot_pos >= 0, routes * capacity + slot_pos, -1), -1)
    target_rows = target_cols.T

    x0 = padded(patches).astype(FULL)
    an, qkv, mixed, x1, vec, fc_bias, router_full = attend_forward(
        place, x0, None, dense_pieces, planes, (0, 2, 4, 5, 6), length, images, experts, inner
    )
    x1, expert_own = tie((x1, expert_own))
    expert_near = plane_near(expert_own)
    expert_bias = jnp.concatenate([expert_in_bias[0], expert_out_bias[0]])
    other_bias = tie([trade(expert_bias, "fsdp", mask) for mask in range(1, planes)])
    expert_bias = in_order([part[None] for part in [expert_bias] + other_bias], plane).astype(FULL)
    hidden_part = expert_in_bias.shape[1]
    in_bias = expert_bias[:, :hidden_part].reshape(1, -1)
    out_bias = expert_bias[:, hidden_part:].reshape(1, -1)

    hn, act, slope, x2 = feed_forward(x1, vec, fc_bias, pack, (1, 3, 7))
    an2, qkv2, mixed2, x3 = attend_forward(
        place, x2, vec, [pack], planes, (8, 10, 12, 13, 14), length, images, experts, inner
    )
    x3, expert_near = tie((x3, expert_near))
    expert_far = plane_far(expert_near)
    mn, gate, pick, outgoing, grad_out = dispatch(
        x3, vec, router_full, route_cols, target_rows, up, experts, slots, (9, 11)
    )

    def exchange(array):
        return lax.all_to_all(
            array.reshape(experts, capacity, width), "expert", split_axis=0, concat_axis=0, tiled=True
        ).reshape(slots, width)

    arrived = exchange(outgoing)
    dy = exchange(grad_out)
    expert_w = jnp.concatenate([expert_own] + expert_near + expert_far, axis=0)
    e_act, e_slope = hidden_forward(place, arrived, in_bias, expert_w, planes)
    home = exchange(expert_out_forward(place, e_act, out_bias, expert_w, expert_rows))
    dh, in_bias_grad, out_bias_grad, back = expert_backward(place, dy, e_slope, expert_w, expert_rows)
    back = exchange(back)
    expert_grad = expert_products(arrived, dh, e_act, dy, planes)
    expert_grad, home = tie((expert_grad, home))
    expert_sum = lax.psum_scatter(expert_grad, "fsdp", scatter_dimension=0, tiled=True)
    bias_grads = jnp.concatenate(
        [in_bias_grad.reshape(planes, -1), out_bias_grad.reshape(planes, -1)], axis=1
    )
    bias_parts = [
        lax.dynamic_index_in_dim(bias_grads, plane ^ mask, 0) for mask in range(planes)
    ]
    bias_came = tie([trade(bias_parts[mask], "fsdp", mask) for mask in range(1, planes)])
    bias_sum = sum_total(bias_parts[0], bias_came)

    output, part, router_grad = combine(
        x3, home, gate, pick, route_cols, target_cols, up, live_rows, mn, router_full
    )
    dx3, gate_sums = return_grad(x3, vec, part, back, target_cols, up, 9)
    dx2, mine2, away2, low_mine2, low_away2, moe_sums = attend_backward(
        place, dx3, x2, vec, qkv2, [pack], planes, 8, length, images
    )
    moe_grad = products(
        [
            [(an2, mine2), (far(an2), far(away2))],
            [(mixed2, low_mine2), (far(mixed2), far(low_away2))],
        ]
    )
    moe_grad, dx2 = tie((moe_grad, dx2))
    moe_parts, moe_got = sum_first(in_blocks(moe_grad))
    dx1, mine1, away1, low_mine1, low_away1, feed_sums, fc_bias_grad = feed_backward(
        place, dx2, x1, vec, slope, pack, 1
    )
    moe_got, dx1 = tie((moe_got, dx1))
    moe_came = sum_second(moe_parts, moe_got)
    if (2 * shard_rows) % 16 == 0:
        feed_grad = feed_products(
            hn, far(hn), mine1, far(away1), act, far(act), low_mine1, far(low_away1),
            planes * layers, fold,
        )
    else:
        in_part = products([[(hn, mine1), (far(hn), far(away1))]])
        out_part = products([[(act, low_mine1), (far(act), far(low_away1))]], part=768)
        in_part = in_blocks(in_part)
        in_part = in_part.reshape(in_part.shape[:3] + (fold, -1)).swapaxes(2, 3)
        in_part = in_part.reshape(planes, layers, -1, in_part.shape[-1])
        feed_grad = jnp.concatenate([in_part, in_blocks(out_part)], axis=2)
        feed_grad = feed_grad.reshape(-1, feed_grad.shape[-1])
    feed_grad, dx1 = tie((feed_grad, dx1))
    feed_parts, feed_got = sum_first(in_blocks(feed_grad))
    dx0, mine0, away0, low_mine0, low_away0, vectors = attend_backward(
        place, dx1, x0, vec, qkv, dense_pieces, planes, 0, length, images, experts,
        [feed_sums, moe_sums, gate_sums, fc_bias_grad, router_grad],
    )
    moe_came, feed_got, mine0, expert_sum = tie((moe_came, feed_got, mine0, expert_sum))
    feed_came = sum_second(feed_parts, feed_got)
    moe_mine, moe_layers = layer_first(sum_total(moe_parts[0], moe_came).astype(LOW))
    dense_grad = products(
        [
            [(an, mine0), (far(an), far(away0))],
            [(mixed, low_mine0), (far(mixed), far(low_away0))],
        ],
        vectors,
    )
    dense_parts, dense_got = sum_first(in_blocks(dense_grad))
    dense_got, feed_came, moe_layers = tie((dense_got, feed_came, moe_layers))
    feed_mine, feed_layers = layer_first(sum_total(feed_parts[0], feed_came).astype(LOW))
    moe_left, moe_right = core_last(sum_total(moe_mine, moe_layers))
    dense_came = sum_second(dense_parts, dense_got)
    feed_left, feed_right = feed_last(sum_total(feed_mine, feed_layers), fold)
    dense_mine, dense_layers = layer_first(sum_total(dense_parts[0], dense_came).astype(LOW))
    dense_left, dense_right = core_last(sum_total(dense_mine, dense_layers))
    third = 3 * width // 2

    def split(left, right):
        return (
            jnp.concatenate([left[:, :third], right[:, :third]], axis=1),
            jnp.concatenate([left[:, third : 2 * width], right[:, third : 2 * width]], axis=1),
        )

    dense_qkv_sum, dense_proj_sum = split(dense_left, dense_right)
    moe_qkv_sum, moe_proj_sum = split(moe_left, moe_right)
    small_sum = dense_left[:, 2 * width :] + dense_right[:, 2 * width :]
    feed_in_sum = jnp.concatenate(
        [
            half[at * shard_rows : (at + 1) * shard_rows]
            for half in (feed_left, feed_right)
            for at in range(fold)
        ],
        axis=1,
    )
    feed_out_sum = jnp.concatenate(
        [feed_left[fold * shard_rows :], feed_right[fold * shard_rows :]], axis=1
    )
    expert_in_sum = expert_sum[:expert_rows].astype(FULL)[None]
    expert_out_sum = jnp.concatenate(
        [expert_sum[expert_rows:, at * width : (at + 1) * width] for at in range(fold)], axis=0
    ).astype(FULL)[None]
    small_turn = small_sum[:, :15].T
    return (
        trimmed(output),
        trimmed(dx0),
        small_turn[0:2],
        small_turn[2:8],
        dense_qkv_sum,
        dense_proj_sum,
        feed_in_sum,
        small_sum[:, 15 + experts : small_cols].reshape(-1),
        feed_out_sum,
        small_turn[8:10],
        small_turn[10:15],
        moe_qkv_sum,
        moe_proj_sum,
        small_sum[:, 15 : 15 + experts],
        expert_in_sum,
        bias_sum[:, :hidden_part],
        expert_out_sum,
        bias_sum[:, hidden_part:],
    )


def solution(mesh):
    return jax.shard_map(
        per_device,
        mesh=mesh,
        in_specs=(
            P(("fsdp", "expert"), None, None),
            P(None, ("fsdp", "expert")),
            P(None, ("fsdp", "expert")),
            P(("fsdp", "expert"), None),
            P(("fsdp", "expert"), None),
            P(("fsdp", "expert"), None),
            P(("fsdp", "expert")),
            P(("fsdp", "expert"), None),
            P(None, ("fsdp", "expert")),
            P(None, ("fsdp", "expert")),
            P(("fsdp", "expert"), None),
            P(("fsdp", "expert"), None),
            P(("fsdp", "expert"), None),
            P("expert", "fsdp", None),
            P("expert", "fsdp"),
            P("expert", "fsdp", None),
            P("expert", "fsdp"),
            P(("fsdp", "expert"), None, None),
            P(("fsdp", "expert"), None, None),
            P(("fsdp", "expert")),
            P(("fsdp", "expert"), None, None),
        ),
        out_specs=(
            P(("fsdp", "expert"), None, None),
            P(("fsdp", "expert"), None, None),
            P(None, ("fsdp", "expert")),
            P(None, ("fsdp", "expert")),
            P(("fsdp", "expert"), None),
            P(("fsdp", "expert"), None),
            P(("fsdp", "expert"), None),
            P(("fsdp", "expert")),
            P(("fsdp", "expert"), None),
            P(None, ("fsdp", "expert")),
            P(None, ("fsdp", "expert")),
            P(("fsdp", "expert"), None),
            P(("fsdp", "expert"), None),
            P(("fsdp", "expert"), None),
            P("expert", "fsdp", None),
            P("expert", "fsdp"),
            P("expert", "fsdp", None),
            P("expert", "fsdp"),
        ),
        check_vma=False,
    )
```

profile of v0, /device:TPU:9, one launch (start us, length us, event | category | flops | bytes accessed | tf_op | source)
XLA Modules:
  0.0 541.0 jit_solution(17159846135346646799)
XLA Ops:
  15.8 2.6 collective-permute-start.1
  22.4 15.1 %collective-permute-done.2 = bf16[48,1664]{1,0:T(8,128)(2,1)S(1)} collective-permute-done((bf16[48,1664]{1,0:T(8,128)(2,1)S(1)}, bf16[48,1664]{1,0:T(8,128)(2,1)S(1)}, u32[]{:S(2)}, u32[]{:S(2)}) %collective-permute-start.2) | collective-permute-done | bytes 159776 | tf_op jit(solution)/shard_map/ppermute | solution.py:978
  46.1 3.5 collective-permute-done.5
  54.0 11.6 %collective-permute-done.6 = bf16[96,1664]{1,0:T(8,128)(2,1)S(1)} collective-permute-done((bf16[96,1664]{1,0:T(8,128)(2,1)S(1)}, bf16[96,1664]{1,0:T(8,128)(2,1)S(1)}, u32[]{:S(2)}, u32[]{:S(2)}) %collective-permute-start.6) | collective-permute-done | bytes 319520 | tf_op jit(solution)/shard_map/ppermute | solution.py:978
  67.2 11.0 %collective-permute-start.8 = (bf16[768,1664]{1,0:T(8,128)(2,1)}, bf16[768,1664]{1,0:T(8,128)(2,1)}, u32[]{:S(2)}, u32[]{:S(2)}) collective-permute-start(bf16[768,1664]{1,0:T(8,128)(2,1)} %constant_dynamic-update-slice_fusion.refs_2_.refs_5_), channel_id=1, source_target_pairs={{0,1},{1,0},{2,3},{3,2},{4,5},{5,4},{6,7},{7,6},{8,9},{9,8},{10,11... | collective-permute-start | bytes 7667720 | tf_op jit(solution)/shard_map/ppermute | solution.py:978
  78.2 2.4 bitcast_dynamic-update-slice_fusion
  90.0 11.0 %shard_map.340 = (bf16[416,768]{1,0:T(8,128)(2,1)}, bf16[416,2304]{1,0:T(8,128)(2,1)}, bf16[416,768]{1,0:T(8,128)(2,1)}, f32[416,768]{1,0:T(8,128)}, f32[32,768]...) custom-call(s32[2]{0:T(128)} %pad_add_fusion.refs_0_.place_ref, f32[416,768]{1,0:T(8,128)} %bitcast.166, ...), custom_call_target="tpu_custom_call" | custom-call | flops 12650000384 | bytes 11169792 | tf_op jit(solution)/shard_map/pallas_call | solution.py:54
  103.2 3.3 constant_dynamic-update-slice_fusion.11
  106.5 37.3 %all-gather.2.cloned.1.call-done = bf16[1536,4608]{1,0:T(8,128)(2,1)} async-done(((bf16[48,4608]{1,0:T(8,128)(2,1)}), bf16[1536,4608]{1,0:T(8,128)(2,1)}) %all-gather.2.cloned.1.call-update) | async-done | bytes 14155792 | tf_op jit(solution)/shard_map/all_gather | solution.py:1199
  143.8 11.1 %shard_map.341 = (bf16[416,768]{1,0:T(8,128)(2,1)}, bf16[416,3072]{1,0:T(8,128)(2,1)}, bf16[416,3072]{1,0:T(8,128)(2,1)}, f32[416,768]{1,0:T(8,128)}) custom-call(f32[416,768]{1,0:T(8,128)} %get-tuple-element.102.x_ref, f32[32,768]{1,0:T(8,128)} %get-tuple-element.103.vec_ref.refs_2_, f32[1,3072]{1,0:T(1,128)} %get-tuple-element.104.bias_ref, ...), custom_call_target="tpu_custom_call" | custom-call | flops 12650000384 | bytes 36728832 | tf_op jit(solution)/shard_map/pallas_call | solution.py:54
  155.0 10.7 %shard_map.342 = (bf16[416,768]{1,0:T(8,128)(2,1)}, bf16[416,2304]{1,0:T(8,128)(2,1)}, bf16[416,768]{1,0:T(8,128)(2,1)}, f32[416,768]{1,0:T(8,128)}) custom-call(s32[2]{0:T(128)} %pad_add_fusion.refs_0_.place_ref, f32[416,768]{1,0:T(8,128)} %get-tuple-element.105.refs_1_.x_ref, f32[32,768]{1,0:T(8,128)} %get-tuple-element.103.vec_ref.refs_2_, ...), custom_call_target="tpu_custom_call" | custom-call | flops 12650000384 | bytes 20004864 | tf_op jit(solution)/shard_map/pallas_call | solution.py:54
  167.3 2.4 slice.281
  172.2 5.7 %shard_map.343 = (bf16[416,768]{1,0:T(8,128)(2,1)}, f32[416,128]{1,0:T(8,128)}, f32[416,128]{1,0:T(8,128)}, bf16[768,768]{1,0:T(8,128)(2,1)}, bf16[768,768]{1,0:T(8,128)(2,1)}) custom-call(f32[416,768]{1,0:T(8,128)} %get-tuple-element.108.x_ref, f32[32,768]{1,0:T(8,128)} %get-tuple-element.103.vec_ref.refs_2_, ...), custom_call_target="tpu_custom_call" | custom-call | flops 6899999744 | bytes 5642752 | tf_op jit(solution)/shard_map/pallas_call | solution.py:54
  178.0 8.4 %all-to-all-start = ((bf16[8,96,768]{2,1,0:T(8,128)(2,1)}), bf16[8,96,768]{2,1,0:T(8,128)(2,1)S(1)}, u32[]{:S(2)}, u32[]{:S(2)}) async-start(bf16[8,96,768]{2,1,0:T(8,128)(2,1)} %bitcast.176), calls=%async_computation | async-start | bytes 2359296 | tf_op jit(solution)/shard_map/all_to_all | solution.py:1255
  187.9 3.3 constant_dynamic-update-slice_fusion.9
  191.2 5.7 %collective-permute-done.16 = bf16[96,6144]{1,0:T(8,128)(2,1)} collective-permute-done((bf16[96,6144]{1,0:T(8,128)(2,1)}, bf16[96,6144]{1,0:T(8,128)(2,1)}, u32[]{:S(2)}, u32[]{:S(2)}) %collective-permute-start.16) | collective-permute-done | bytes 1179680 | tf_op jit(solution)/shard_map/ppermute | solution.py:978
  196.9 2.4 constant_dynamic-update-slice_fusion.8
  199.3 12.9 %all-to-all-done = bf16[8,96,768]{2,1,0:T(8,128)(2,1)S(1)} async-done(((bf16[8,96,768]{2,1,0:T(8,128)(2,1)}), bf16[8,96,768]{2,1,0:T(8,128)(2,1)S(1)}, u32[]{:S(2)}, u32[]{:S(2)}) %all-to-all-start) | async-done | bytes 1179680 | tf_op jit(solution)/shard_map/all_to_all | solution.py:1255
  212.2 7.3 %all-to-all-start.1 = ((bf16[8,96,768]{2,1,0:T(8,128)(2,1)}), bf16[8,96,768]{2,1,0:T(8,128)(2,1)S(1)}, u32[]{:S(2)}, u32[]{:S(2)}) async-start(bf16[8,96,768]{2,1,0:T(8,128)(2,1)} %bitcast.20), calls=%async_computation.1 | async-start | bytes 2359296 | tf_op jit(solution)/shard_map/all_to_all | solution.py:1255
  219.5 2.5 constant_dynamic-update-slice_fusion.7.pack_ref.in_ref
  222.0 11.4 %shard_map.344 = (bf16[768,3072]{1,0:T(8,128)(2,1)}, bf16[768,3072]{1,0:T(8,128)(2,1)}) custom-call(s32[2]{0:T(128)} %pad_add_fusion.refs_0_.place_ref, bf16[768,768]{1,0:T(8,128)(2,1)} %bitcast.169, f32[1,3072]{1,0:T(1,128)} %bitcast.196, bf16[768,6144]{1,0:T(8,128)(2,1)} %constant_dynamic-update-slice_fusion.7.pack_ref.in_ref), custom_call_target="tpu_custom_call" | custom-call | flops 12650000384 | bytes 20066304 | tf_op jit(solution)/shard_map/pallas_call | solution.py:54
  233.4 8.9 %shard_map.347 = bf16[768,768]{1,0:T(8,128)(2,1)} custom-call(s32[2]{0:T(128)} %pad_add_fusion.refs_0_.place_ref, bf16[768,3072]{1,0:T(8,128)(2,1)} %get-tuple-element.119.act_ref, f32[1,768]{1,0:T(1,128)} %reshape.246.bias_ref, bf16[768,6144]{1,0:T(8,128)(2,1)} %constant_dynamic-update-slice_fusion.7.pack_ref.in_ref), custom_call_target="tpu_custom_call" | custom-call | flops 9200000000 | bytes 15338496 | tf_op jit(solution)/shard_map/pallas_call | solution.py:54
  242.3 3.0 all-to-all-done.1
  245.3 7.1 %all-to-all-start.2 = ((bf16[8,96,768]{2,1,0:T(8,128)(2,1)}), bf16[8,96,768]{2,1,0:T(8,128)(2,1)S(1)}, u32[]{:S(2)}, u32[]{:S(2)}) async-start(bf16[8,96,768]{2,1,0:T(8,128)(2,1)} %bitcast.175), calls=%async_computation.2 | async-start | bytes 2359296 | tf_op jit(solution)/shard_map/all_to_all | solution.py:1255
  252.3 15.5 %shard_map.345 = (bf16[768,3072]{1,0:T(8,128)(2,1)}, f32[1,3072]{1,0:T(1,128)}, f32[1,768]{1,0:T(1,128)}, bf16[768,768]{1,0:T(8,128)(2,1)}) custom-call(s32[2]{0:T(128)} %pad_add_fusion.refs_0_.place_ref, bf16[768,768]{1,0:T(8,128)(2,1)} %bitcast.172, bf16[768,3072]{1,0:T(8,128)(2,1)} %get-tuple-element.117.slope_ref, ...), custom_call_target="tpu_custom_call" | custom-call | flops 16099999744 | bytes 30686208 | tf_op jit(solution)/shard_map/pallas_call | solution.py:54
  267.9 13.4 %shard_map.346 = bf16[1536,3072]{1,0:T(8,128)(2,1)} custom-call(bf16[768,768]{1,0:T(8,128)(2,1)} %bitcast.170, bf16[768,3072]{1,0:T(8,128)(2,1)} %get-tuple-element.118.dh_ref, bf16[768,3072]{1,0:T(8,128)(2,1)} %get-tuple-element.119.act_ref, bf16[768,768]{1,0:T(8,128)(2,1)} %bitcast.173), custom_call_target="tpu_custom_call" | custom-call | flops 16099999744 | bytes 21233664 | tf_op jit(solution)/shard_map/pallas_call | solution.py:54
  282.3 5.1 all-to-all-start.3
  288.4 8.1 %shard_map.348 = (bf16[416,768]{1,0:T(8,128)(2,1)}, f32[416,768]{1,0:T(8,128)}, f32[768,128]{1,0:T(8,128)}) custom-call(f32[416,768]{1,0:T(8,128)} %get-tuple-element.108.x_ref, bf16[768,768]{1,0:T(8,128)(2,1)} %bitcast.171, f32[416,128]{1,0:T(8,128)} %get-tuple-element.121.gate_ref, f32[416,128]{1,0:T(8,128)} %get-tuple-element.122.pick_ref, ...), custom_call_target="tpu_custom_call" | custom-call | flops 9200000000 | bytes 6676608 | tf_op jit(solution)/shard_map/pallas_call | solution.py:54
  296.5 16.8 %all-to-all-done.3 = bf16[8,96,768]{2,1,0:T(8,128)(2,1)S(1)} async-done(((bf16[8,96,768]{2,1,0:T(8,128)(2,1)}), bf16[8,96,768]{2,1,0:T(8,128)(2,1)S(1)}, u32[]{:S(2)}, u32[]{:S(2)}) %all-to-all-start.3) | async-done | bytes 1179680 | tf_op jit(solution)/shard_map/all_to_all | solution.py:1255
  314.3 4.8 shard_map.349
  319.2 19.4 %shard_map.350 = (f32[416,768]{1,0:T(8,128)}, bf16[416,1152]{1,0:T(8,128)(2,1)}, bf16[416,1152]{1,0:T(8,128)(2,1)}, bf16[416,384]{1,0:T(8,128)(2,1)}, bf16[416,384]{1,0:T(8,128)(2,1)}, /*index=5*/f32[8,768]{1,0:T(8,128)}) custom-call(s32[2]{0:T(128)} %pad_add_fusion.refs_0_.place_ref, f32[416,768]{1,0:T(8,128)} %get-tuple-element.129.up_ref, ...), custom_call_target="tpu_custom_call" | custom-call | flops 21849999360 | bytes 22585344 | tf_op jit(solution)/shard_map/pallas_call | solution.py:54
  341.4 3.0 collective-permute-done.19.refs_2_
  345.6 6.8 %shard_map.351 = bf16[768,1536]{1,0:T(8,128)(2,1)} custom-call(bf16[416,768]{1,0:T(8,128)(2,1)} %get-tuple-element.126.refs_0_, bf16[416,1152]{1,0:T(8,128)(2,1)} %get-tuple-element.131.refs_1_, bf16[416,768]{1,0:T(8,128)(2,1)} %copy-done.31, bf16[416,1152]{1,0:T(8,128)(2,1)} %copy-done.28, bf16[416,768]{1,0:T(8,128)(2,1)} %get-tuple-element.133.refs_4_, ...), custom_call_target="tpu_custom_call" | custom-call | flops 8049999872 | bytes 7471104 | tf_op jit(solution)/shard_map/pallas_call | solution.py:54
  356.4 13.2 %shard_map.352 = (f32[416,768]{1,0:T(8,128)}, bf16[416,1536]{1,0:T(8,128)(2,1)}, bf16[416,1536]{1,0:T(8,128)(2,1)}, bf16[416,384]{1,0:T(8,128)(2,1)}, bf16[416,3...) custom-call(s32[2]{0:T(128)} %pad_add_fusion.refs_0_.place_ref, f32[416,768]{1,0:T(8,128)} %get-tuple-element.137.up_ref, ...), custom_call_target="tpu_custom_call" | custom-call | flops 14949999616 | bytes 38031360 | tf_op jit(solution)/shard_map/pallas_call | solution.py:54
  371.0 2.9 collective-permute-done.54
  378.8 2.6 collective-permute-done.56
  381.4 2.3 collective-permute-start.32
  392.8 11.5 %shard_map.353 = bf16[6144,384]{1,0:T(8,128)(2,1)} custom-call(bf16[416,768]{1,0:T(8,128)(2,1)} %get-tuple-element.125.hn_ref, bf16[416,768]{1,0:T(8,128)(2,1)} %copy-done.32, bf16[416,1536]{1,0:T(8,128)(2,1)} %get-tuple-element.139.du_ref, bf16[416,1536]{1,0:T(8,128)(2,1)} %collective-permute-done.23.du_far_ref, ...), custom_call_target="tpu_custom_call" | custom-call | flops 12650000384 | bytes 14303232 | tf_op jit(solution)/shard_map/pallas_call | solution.py:54
  407.7 18.7 %shard_map.354 = (f32[416,768]{1,0:T(8,128)}, bf16[416,1152]{1,0:T(8,128)(2,1)}, bf16[416,1152]{1,0:T(8,128)(2,1)}, bf16[416,384]{1,0:T(8,128)(2,1)}, bf16[416,384]{1,0:T(8,128)(2,1)}, /*index=5*/f32[768,128]{1,0:T(8,128)}) custom-call(s32[2]{0:T(128)} %pad_add_fusion.refs_0_.place_ref, f32[416,768]{1,0:T(8,128)} %get-tuple-element.147.up_ref, ...), custom_call_target="tpu_custom_call" | custom-call | flops 21849999360 | bytes 14389248 | tf_op jit(solution)/shard_map/pallas_call | solution.py:54
  432.7 3.7 collective-permute-start.40
  440.0 7.1 %shard_map.355 = bf16[768,1664]{1,0:T(8,128)(2,1)} custom-call(bf16[416,768]{1,0:T(8,128)(2,1)} %get-tuple-element.155.refs_0_, bf16[416,1152]{1,0:T(8,128)(2,1)} %get-tuple-element.161.refs_1_, bf16[416,768]{1,0:T(8,128)(2,1)} %collective-permute-done.32.refs_2_, bf16[416,1152]{1,0:T(8,128)(2,1)} %collective-permute-done.33.refs_3_, ...), custom_call_target="tpu_custom_call" | custom-call | flops 8049999872 | bytes 8060928 | tf_op jit(solution)/shard_map/pallas_call | solution.py:54
  456.5 17.3 %collective-permute-done.36 = bf16[2,48,1664]{2,1,0:T(8,128)(2,1)S(1)} collective-permute-done((bf16[2,48,1664]{2,1,0:T(8,128)(2,1)S(1)}, bf16[2,48,1664]{2,1,0:T(8,128)(2,1)S(1)}, u32[]{:S(2)}, u32[]{:S(2)}) %collective-permute-start.36) | collective-permute-done | bytes 319520 | tf_op jit(solution)/shard_map/ppermute | solution.py:978
  482.1 8.6 %collective-permute-done.49 = bf16[384,384]{1,0:T(8,128)(2,1)S(1)} collective-permute-done((bf16[384,384]{1,0:T(8,128)(2,1)S(1)}, bf16[384,384]{1,0:T(8,128)(2,1)S(1)}, u32[]{:S(2)}, u32[]{:S(2)}) %collective-permute-start.49) | collective-permute-done | bytes 294944 | tf_op jit(solution)/shard_map/ppermute | solution.py:978
  493.0 12.8 %collective-permute-done.51 = bf16[384,384]{1,0:T(8,128)(2,1)S(1)} collective-permute-done((bf16[384,384]{1,0:T(8,128)(2,1)S(1)}, bf16[384,384]{1,0:T(8,128)(2,1)S(1)}, u32[]{:S(2)}, u32[]{:S(2)}) %collective-permute-start.51) | collective-permute-done | bytes 294944 | tf_op jit(solution)/shard_map/ppermute | solution.py:978
  508.9 2.3 collective-permute-start.46
  511.6 3.0 collective-permute-done.45
  514.6 4.0 collective-permute-done.46
  518.6 6.9 %collective-permute-done.47 = bf16[48,1664]{1,0:T(8,128)(2,1)S(1)} collective-permute-done((bf16[48,1664]{1,0:T(8,128)(2,1)S(1)}, bf16[48,1664]{1,0:T(8,128)(2,1)S(1)}, u32[]{:S(2)}, u32[]{:S(2)}) %collective-permute-start.47) | collective-permute-done | bytes 159776 | tf_op jit(solution)/shard_map/ppermute | solution.py:978
  (321 shorter events, 114.2 us)
Async XLA Ops:
  7.3 136.5 %all-gather.2.cloned.1.call-start = ((), (), s32[]{:S(2)}) async-start(), calls=%async_computation.5 | async-start | bytes 14598144 | tf_op jit(solution)/shard_map/all_gather | solution.py:1199
  15.8 6.6 %collective-permute-start.1 = (bf16[48,1664]{1,0:T(8,128)(2,1)S(1)}, bf16[48,1664]{1,0:T(8,128)(2,1)S(1)}, u32[]{:S(2)}, u32[]{:S(2)}) collective-permute-start(bf16[48,1664]{1,0:T(8,128)(2,1)S(1)} %maximum_select_fusion.4), channel_id=1, source_target_pairs={{0,6},{1,7},{2,4},{3,5},{4,2},{5,3},{6,0},{7,1},{8,14},{9,15},{10,... | collective-permute-start | bytes 479240 | tf_op jit(solution)/shard_map/ppermute | solution.py:978
  18.3 19.2 %collective-permute-start.2 = (bf16[48,1664]{1,0:T(8,128)(2,1)S(1)}, bf16[48,1664]{1,0:T(8,128)(2,1)S(1)}, u32[]{:S(2)}, u32[]{:S(2)}) collective-permute-start(bf16[48,1664]{1,0:T(8,128)(2,1)S(1)} %maximum_select_fusion.4), channel_id=1, source_target_pairs={{0,4},{1,5},{2,6},{3,7},{4,0},{5,1},{6,2},{7,3},{8,12},{9,13},{10,... | collective-permute-start | bytes 479240 | tf_op jit(solution)/shard_map/ppermute | solution.py:978
  38.5 11.0 %collective-permute-start.5 = (bf16[192,1664]{1,0:T(8,128)(2,1)S(1)}, bf16[192,1664]{1,0:T(8,128)(2,1)S(1)}, u32[]{:S(2)}, u32[]{:S(2)}) collective-permute-start(bf16[192,1664]{1,0:T(8,128)(2,1)S(1)} %get-tuple-element.239), channel_id=1, source_target_pairs={{0,16},{8,24},{16,0},{24,8},{1,17},{9,25},{17,1},{25,9},{2,18},{10... | collective-permute-start | bytes 1916936 | tf_op jit(solution)/shard_map/ppermute | solution.py:978
  39.8 11.1 %collective-permute-start.4 = (bf16[192,1664]{1,0:T(8,128)(2,1)S(1)}, bf16[192,1664]{1,0:T(8,128)(2,1)S(1)}, u32[]{:S(2)}, u32[]{:S(2)}) collective-permute-start(bf16[192,1664]{1,0:T(8,128)(2,1)S(1)} %get-tuple-element.239), channel_id=1, source_target_pairs={{0,8},{8,0},{16,24},{24,16},{1,9},{9,1},{17,25},{25,17},{2,10},{10... | collective-permute-start | bytes 1916936 | tf_op jit(solution)/shard_map/ppermute | solution.py:978
  41.1 47.5 %collective-permute-start.13 = (bf16[960]{0:T(1024)(128)(2,1)S(1)}, bf16[960]{0:T(1024)(128)(2,1)S(1)}, u32[]{:S(2)}, u32[]{:S(2)}) collective-permute-start(bf16[960]{0:T(1024)(128)(2,1)S(1)} %pad_maximum_fusion.14), channel_id=1, source_target_pairs={{0,8},{8,0},{16,24},{24,16},{1,9},{9,1},{17,25},{25,17},{2,10},{10... | collective-permute-start | bytes 5768 | tf_op jit(solution)/shard_map/ppermute | solution.py:978
  41.4 47.2 %collective-permute-start.14 = (bf16[960]{0:T(1024)(128)(2,1)S(1)}, bf16[960]{0:T(1024)(128)(2,1)S(1)}, u32[]{:S(2)}, u32[]{:S(2)}) collective-permute-start(bf16[960]{0:T(1024)(128)(2,1)S(1)} %pad_maximum_fusion.14), channel_id=1, source_target_pairs={{0,16},{8,24},{16,0},{24,8},{1,17},{9,25},{17,1},{25,9},{2,18},{10... | collective-permute-start | bytes 5768 | tf_op jit(solution)/shard_map/ppermute | solution.py:978
  41.6 47.0 %collective-permute-start.15 = (bf16[960]{0:T(1024)(128)(2,1)S(1)}, bf16[960]{0:T(1024)(128)(2,1)S(1)}, u32[]{:S(2)}, u32[]{:S(2)}) collective-permute-start(bf16[960]{0:T(1024)(128)(2,1)S(1)} %pad_maximum_fusion.14), channel_id=1, source_target_pairs={{0,24},{8,16},{16,8},{24,0},{1,25},{9,17},{17,9},{25,1},{2,26},{10... | collective-permute-start | bytes 5768 | tf_op jit(solution)/shard_map/ppermute | solution.py:978
  49.6 16.1 %collective-permute-start.6 = (bf16[96,1664]{1,0:T(8,128)(2,1)S(1)}, bf16[96,1664]{1,0:T(8,128)(2,1)S(1)}, u32[]{:S(2)}, u32[]{:S(2)}) collective-permute-start(bf16[96,1664]{1,0:T(8,128)(2,1)S(1)} %slice.352), channel_id=1, source_target_pairs={{0,8},{8,0},{16,24},{24,16},{1,9},{9,1},{17,25},{25,17},{2,10},{10... | collective-permute-start | bytes 958472 | tf_op jit(solution)/shard_map/ppermute | solution.py:978
  51.0 15.5 %collective-permute-start.7 = (bf16[96,1664]{1,0:T(8,128)(2,1)S(1)}, bf16[96,1664]{1,0:T(8,128)(2,1)S(1)}, u32[]{:S(2)}, u32[]{:S(2)}) collective-permute-start(bf16[96,1664]{1,0:T(8,128)(2,1)S(1)} %slice.353), channel_id=1, source_target_pairs={{0,16},{8,24},{16,0},{24,8},{1,17},{9,25},{17,1},{25,9},{2,18},{10... | collective-permute-start | bytes 958472 | tf_op jit(solution)/shard_map/ppermute | solution.py:978
  67.2 22.8 %collective-permute-start.8 = (bf16[768,1664]{1,0:T(8,128)(2,1)}, bf16[768,1664]{1,0:T(8,128)(2,1)}, u32[]{:S(2)}, u32[]{:S(2)}) collective-permute-start(bf16[768,1664]{1,0:T(8,128)(2,1)} %constant_dynamic-update-slice_fusion.refs_2_.refs_5_), channel_id=1, source_target_pairs={{0,1},{1,0},{2,3},{3,2},{4,5},{5,4},{6,7},{7,6},{8,9},{9,8},{10,11... | collective-permute-start | bytes 7667720 | tf_op jit(solution)/shard_map/ppermute | solution.py:978
  101.0 66.2 %collective-permute-start.11 = (bf16[192,6144]{1,0:T(8,128)(2,1)}, bf16[192,6144]{1,0:T(8,128)(2,1)S(1)}, u32[]{:S(2)}, u32[]{:S(2)}) collective-permute-start(bf16[192,6144]{1,0:T(8,128)(2,1)} %bitcast_dynamic-update-slice_fusion.1), channel_id=1, source_target_pairs={{0,8},{8,0},{16,24},{24,16},{1,9},{9,1},{17,25},{25,17},{2,10},{10... | collective-permute-start | bytes 7077896 | tf_op jit(solution)/shard_map/ppermute | solution.py:978
  102.9 64.4 %collective-permute-start.12 = (bf16[192,6144]{1,0:T(8,128)(2,1)}, bf16[192,6144]{1,0:T(8,128)(2,1)}, u32[]{:S(2)}, u32[]{:S(2)}) collective-permute-start(bf16[192,6144]{1,0:T(8,128)(2,1)} %bitcast_dynamic-update-slice_fusion.1), channel_id=1, source_target_pairs={{0,16},{8,24},{16,0},{24,8},{1,17},{9,25},{17,1},{25,9},{2,18},{10... | collective-permute-start | bytes 7077896 | tf_op jit(solution)/shard_map/ppermute | solution.py:978
  169.7 27.3 %collective-permute-start.16 = (bf16[96,6144]{1,0:T(8,128)(2,1)}, bf16[96,6144]{1,0:T(8,128)(2,1)}, u32[]{:S(2)}, u32[]{:S(2)}) collective-permute-start(bf16[96,6144]{1,0:T(8,128)(2,1)} %slice.281), channel_id=1, source_target_pairs={{0,8},{8,0},{16,24},{24,16},{1,9},{9,1},{17,25},{25,17},{2,10},{10... | collective-permute-start | bytes 3538952 | tf_op jit(solution)/shard_map/ppermute | solution.py:978
  172.0 47.5 %collective-permute-start.17 = (bf16[96,6144]{1,0:T(8,128)(2,1)}, bf16[96,6144]{1,0:T(8,128)(2,1)}, u32[]{:S(2)}, u32[]{:S(2)}) collective-permute-start(bf16[96,6144]{1,0:T(8,128)(2,1)} %slice.282), channel_id=1, source_target_pairs={{0,16},{8,24},{16,0},{24,8},{1,17},{9,25},{17,1},{25,9},{2,18},{10... | collective-permute-start | bytes 3538952 | tf_op jit(solution)/shard_map/ppermute | solution.py:978
  178.0 34.2 %all-to-all-start = ((bf16[8,96,768]{2,1,0:T(8,128)(2,1)}), bf16[8,96,768]{2,1,0:T(8,128)(2,1)S(1)}, u32[]{:S(2)}, u32[]{:S(2)}) async-start(bf16[8,96,768]{2,1,0:T(8,128)(2,1)} %bitcast.176), calls=%async_computation | async-start | bytes 2359296 | tf_op jit(solution)/shard_map/all_to_all | solution.py:1255
  212.2 33.1 %all-to-all-start.1 = ((bf16[8,96,768]{2,1,0:T(8,128)(2,1)}), bf16[8,96,768]{2,1,0:T(8,128)(2,1)S(1)}, u32[]{:S(2)}, u32[]{:S(2)}) async-start(bf16[8,96,768]{2,1,0:T(8,128)(2,1)} %bitcast.20), calls=%async_computation.1 | async-start | bytes 2359296 | tf_op jit(solution)/shard_map/all_to_all | solution.py:1255
  245.3 36.0 %all-to-all-start.2 = ((bf16[8,96,768]{2,1,0:T(8,128)(2,1)}), bf16[8,96,768]{2,1,0:T(8,128)(2,1)S(1)}, u32[]{:S(2)}, u32[]{:S(2)}) async-start(bf16[8,96,768]{2,1,0:T(8,128)(2,1)} %bitcast.175), calls=%async_computation.2 | async-start | bytes 2359296 | tf_op jit(solution)/shard_map/all_to_all | solution.py:1255
  252.3 178.9 %reduce-scatter.2.cloned.1.call-start = ((), (), s32[]{:S(2)}) async-start(), calls=%async_computation.6 | async-start | bytes 11796480 | tf_op jit(solution)/shard_map/reduce_scatter | solution.py:1268
  282.3 31.0 %all-to-all-start.3 = ((bf16[8,96,768]{2,1,0:T(8,128)(2,1)}), bf16[8,96,768]{2,1,0:T(8,128)(2,1)S(1)}, u32[]{:S(2)}, u32[]{:S(2)}) async-start(bf16[8,96,768]{2,1,0:T(8,128)(2,1)} %bitcast.25), calls=%async_computation.3 | async-start | bytes 2359296 | tf_op jit(solution)/shard_map/all_to_all | solution.py:1255
  338.5 6.0 %collective-permute-start.20 = (bf16[416,1152]{1,0:T(8,128)(2,1)}, bf16[416,1152]{1,0:T(8,128)(2,1)S(1)}, u32[]{:S(2)}, u32[]{:S(2)}) collective-permute-start(bf16[416,1152]{1,0:T(8,128)(2,1)} %get-tuple-element.132), channel_id=1, source_target_pairs={{0,1},{1,0},{2,3},{3,2},{4,5},{5,4},{6,7},{7,6},{8,9},{9,8},{10,11... | collective-permute-start | bytes 2875400 | tf_op jit(solution)/shard_map/ppermute | solution.py:978
  339.6 52.4 %collective-permute-start.24 = (bf16[416,3072]{1,0:T(8,128)(2,1)}, bf16[416,3072]{1,0:T(8,128)(2,1)}, u32[]{:S(2)}, u32[]{:S(2)}) collective-permute-start(bf16[416,3072]{1,0:T(8,128)(2,1)} %get-tuple-element.141.act_ref), channel_id=1, source_target_pairs={{0,1},{1,0},{2,3},{3,2},{4,5},{5,4},{6,7},{7,6},{8,9},{9,8},{10,11... | collective-permute-start | bytes 7667720 | tf_op jit(solution)/shard_map/ppermute | solution.py:978
  354.6 33.4 %collective-permute-start.26 = (bf16[2,48,1536]{2,1,0:T(8,128)(2,1)}, bf16[2,48,1536]{2,1,0:T(8,128)(2,1)S(1)}, u32[]{:S(2)}, u32[]{:S(2)}) collective-permute-start(bf16[2,48,1536]{2,1,0:T(8,128)(2,1)} %get-tuple-element.260), channel_id=1, source_target_pairs={{0,8},{8,0},{16,24},{24,16},{1,9},{9,1},{17,25},{25,17},{2,10},{10... | collective-permute-start | bytes 884744 | tf_op jit(solution)/shard_map/ppermute | solution.py:978
  356.3 31.7 %collective-permute-start.27 = (bf16[2,48,1536]{2,1,0:T(8,128)(2,1)}, bf16[2,48,1536]{2,1,0:T(8,128)(2,1)S(1)}, u32[]{:S(2)}, u32[]{:S(2)}) collective-permute-start(bf16[2,48,1536]{2,1,0:T(8,128)(2,1)} %get-tuple-element.261), channel_id=1, source_target_pairs={{0,16},{8,24},{16,0},{24,8},{1,17},{9,25},{17,1},{25,9},{2,18},{10... | collective-permute-start | bytes 884744 | tf_op jit(solution)/shard_map/ppermute | solution.py:978
  369.6 22.4 %collective-permute-start.23 = (bf16[416,1536]{1,0:T(8,128)(2,1)}, bf16[416,1536]{1,0:T(8,128)(2,1)}, u32[]{:S(2)}, u32[]{:S(2)}) collective-permute-start(bf16[416,1536]{1,0:T(8,128)(2,1)} %get-tuple-element.140), channel_id=1, source_target_pairs={{0,1},{1,0},{2,3},{3,2},{4,5},{5,4},{6,7},{7,6},{8,9},{9,8},{10,11... | collective-permute-start | bytes 3833864 | tf_op jit(solution)/shard_map/ppermute | solution.py:978
  381.4 57.2 %collective-permute-start.32 = (bf16[416,768]{1,0:T(8,128)(2,1)}, bf16[416,768]{1,0:T(8,128)(2,1)}, u32[]{:S(2)}, u32[]{:S(2)}) collective-permute-start(bf16[416,768]{1,0:T(8,128)(2,1)} %get-tuple-element.155.refs_0_), channel_id=1, source_target_pairs={{0,1},{1,0},{2,3},{3,2},{4,5},{5,4},{6,7},{7,6},{8,9},{9,8},{10,11... | collective-permute-start | bytes 1916936 | tf_op jit(solution)/shard_map/ppermute | solution.py:978
  390.3 39.2 %collective-permute-start.29 = (bf16[4,48,1536]{2,1,0:T(8,128)(2,1)S(1)}, bf16[4,48,1536]{2,1,0:T(8,128)(2,1)}, u32[]{:S(2)}, u32[]{:S(2)}) collective-permute-start(bf16[4,48,1536]{2,1,0:T(8,128)(2,1)S(1)} %pad_maximum_fusion.5), channel_id=1, source_target_pairs={{0,16},{8,24},{16,0},{24,8},{1,17},{9,25},{17,1},{25,9},{2,18},{10... | collective-permute-start | bytes 1769480 | tf_op jit(solution)/shard_map/ppermute | solution.py:978
  392.0 38.4 %collective-permute-start.28 = (bf16[4,48,1536]{2,1,0:T(8,128)(2,1)S(1)}, bf16[4,48,1536]{2,1,0:T(8,128)(2,1)}, u32[]{:S(2)}, u32[]{:S(2)}) collective-permute-start(bf16[4,48,1536]{2,1,0:T(8,128)(2,1)S(1)} %pad_maximum_fusion.4), channel_id=1, source_target_pairs={{0,8},{8,0},{16,24},{24,16},{1,9},{9,1},{17,25},{25,17},{2,10},{10... | collective-permute-start | bytes 1769480 | tf_op jit(solution)/shard_map/ppermute | solution.py:978
  406.1 24.4 %collective-permute-start.30 = (bf16[2,384,384]{2,1,0:T(8,128)(2,1)S(1)}, bf16[2,384,384]{2,1,0:T(8,128)(2,1)}, u32[]{:S(2)}, u32[]{:S(2)}) collective-permute-start(bf16[2,384,384]{2,1,0:T(8,128)(2,1)S(1)} %get-tuple-element.244), channel_id=1, source_target_pairs={{0,8},{8,0},{16,24},{24,16},{1,9},{9,1},{17,25},{25,17},{2,10},{10... | collective-permute-start | bytes 1769480 | tf_op jit(solution)/shard_map/ppermute | solution.py:978
  407.7 23.5 %collective-permute-start.31 = (bf16[2,384,384]{2,1,0:T(8,128)(2,1)S(1)}, bf16[2,384,384]{2,1,0:T(8,128)(2,1)}, u32[]{:S(2)}, u32[]{:S(2)}) collective-permute-start(bf16[2,384,384]{2,1,0:T(8,128)(2,1)S(1)} %get-tuple-element.245), channel_id=1, source_target_pairs={{0,16},{8,24},{16,0},{24,8},{1,17},{9,25},{17,1},{25,9},{2,18},{10... | collective-permute-start | bytes 1769480 | tf_op jit(solution)/shard_map/ppermute | solution.py:978
  429.5 9.2 %collective-permute-start.34 = (bf16[416,768]{1,0:T(8,128)(2,1)}, bf16[416,768]{1,0:T(8,128)(2,1)}, u32[]{:S(2)}, u32[]{:S(2)}) collective-permute-start(bf16[416,768]{1,0:T(8,128)(2,1)} %get-tuple-element.163.refs_4_), channel_id=1, source_target_pairs={{0,1},{1,0},{2,3},{3,2},{4,5},{5,4},{6,7},{7,6},{8,9},{9,8},{10,11... | collective-permute-start | bytes 1916936 | tf_op jit(solution)/shard_map/ppermute | solution.py:978
  430.5 9.5 %collective-permute-start.33 = (bf16[416,1152]{1,0:T(8,128)(2,1)}, bf16[416,1152]{1,0:T(8,128)(2,1)}, u32[]{:S(2)}, u32[]{:S(2)}) collective-permute-start(bf16[416,1152]{1,0:T(8,128)(2,1)} %get-tuple-element.162), channel_id=1, source_target_pairs={{0,1},{1,0},{2,3},{3,2},{4,5},{5,4},{6,7},{7,6},{8,9},{9,8},{10,11... | collective-permute-start | bytes 2875400 | tf_op jit(solution)/shard_map/ppermute | solution.py:978
  430.5 9.5 %collective-permute-start.35 = (bf16[416,384]{1,0:T(8,128)(2,1)}, bf16[416,384]{1,0:T(8,128)(2,1)}, u32[]{:S(2)}, u32[]{:S(2)}) collective-permute-start(bf16[416,384]{1,0:T(8,128)(2,1)} %get-tuple-element.165), channel_id=1, source_target_pairs={{0,1},{1,0},{2,3},{3,2},{4,5},{5,4},{6,7},{7,6},{8,9},{9,8},{10,11... | collective-permute-start | bytes 958472 | tf_op jit(solution)/shard_map/ppermute | solution.py:978
  432.7 19.1 %collective-permute-start.40 = (bf16[48,1536]{1,0:T(8,128)(2,1)S(1)}, bf16[48,1536]{1,0:T(8,128)(2,1)S(1)}, u32[]{:S(2)}, u32[]{:S(2)}) collective-permute-start(bf16[48,1536]{1,0:T(8,128)(2,1)S(1)} %get-tuple-element.272), channel_id=1, source_target_pairs={{0,2},{1,3},{2,0},{3,1},{4,6},{5,7},{6,4},{7,5},{8,10},{9,11},{10,... | collective-permute-start | bytes 442376 | tf_op jit(solution)/shard_map/ppermute | solution.py:978
  438.6 13.5 %collective-permute-start.41 = (bf16[48,1536]{1,0:T(8,128)(2,1)S(1)}, bf16[48,1536]{1,0:T(8,128)(2,1)S(1)}, u32[]{:S(2)}, u32[]{:S(2)}) collective-permute-start(bf16[48,1536]{1,0:T(8,128)(2,1)S(1)} %get-tuple-element.271), channel_id=1, source_target_pairs={{0,4},{1,5},{2,6},{3,7},{4,0},{5,1},{6,2},{7,3},{8,12},{9,13},{10,... | collective-permute-start | bytes 442376 | tf_op jit(solution)/shard_map/ppermute | solution.py:978
  438.7 35.1 %collective-permute-start.39 = (bf16[4,384,384]{2,1,0:T(8,128)(2,1)S(1)}, bf16[4,384,384]{2,1,0:T(8,128)(2,1)S(1)}, u32[]{:S(2)}, u32[]{:S(2)}) collective-permute-start(bf16[4,384,384]{2,1,0:T(8,128)(2,1)S(1)} %pad_maximum_fusion.1), channel_id=1, source_target_pairs={{0,16},{8,24},{16,0},{24,8},{1,17},{9,25},{17,1},{25,9},{2,18},{10... | collective-permute-start | bytes 3538952 | tf_op jit(solution)/shard_map/ppermute | solution.py:978
  440.0 33.7 %collective-permute-start.38 = (bf16[4,384,384]{2,1,0:T(8,128)(2,1)S(1)}, bf16[4,384,384]{2,1,0:T(8,128)(2,1)S(1)}, u32[]{:S(2)}, u32[]{:S(2)}) collective-permute-start(bf16[4,384,384]{2,1,0:T(8,128)(2,1)S(1)} %pad_maximum_fusion), channel_id=1, source_target_pairs={{0,8},{8,0},{16,24},{24,16},{1,9},{9,1},{17,25},{25,17},{2,10},{10... | collective-permute-start | bytes 3538952 | tf_op jit(solution)/shard_map/ppermute | solution.py:978
  448.6 25.1 %collective-permute-start.36 = (bf16[2,48,1664]{2,1,0:T(8,128)(2,1)S(1)}, bf16[2,48,1664]{2,1,0:T(8,128)(2,1)S(1)}, u32[]{:S(2)}, u32[]{:S(2)}) collective-permute-start(bf16[2,48,1664]{2,1,0:T(8,128)(2,1)S(1)} %get-tuple-element.247), channel_id=1, source_target_pairs={{0,8},{8,0},{16,24},{24,16},{1,9},{9,1},{17,25},{25,17},{2,10},{10... | collective-permute-start | bytes 958472 | tf_op jit(solution)/shard_map/ppermute | solution.py:978
  451.8 21.9 %collective-permute-start.37 = (bf16[2,48,1664]{2,1,0:T(8,128)(2,1)S(1)}, bf16[2,48,1664]{2,1,0:T(8,128)(2,1)S(1)}, u32[]{:S(2)}, u32[]{:S(2)}) collective-permute-start(bf16[2,48,1664]{2,1,0:T(8,128)(2,1)S(1)} %get-tuple-element.249), channel_id=1, source_target_pairs={{0,16},{8,24},{16,0},{24,8},{1,17},{9,25},{17,1},{25,9},{2,18},{10... | collective-permute-start | bytes 958472 | tf_op jit(solution)/shard_map/ppermute | solution.py:978
  473.9 6.6 %collective-permute-start.53 = (bf16[24,1536]{1,0:T(8,128)(2,1)S(1)}, bf16[24,1536]{1,0:T(8,128)(2,1)S(1)}, u32[]{:S(2)}, u32[]{:S(2)}) collective-permute-start(bf16[24,1536]{1,0:T(8,128)(2,1)S(1)} %dynamic-slice_convert_fusion.1), channel_id=1, source_target_pairs={{0,1},{1,0},{2,3},{3,2},{4,5},{5,4},{6,7},{7,6},{8,9},{9,8},{10,11... | collective-permute-start | bytes 221192 | tf_op jit(solution)/shard_map/ppermute | solution.py:978
  477.3 13.5 %collective-permute-start.49 = (bf16[384,384]{1,0:T(8,128)(2,1)S(1)}, bf16[384,384]{1,0:T(8,128)(2,1)S(1)}, u32[]{:S(2)}, u32[]{:S(2)}) collective-permute-start(bf16[384,384]{1,0:T(8,128)(2,1)S(1)} %get-tuple-element.262), channel_id=1, source_target_pairs={{0,2},{1,3},{2,0},{3,1},{4,6},{5,7},{6,4},{7,5},{8,10},{9,11},{10,... | collective-permute-start | bytes 884744 | tf_op jit(solution)/shard_map/ppermute | solution.py:978
  478.8 14.2 %collective-permute-start.50 = (bf16[384,384]{1,0:T(8,128)(2,1)S(1)}, bf16[384,384]{1,0:T(8,128)(2,1)S(1)}, u32[]{:S(2)}, u32[]{:S(2)}) collective-permute-start(bf16[384,384]{1,0:T(8,128)(2,1)S(1)} %get-tuple-element.264), channel_id=1, source_target_pairs={{0,4},{1,5},{2,6},{3,7},{4,0},{5,1},{6,2},{7,3},{8,12},{9,13},{10,... | collective-permute-start | bytes 884744 | tf_op jit(solution)/shard_map/ppermute | solution.py:978
  479.7 26.1 %collective-permute-start.51 = (bf16[384,384]{1,0:T(8,128)(2,1)S(1)}, bf16[384,384]{1,0:T(8,128)(2,1)S(1)}, u32[]{:S(2)}, u32[]{:S(2)}) collective-permute-start(bf16[384,384]{1,0:T(8,128)(2,1)S(1)} %get-tuple-element.263), channel_id=1, source_target_pairs={{0,6},{1,7},{2,4},{3,5},{4,2},{5,3},{6,0},{7,1},{8,14},{9,15},{10,... | collective-permute-start | bytes 884744 | tf_op jit(solution)/shard_map/ppermute | solution.py:978
  480.3 28.2 %collective-permute-start.43 = (bf16[4,48,1664]{2,1,0:T(8,128)(2,1)S(1)}, bf16[4,48,1664]{2,1,0:T(8,128)(2,1)S(1)}, u32[]{:S(2)}, u32[]{:S(2)}) collective-permute-start(bf16[4,48,1664]{2,1,0:T(8,128)(2,1)S(1)} %pad_maximum_fusion.2), channel_id=1, source_target_pairs={{0,8},{8,0},{16,24},{24,16},{1,9},{9,1},{17,25},{25,17},{2,10},{10... | collective-permute-start | bytes 1916936 | tf_op jit(solution)/shard_map/ppermute | solution.py:978
  480.5 28.1 %collective-permute-start.44 = (bf16[4,48,1664]{2,1,0:T(8,128)(2,1)S(1)}, bf16[4,48,1664]{2,1,0:T(8,128)(2,1)S(1)}, u32[]{:S(2)}, u32[]{:S(2)}) collective-permute-start(bf16[4,48,1664]{2,1,0:T(8,128)(2,1)S(1)} %pad_maximum_fusion.3), channel_id=1, source_target_pairs={{0,16},{8,24},{16,0},{24,8},{1,17},{9,25},{17,1},{25,9},{2,18},{10... | collective-permute-start | bytes 1916936 | tf_op jit(solution)/shard_map/ppermute | solution.py:978
  508.9 5.8 %collective-permute-start.45 = (bf16[48,1664]{1,0:T(8,128)(2,1)S(1)}, bf16[48,1664]{1,0:T(8,128)(2,1)S(1)}, u32[]{:S(2)}, u32[]{:S(2)}) collective-permute-start(bf16[48,1664]{1,0:T(8,128)(2,1)S(1)} %get-tuple-element.265), channel_id=1, source_target_pairs={{0,2},{1,3},{2,0},{3,1},{4,6},{5,7},{6,4},{7,5},{8,10},{9,11},{10,... | collective-permute-start | bytes 479240 | tf_op jit(solution)/shard_map/ppermute | solution.py:978
  508.9 9.6 %collective-permute-start.46 = (bf16[48,1664]{1,0:T(8,128)(2,1)S(1)}, bf16[48,1664]{1,0:T(8,128)(2,1)S(1)}, u32[]{:S(2)}, u32[]{:S(2)}) collective-permute-start(bf16[48,1664]{1,0:T(8,128)(2,1)S(1)} %get-tuple-element.267), channel_id=1, source_target_pairs={{0,4},{1,5},{2,6},{3,7},{4,0},{5,1},{6,2},{7,3},{8,12},{9,13},{10,... | collective-permute-start | bytes 479240 | tf_op jit(solution)/shard_map/ppermute | solution.py:978
  511.2 14.3 %collective-permute-start.47 = (bf16[48,1664]{1,0:T(8,128)(2,1)S(1)}, bf16[48,1664]{1,0:T(8,128)(2,1)S(1)}, u32[]{:S(2)}, u32[]{:S(2)}) collective-permute-start(bf16[48,1664]{1,0:T(8,128)(2,1)S(1)} %get-tuple-element.266), channel_id=1, source_target_pairs={{0,6},{1,7},{2,4},{3,5},{4,2},{5,3},{6,0},{7,1},{8,14},{9,15},{10,... | collective-permute-start | bytes 479240 | tf_op jit(solution)/shard_map/ppermute | solution.py:978
  (50 other events, 425.0 us)
Sparse Core Ops, SparseCore 0:
  13.6 130.1 all-gather.1
  281.5 101.6 reduce-scatter.1
where the time goes:
time: 550 us; the launch traced here: 541 us
  waiting for transfers between devices  181 us (33%)
  Pallas kernels  178 us (32%)
  starting transfers between devices  87.7 us (16%)
  local copies, waits for them, and re-layouts  58.2 us (11%)
  other arithmetic  20.5 us (4%)
  between operations  16.3 us (3%)
    pallas_call x16, Pallas kernels, run_kernel(): pl.pallas_call(kernel, out_shape=list(outs), compiler_params=pltpu.Compil...  178 us
    ppermute x57, waiting for transfers between devices, trade(): lax.ppermute(value, axis_name, [(place, place ^ mask) for place in range(...  111 us
    ppermute x57, starting transfers between devices, trade(): lax.ppermute(value, axis_name, [(place, place ^ mask) for place in range(...  59.8 us
    all_gather x1, waiting for transfers between devices, per_device(): pack = lax.all_gather(later, ('fsdp', 'expert'), axis=0, tiled=True)  37.3 us
    all_to_all x4, waiting for transfers between devices, exchange(): lax.all_to_all(array.reshape(experts, capacity, width), 'expert', split_a...  32.7 us
    unnamed x107, local copies, waits for them, and re-layouts  30.8 us
    all_to_all x4, starting transfers between devices, exchange(): lax.all_to_all(array.reshape(experts, capacity, width), 'expert', split_a...  27.8 us
  transfers between devices with their start and end apart: 63, of which 28 were waited for; matrix products, arithmetic and copies ran while one was open for 12% of the time, Pallas kernels for 33%

commit v1 on v0

--- a/solution.py
+++ b/solution.py
@@ -56,7 +56,7 @@
         out_shape=list(outs),
         compiler_params=pltpu.CompilerParams(vmem_limit_bytes=56 * 1024 * 1024),
         cost_estimate=pl.CostEstimate(
-            flops=int(micros * 1.15e9), bytes_accessed=nbytes, transcendentals=0
+            flops=int(micros * 0.4e9), bytes_accessed=nbytes, transcendentals=0
         ),
         **more,
     )(*scalars, *arrays, *far)
@@ -147,20 +147,6 @@
     return copies
 
 
-def pack_copies(pack_ref, target, sems):
-    groups, cores, lines, wide = pack_ref.shape
-    half_cols = target.shape[1] // cores
-    return [
-        pltpu.make_async_copy(
-            pack_ref.at[group, core, :, wide - half_cols : wide],
-            target.at[span(group, lines), span(core, half_cols)],
-            sems.at[group * cores + core],
-        )
-        for group in range(groups)
-        for core in range(cores)
-    ]
-
-
 def score_parts(query, key, mask, keep):
     scores = mul_turned(query * (0.125 * mask).astype(LOW), key)
     scores = jnp.where(keep, scores, -1e30)
@@ -174,10 +160,12 @@
             place_ref, x_ref, near_ref, other_ref,
             an_ref, qkv_ref, o_ref, out_ref, vec_ref, wide_ref, router_ref, w_ref, sems,
         ) = refs
-        copies = near_copies(place_ref, near_ref, other_ref, w_ref, sems)
     else:
-        place_ref, x_ref, vec_ref, pack_ref, an_ref, qkv_ref, o_ref, out_ref, w_ref, sems = refs
-        copies = pack_copies(pack_ref, w_ref, sems)
+        (
+            place_ref, x_ref, vec_ref, near_ref, other_ref,
+            an_ref, qkv_ref, o_ref, out_ref, w_ref, sems,
+        ) = refs
+    copies = near_copies(place_ref, near_ref, other_ref, w_ref, sems)
     gain, shift, q_line, v_line, o_line = lines_of
     for copy in copies:
         copy.start()
@@ -240,11 +228,8 @@
 
 
 def weight_scratch(width, pieces, planes):
-    if len(pieces) == 2:
-        cols, count = 2 * pieces[0].shape[1], 2 * planes
-    else:
-        cols, count = 4 * width, pieces[0].shape[0] * pieces[0].shape[1]
-    return [pltpu.VMEM((width, cols), LOW), pltpu.SemaphoreType.DMA((count,))]
+    cols = 2 * pieces[0].shape[1]
+    return [pltpu.VMEM((width, cols), LOW), pltpu.SemaphoreType.DMA((2 * planes,))]
 
 
 def attend_forward(place, x, vec, pieces, planes, lines_of, length, images, experts, inner):
@@ -277,13 +262,12 @@
             din_ref, mine_ref, away_ref, low_mine_ref, low_away_ref, small_ref,
             dol_ref, mix_ref, grad_ref, sums_ref, w_ref, sems,
         ) = refs
-        copies = near_copies(place_ref, near_ref, other_ref, w_ref, sems)
     else:
         (
-            pack_ref, din_ref, mine_ref, away_ref, low_mine_ref, low_away_ref, sums_ref,
+            near_ref, other_ref, din_ref, mine_ref, away_ref, low_mine_ref, low_away_ref, sums_ref,
             dol_ref, mix_ref, grad_ref, w_ref, sems,
         ) = refs
-        copies = pack_copies(pack_ref, w_ref, sems)
+    copies = near_copies(place_ref, near_ref, other_ref, w_ref, sems)
     for copy in copies:
         copy.start()
     rows, width = x_ref.shape
@@ -608,12 +592,19 @@
     return jnp.where(hit, 1.0, 0.0).astype(LOW)
 
 
+def slot_lanes(expert, slots, capacity):
+    line = lax.broadcasted_iota(jnp.int32, (slots, 128), 0)
+    lane = lax.broadcasted_iota(jnp.int32, (slots, 128), 1)
+    return jnp.where((line == lane + expert * capacity) & (lane < capacity), 1.0, 0.0).astype(LOW)
+
+
 def dispatch_kernel(
-    experts, lines_of, x_ref, vec_ref, router_ref, route_ref, target_ref, up_ref,
-    mn_ref, gate_ref, pick_ref, out_ref, grad_ref, spot_ref, low_ref,
+    experts, lines_of, x_ref, vec_ref, router_ref, route_ref, target_ref,
+    mn_ref, gate_ref, pick_ref, out_ref, spot_ref,
 ):
     gain, shift = lines_of
     slots = out_ref.shape[0]
+    capacity = slots // experts
     mn_ref[...] = norm_low(x_ref[...], vec_ref[gain : gain + 1, :], vec_ref[shift : shift + 1, :])
     logits = mul(mn_ref[...], router_ref[...])
     lane = lax.broadcasted_iota(jnp.int32, logits.shape, 1)
@@ -625,21 +616,30 @@
         jnp.sum(jnp.where(lane == route_ref[:, k : k + 1], gate, 0.0), axis=-1, keepdims=True)
         for k in range(2)
     ]
-    pick_ref[...] = jnp.where(lane == 0, picks[0], jnp.where(lane == 1, picks[1], 0.0))
-    spots = [one_hot_rows(target_ref[k : k + 1, :], slots) for k in range(2)]
-    spot_ref[0, :, :] = spots[0]
-    spot_ref[1, :, :] = spots[1]
-    low_ref[0, :, :] = (picks[0] * up_ref[...].astype(FULL)).astype(LOW)
-    low_ref[1, :, :] = (picks[1] * up_ref[...].astype(FULL)).astype(LOW)
+    pick = jnp.where(lane == 0, picks[0], jnp.where(lane == 1, picks[1], 0.0))
+    pick_ref[...] = pick
+    turned = pick.T
+    for k in range(2):
+        spot_ref[k, :, :] = one_hot_rows(target_ref[k : k + 1, :], slots)
     for at in range(out_ref.shape[1] // TILE):
         cols = span(at, TILE)
         out_ref[:, cols] = mul(spot_ref[0, :, :] + spot_ref[1, :, :], mn_ref[:, cols]).astype(LOW)
-        grad_ref[:, cols] = (
-            mul(spot_ref[0, :, :], low_ref[0, :, cols]) + mul(spot_ref[1, :, :], low_ref[1, :, cols])
+    row = lax.broadcasted_iota(jnp.int32, (16, 1), 0)
+    weights = jnp.zeros((16, slots), FULL)
+    for k in range(2):
+        high, rest = split_low(turned[k : k + 1, :])
+        both = jnp.where(row == 14, high.astype(FULL), jnp.where(row == 15, rest.astype(FULL), 0.0))
+        weights += mul_turned(both.astype(LOW), spot_ref[k, :, :])
+    weights = weights.astype(LOW)
+    for expert in range(experts):
+        lines = slice((expert + 1) * capacity - 16, (expert + 1) * capacity)
+        chosen = mul(weights, slot_lanes(expert, slots, capacity))
+        out_ref[lines, 0:128] = jnp.where(
+            row >= 14, chosen, out_ref[lines, 0:128].astype(FULL)
         ).astype(LOW)
 
 
-def dispatch(x, vec, router, routes, targets, up, experts, slots, lines_of):
+def dispatch(x, vec, router, routes, targets, experts, slots, lines_of):
     rows, width = x.shape
     return run_kernel(
         partial(dispatch_kernel, experts, lines_of),
@@ -648,11 +648,10 @@
             shape_of(rows, 128, FULL),
             shape_of(rows, 128, FULL),
             shape_of(slots, width, LOW),
-            shape_of(slots, width, LOW),
-        ],
-        [x, vec, router, routes, targets, up],
+        ],
+        [x, vec, router, routes, targets],
         6,
-        scratch=[pltpu.VMEM((2, slots, rows), LOW), pltpu.VMEM((2, rows, width), LOW)],
+        scratch=[pltpu.VMEM((2, slots, rows), LOW)],
     )
 
 
@@ -675,8 +674,28 @@
             ]
 
 
-def hidden_kernel(place_ref, x_ref, bias_ref, pack_ref, act_ref, slope_ref, w_ref):
+def hidden_kernel(
+    experts, place_ref, x_ref, bias_ref, pack_ref, up_ref, act_ref, slope_ref, dy_ref, last_ref, w_ref
+):
     restore(place_ref, pack_ref, w_ref)
+
+    @pl.when(pl.program_id(0) == 0)
+    def _():
+        capacity = x_ref.shape[0] // experts
+        row = lax.broadcasted_iota(jnp.int32, (128, 1), 0)
+        table = jnp.zeros((128, 128), FULL)
+        for group in range(experts):
+            mark = x_ref[(group + 1) * capacity - 16 : (group + 1) * capacity, 0:128].astype(FULL)
+            table = jnp.where(row == group, mark[14:15, :] + mark[15:16, :], table)
+        table = table.T
+        total = jnp.zeros(last_ref.shape, FULL)
+        for group in range(experts):
+            spots = slice(group * capacity, (group + 1) * capacity)
+            part = (table[0:capacity, group : group + 1] * up_ref[spots, :].astype(FULL)).astype(LOW)
+            dy_ref[spots, :] = part
+            total += jnp.sum(part.astype(FULL), axis=0, keepdims=True)
+        last_ref[...] = total
+
     for at in range(act_ref.shape[1] // TILE):
         cols = span(at, TILE)
         weight = w_ref[:, :, cols].reshape(x_ref.shape[1], TILE)
@@ -685,14 +704,19 @@
         slope_ref[:, cols] = slope
 
 
-def hidden_forward(place, x, bias, weight, planes):
+def hidden_forward(place, x, bias, weight, up, planes, experts):
     rows, width = x.shape
     inner = bias.shape[1]
     part = 768
     return run_kernel(
-        hidden_kernel,
-        [shape_of(rows, inner, LOW), shape_of(rows, inner, LOW)],
-        [x, bias, weight],
+        partial(hidden_kernel, experts),
+        [
+            shape_of(rows, inner, LOW),
+            shape_of(rows, inner, LOW),
+            shape_of(rows, width, LOW),
+            shape_of(1, width, FULL),
+        ],
+        [x, bias, weight, up],
         11,
         scalars=[place],
         scratch=[pltpu.VMEM((planes, width // planes, part), LOW)],
@@ -701,12 +725,16 @@
             whole(x.shape),
             pl.BlockSpec((1, part), lambda at: (0, at)),
             pl.BlockSpec((width, part), lambda at: (0, at)),
-        ],
-        out_blocks=[pl.BlockSpec((rows, part), lambda at: (0, at))] * 2,
-    )
-
-
-def expert_out_kernel(lines, place_ref, act_ref, bias_ref, pack_ref, out_ref, sum_ref, w_ref):
+            whole(up.shape),
+        ],
+        out_blocks=[pl.BlockSpec((rows, part), lambda at: (0, at))] * 2
+        + [whole((rows, width)), whole((1, width))],
+    )
+
+
+def expert_out_kernel(
+    lines, experts, place_ref, act_ref, bias_ref, pack_ref, up_ref, out_ref, dot_ref, sum_ref, w_ref
+):
     step = pl.program_id(0)
     unfold_lines(place_ref, pack_ref, w_ref, lines)
 
@@ -720,44 +748,66 @@
 
     @pl.when(step == pl.num_programs(0) - 1)
     def _():
-        out_ref[...] = sum_ref[...].astype(LOW)
-
-
-def expert_out_forward(place, act, bias, weight, lines):
-    rows, width = act.shape[0], weight.shape[0]
+        result = sum_ref[...].astype(LOW)
+        out_ref[...] = result
+        dots = jnp.sum(result.astype(FULL) * up_ref[...].astype(FULL), axis=-1, keepdims=True)
+        capacity = result.shape[0] // experts
+        lane = lax.broadcasted_iota(jnp.int32, (capacity, 128), 1)
+        table = jnp.zeros((capacity, 128), FULL)
+        for group in range(experts):
+            table = jnp.where(lane == group, dots[group * capacity : (group + 1) * capacity], table)
+        if capacity < 128:
+            table = jnp.concatenate([table, jnp.zeros((128 - capacity, 128), FULL)], axis=0)
+        table = table.T
+        row = lax.broadcasted_iota(jnp.int32, (16, 1), 0)
+        for group in range(experts):
+            high, rest = split_low(table[group : group + 1, :])
+            both = jnp.where(
+                row == 14, high.astype(FULL), jnp.where(row == 15, rest.astype(FULL), 0.0)
+            )
+            dot_ref[group * 16 : (group + 1) * 16, :] = both.astype(LOW)
+
+
+def expert_out_forward(place, act, bias, weight, up, lines, experts):
+    rows, width = act.shape[0], weight.shape[1]
     inner = act.shape[1]
     part = 768
-    many = part * width // (inner * lines)
+    many = part // lines
     return run_kernel(
-        partial(expert_out_kernel, lines),
-        [shape_of(rows, width, LOW)],
-        [act, bias, weight],
-        8,
+        partial(expert_out_kernel, lines, experts),
+        [shape_of(rows, width, LOW), shape_of(experts * 16, 128, LOW)],
+        [act, bias, weight, up],
+        9,
         scalars=[place],
         scratch=[pltpu.VMEM((rows, width), FULL), pltpu.VMEM((part, width), LOW)],
         grid=(inner // part,),
         in_blocks=[
             pl.BlockSpec((rows, part), lambda at, place: (0, at ^ (place[0] // many))),
             pl.BlockSpec(bias.shape, lambda at, place: (0, 0)),
-            pl.BlockSpec((many * lines, inner), lambda at, place: (at, 1)),
-        ],
-        out_blocks=[pl.BlockSpec((rows, width), lambda at, place: (0, 0))],
+            pl.BlockSpec((part, width), lambda at, place: (at, 0)),
+            pl.BlockSpec(up.shape, lambda at, place: (0, 0)),
+        ],
+        out_blocks=[
+            pl.BlockSpec((rows, width), lambda at, place: (0, 0)),
+            pl.BlockSpec((experts * 16, 128), lambda at, place: (0, 0)),
+        ],
         ahead=True,
-    )[0]
+    )
 
 
 def expert_backward_kernel(
-    lines, place_ref, dy_ref, slope_ref, pack_ref, in_ref,
-    dh_ref, bias_ref, last_ref, back_ref, sum_ref, out_w_ref, in_w_ref,
+    lines, experts, place_ref, dy_ref, slope_ref, pack_ref, in_ref, dot_ref,
+    dh_ref, bias_ref, back_ref, sum_ref, out_w_ref, in_w_ref,
 ):
     step = pl.program_id(0)
+    rows = dy_ref.shape[0]
+    capacity = rows // experts
     unfold_lines(place_ref, pack_ref, out_w_ref, lines)
     restore(place_ref, in_ref, in_w_ref)
 
     @pl.when(step == 0)
     def _():
         sum_ref[...] = jnp.zeros(sum_ref.shape, FULL)
-        last_ref[...] = jnp.sum(dy_ref[...].astype(FULL), axis=0, keepdims=True)
 
     for at in range(slope_ref.shape[1] // TILE):
         cols = span(at, TILE)
@@ -766,21 +816,30 @@
         ).astype(LOW)
         dh_ref[:, cols] = part
         bias_ref[:, cols] = jnp.sum(part.astype(FULL), axis=0, keepdims=True)
-    planes, lines, part_cols = in_w_ref.shape
+    planes, tall, part_cols = in_w_ref.shape
     for at in range(2):
-        weight = in_w_ref[span(at, planes // 2), :, :].reshape(planes * lines // 2, part_cols)
-        sum_ref[:, span(at, planes * lines // 2)] += mul_turned(dh_ref[...], weight)
+        weight = in_w_ref[span(at, planes // 2), :, :].reshape(planes * tall // 2, part_cols)
+        sum_ref[:, span(at, planes * tall // 2)] += mul_turned(dh_ref[...], weight)
 
     @pl.when(step == pl.num_programs(0) - 1)
     def _():
         back_ref[...] = sum_ref[...].astype(LOW)
-
-
-def expert_backward(place, dy, slope, weight, lines):
+        row = lax.broadcasted_iota(jnp.int32, (16, 1), 0)
+        for group in range(experts):
+            spots = slice((group + 1) * capacity - 16, (group + 1) * capacity)
+            back_ref[spots, 0:128] = jnp.where(
+                row >= 14,
+                dot_ref[group * 16 : (group + 1) * 16, :].astype(FULL),
+                sum_ref[spots, 0:128],
+            ).astype(LOW)
+
+
+def expert_backward(place, dy, slope, w_out, w_in, dots, lines, experts):
     rows, width = dy.shape
     inner = slope.shape[1]
+    planes = inner // lines
     part = 768
-    many = part * width // (inner * lines)
+    many = part // lines
 
     def moved(at, place):
         return (0, at ^ (place[0] // many))
@@ -789,90 +848,91 @@
         return (0, 0)
 
     return run_kernel(
-        partial(expert_backward_kernel, lines),
+        partial(expert_backward_kernel, lines, experts),
         [
             shape_of(rows, inner, LOW),
             shape_of(1, inner, FULL),
-            shape_of(1, width, FULL),
             shape_of(rows, width, LOW),
         ],
-        [dy, slope, weight, weight],
-        14,
+        [dy, slope, w_out, w_in, dots],
+        15,
         scalars=[place],
         scratch=[
             pltpu.VMEM((rows, width), FULL),
             pltpu.VMEM((part, width), LOW),
-            pltpu.VMEM((width // lines, lines, part), LOW),
+            pltpu.VMEM((planes, width // planes, part), LOW),
         ],
         grid=(inner // part,),
         in_blocks=[
-            pl.BlockSpec(dy.shape, fixed),
+            pl.BlockSpec((rows, width), fixed),
             pl.BlockSpec((rows, part), moved),
-            pl.BlockSpec((many * lines, inner), lambda at, place: (at, 1)),
+            pl.BlockSpec((part, width), lambda at, place: (at, 0)),
             pl.BlockSpec((width, part), moved),
+            pl.BlockSpec(dots.shape, fixed),
         ],
         out_blocks=[
             pl.BlockSpec((rows, part), moved),
             pl.BlockSpec((1, part), moved),
-            pl.BlockSpec((1, width), fixed),
             pl.BlockSpec((rows, width), fixed),
         ],
         ahead=True,
     )
 
 
-def combine_kernel(
-    x_ref, home_ref, gate_ref, pick_ref, route_ref, target_ref, up_ref, live_ref, mn_ref, router_ref,
-    out_ref, part_ref, router_grad_ref, spot_ref, dot_ref,
+def output_kernel(x_ref, home_ref, pick_ref, target_ref, live_ref, out_ref, spot_ref):
+    slots = home_ref.shape[0]
+    for k in range(2):
+        spot_ref[k, :, :] = one_hot_cols(target_ref[:, k : k + 1], slots)
+    for at in range(x_ref.shape[1] // TILE):
+        cols = span(at, TILE)
+        total = x_ref[:, cols]
+        for k in range(2):
+            total += pick_ref[:, k : k + 1] * mul(spot_ref[k, :, :], home_ref[:, cols])
+        out_ref[:, cols] = (total * live_ref[...]).astype(LOW)
+
+
+def output_rows(x, home, pick, targets, live):
+    rows, width = x.shape
+    return run_kernel(
+        output_kernel,
+        [shape_of(rows, width, LOW)],
+        [x, home, pick, targets, live],
+        7,
+        scratch=[pltpu.VMEM((2, rows, home.shape[0]), LOW)],
+    )[0]
+
+
+def return_kernel(
+    gain, experts, x_ref, vec_ref, home_ref, gate_ref, route_ref, target_ref, up_ref, mn_ref,
+    router_ref, out_ref, sums_ref, router_grad_ref, spot_ref,
 ):
     rows, width = x_ref.shape
     slots = home_ref.shape[0]
+    capacity = slots // experts
     for k in range(2):
         spot_ref[k, :, :] = one_hot_cols(target_ref[:, k : k + 1], slots)
+    line = jnp.zeros((16, slots), FULL)
+    for expert in range(experts):
+        marks = home_ref[(expert + 1) * capacity - 16 : (expert + 1) * capacity, 0:128]
+        line += mul_turned(marks, slot_lanes(expert, slots, capacity))
+    line = line.astype(LOW)
     lane = lax.broadcasted_iota(jnp.int32, (rows, 128), 1)
-    dot_ref[...] = jnp.zeros((rows, 128), FULL)
-
-    @pl.loop(0, width // TILE)
-    def _(at):
-        cols = span(at, TILE)
-        up = up_ref[:, cols].astype(FULL)
-        total = x_ref[:, cols]
-        for k in range(2):
-            fetched = mul(spot_ref[k, :, :], home_ref[:, cols])
-            total += pick_ref[:, k : k + 1] * fetched
-            dot_ref[...] += jnp.where(lane == k, jnp.sum(up * fetched, axis=-1, keepdims=True), 0.0)
-        out_ref[:, cols] = (total * live_ref[...]).astype(LOW)
-
     gate = gate_ref[...]
     spread = jnp.zeros((rows, 128), FULL)
     for k in range(2):
-        spread += jnp.where(lane == route_ref[:, k : k + 1], dot_ref[:, k : k + 1], 0.0)
+        dots = mul_turned(spot_ref[k, :, :], line)
+        spread += jnp.where(lane == route_ref[:, k : k + 1], dots[:, 14:15] + dots[:, 15:16], 0.0)
     logit = gate * (spread - jnp.sum(gate * spread, axis=-1, keepdims=True))
     high, rest = split_low(pltpu.roll(logit, 15, 1))
     router_grad_ref[...] = turned_mul(mn_ref[...], high) + turned_mul(mn_ref[...], rest)
     high, rest = split_low(logit)
-    part_ref[...] = mul_turned(high, router_ref[...]) + mul_turned(rest, router_ref[...])
-
-
-def combine(x, home, gate, pick, routes, targets, up, live, mn, router):
-    rows, width = x.shape
-    slots = home.shape[0]
-    return run_kernel(
-        combine_kernel,
-        [shape_of(rows, width, LOW), shape_of(rows, width, FULL), shape_of(width, 128, FULL)],
-        [x, home, gate, pick, routes, targets, up, live, mn, router],
-        8,
-        scratch=[pltpu.VMEM((2, rows, slots), LOW), pltpu.VMEM((rows, 128), FULL)],
-    )
-
-
-def return_kernel(gain, x_ref, vec_ref, part_ref, home_ref, target_ref, up_ref, out_ref, sums_ref, spot_ref):
-    width = x_ref.shape[1]
-    slots = home_ref.shape[0]
-    spot_ref[...] = one_hot_cols(target_ref[:, 0:1], slots) + one_hot_cols(target_ref[:, 1:2], slots)
     for at in range(width // TILE):
         cols = span(at, TILE)
-        out_ref[:, cols] = part_ref[:, cols] + mul(spot_ref[...], home_ref[:, cols])
+        out_ref[:, cols] = (
+            mul_turned(high, router_ref[cols, :])
+            + mul_turned(rest, router_ref[cols, :])
+            + mul(spot_ref[0, :, :] + spot_ref[1, :, :], home_ref[:, cols])
+        )
 
     grad, gain_sum, shift_sum = norm_back(x_ref[...], vec_ref[gain : gain + 1, :], out_ref[...])
     out_ref[...] = up_ref[...].astype(FULL) + grad
@@ -881,15 +941,16 @@
     sums_ref[2:8, :] = jnp.zeros((6, width), FULL)
 
 
-def return_grad(x, vec, part, home, targets, up, gain):
+def return_grad(x, vec, home, gate, routes, targets, up, mn, router, gain, experts, after):
     rows, width = x.shape
     slots = home.shape[0]
     return run_kernel(
-        partial(return_kernel, gain),
-        [shape_of(rows, width, FULL), shape_of(8, width, FULL)],
-        [x, vec, part, home, targets, up],
-        5,
-        scratch=[pltpu.VMEM((rows, slots), LOW)],
+        partial(return_kernel, gain, experts),
+        [shape_of(rows, width, FULL), shape_of(8, width, FULL), shape_of(width, 128, FULL)],
+        [x, vec, home, gate, routes, targets, up, mn, router],
+        7,
+        far=after,
+        scratch=[pltpu.VMEM((2, rows, slots), LOW)],
     )
 
 
@@ -932,41 +993,59 @@
     )[0]
 
 
-def expert_products_kernel(lines, fold, x_ref, dh_ref, act_ref, dy_ref, out_ref):
-    width = dy_ref.shape[1]
-    tile = x_ref.shape[1]
-    for at in range(fold):
-        part = turned_mul(x_ref[...], dh_ref[:, span(at, width)]).astype(LOW)
-        for spot in range(tile // lines):
-            start = 2 * spot * lines
-            out_ref[start : start + lines, span(at, width)] = part[spot * lines : (spot + 1) * lines, :]
-    for at in range(fold):
-        part = turned_mul(act_ref[:, span(at, tile)], dy_ref[...]).astype(LOW)
-        for spot in range(tile // lines):
-            group = at * (tile // lines) + spot
-            start = (2 * (group // fold) + 1) * lines
-            out_ref[start : start + lines, span(group % fold, width)] = part[
-                spot * lines : (spot + 1) * lines, :
-            ]
-
-
-def expert_products(x, dh, act, dy, planes):
+def expert_products_kernel(lines, x_ref, dh_ref, in_bias_ref, out_bias_ref, out_ref):
+    width = out_bias_ref.shape[1]
+    planes = width // lines
+    tall = lines + 16
+    step = pl.program_id(0)
+    row = lax.broadcasted_iota(jnp.int32, (16, 1), 0)
+    last = jnp.where(step == 0, 1.0, 0.0) * out_bias_ref[...]
+    both = jnp.where(row == 0, in_bias_ref[...], jnp.where(row == 1, last, 0.0)).astype(LOW)
+    many = max(1, 384 // lines)
+    for at in range(planes // many):
+        part = turned_mul(x_ref[:, span(at, many * lines)], dh_ref[...]).astype(LOW)
+        for spot in range(many):
+            start = (at * many + spot) * tall
+            out_ref[start : start + lines, :] = part[spot * lines : (spot + 1) * lines, :]
+            out_ref[start + lines : start + tall, :] = both
+
+
+def expert_products(x, dh, in_bias, out_bias, planes):
     slots, width = x.shape
-    fold = dh.shape[1] // width
-    steps = 2
+    inner = dh.shape[1]
+    lines = width + 16 * planes
     return run_kernel(
-        partial(expert_products_kernel, width // planes, fold),
-        [shape_of(2 * width, fold * width, LOW)],
-        [x, dh, act, dy],
-        14,
-        grid=(steps,),
+        partial(expert_products_kernel, width // planes),
+        [shape_of(lines, inner, LOW)],
+        [x, dh, in_bias, out_bias],
+        8,
+        grid=(inner // width,),
         in_blocks=[
-            pl.BlockSpec((slots, width // steps), lambda at: (0, at)),
-            whole(dh.shape),
-            pl.BlockSpec((slots, fold * width // steps), lambda at: (0, at)),
-            whole(dy.shape),
-        ],
-        out_blocks=[pl.BlockSpec((2 * width // steps, fold * width), lambda at: (at, 0))],
+            whole(x.shape),
+            pl.BlockSpec((slots, width), lambda at: (0, at)),
+            pl.BlockSpec((1, width), lambda at: (0, at)),
+            whole(out_bias.shape),
+        ],
+        out_blocks=[pl.BlockSpec((lines, width), lambda at: (0, at))],
+    )[0]
+
+
+def spread_kernel(target_ref, up_ref, out_ref, spot_ref):
+    slots = out_ref.shape[0]
+    spot_ref[...] = one_hot_rows(target_ref[0:1, :], slots) + one_hot_rows(target_ref[1:2, :], slots)
+    for at in range(out_ref.shape[1] // TILE):
+        cols = span(at, TILE)
+        out_ref[:, cols] = mul(spot_ref[...], up_ref[:, cols]).astype(LOW)
+
+
+def spread_up(targets, up, slots):
+    rows, width = up.shape
+    return run_kernel(
+        spread_kernel,
+        [shape_of(slots, width, LOW)],
+        [targets, up],
+        4,
+        scratch=[pltpu.VMEM((slots, rows), LOW)],
     )[0]
 
 
@@ -1163,7 +1242,7 @@
     block = fit(length, 16)
     rows = images * block
     lowest = (images + 1) // 2
-    capacity = fit(5 * (images + lowest) * length // (4 * experts) + 2, 16)
+    capacity = fit(5 * (images + lowest) * length // (4 * experts) + 4, 16)
     slots = experts * capacity
 
     def padded(array, fill=0):
@@ -1193,33 +1272,25 @@
     small_cols = small_rows.shape[1]
     small_rows = jnp.pad(small_rows, ((0, 0), (0, 256 - small_cols)))
     first_half = core_half(jnp.concatenate([dense_qkv, dense_proj, small_rows], axis=1))
-    moe_rows = jnp.concatenate([moe_qkv, moe_proj], axis=1)
+    moe_half = core_half(jnp.concatenate([moe_qkv, moe_proj], axis=1))
     if (2 * shard_rows) % 16 == 0:
-        later = jnp.concatenate([feed_half(dense_fc_in, dense_fc_out), core_half(moe_rows)], axis=1)
+        later = feed_half(dense_fc_in, dense_fc_out)
         pack = lax.all_gather(later, ("fsdp", "expert"), axis=0, tiled=True)
         pack = pack.reshape(planes * layers, 2, 2 * shard_rows, later.shape[1])
     else:
         groups = width // 48
         whole_in = lax.all_gather(dense_fc_in, ("fsdp", "expert"), axis=0, tiled=True)
         whole_out = lax.all_gather(dense_fc_out, ("fsdp", "expert"), axis=0, tiled=True)
-        whole_moe = lax.all_gather(moe_rows, ("fsdp", "expert"), axis=0, tiled=True)
         folded = whole_out.reshape(groups, fold, 48, width).swapaxes(1, 2).reshape(groups, 48, inner)
-        pack = jnp.concatenate(
-            [
-                jnp.stack([whole_in.reshape(groups, 48, inner), folded], axis=1),
-                whole_moe.reshape(groups, 48, 2, 2 * width).swapaxes(1, 2),
-            ],
-            axis=3,
-        )
+        pack = jnp.stack([whole_in.reshape(groups, 48, inner), folded], axis=1)
     dense_own = layer_gather(first_half)
+    dense_own, moe_half = tie((dense_own, moe_half))
     dense_near = plane_near(dense_own)
-    expert_rows = width // planes
-    expert_own = jnp.concatenate(
-        [expert_in[0]]
-        + [expert_out[0, at * expert_rows : (at + 1) * expert_rows] for at in range(fold)],
-        axis=1,
-    )
-    dense_pieces = both_cores(dense_own, dense_near, plane_far(dense_near))
+    moe_own = layer_gather(moe_half)
+    dense_near, moe_own = tie((dense_near, moe_own))
+    dense_far = plane_far(dense_near)
+    moe_near = plane_near(moe_own)
+    dense_pieces = both_cores(dense_own, dense_near, dense_far)
 
     live_images = jnp.arange(images) < image_counts[0]
     live_rows = jnp.repeat(live_images, block).astype(FULL)[:, None]
@@ -1228,12 +1299,20 @@
     target_cols = padded(jnp.where(slot_pos >= 0, routes * capacity + slot_pos, -1), -1)
     target_rows = target_cols.T
 
-    x0 = padded(patches).astype(FULL)
+    def exchange(array):
+        return lax.all_to_all(
+            array.reshape(experts, capacity, width), "expert", split_axis=0, concat_axis=0, tiled=True
+        ).reshape(slots, width)
+
+    x0, up_spread = tie((padded(patches).astype(FULL), spread_up(target_rows, up, slots)))
+    up_slots = exchange(up_spread)
     an, qkv, mixed, x1, vec, fc_bias, router_full = attend_forward(
         place, x0, None, dense_pieces, planes, (0, 2, 4, 5, 6), length, images, experts, inner
     )
-    x1, expert_own = tie((x1, expert_own))
-    expert_near = plane_near(expert_own)
+    x1, moe_near, in_own, out_own = tie((x1, moe_near, expert_in[0], expert_out[0]))
+    moe_pieces = both_cores(moe_own, moe_near, plane_far(moe_near))
+    in_near = plane_near(in_own)
+    out_near = plane_near(out_own)
     expert_bias = jnp.concatenate([expert_in_bias[0], expert_out_bias[0]])
     other_bias = tie([trade(expert_bias, "fsdp", mask) for mask in range(1, planes)])
     expert_bias = in_order([part[None] for part in [expert_bias] + other_bias], plane).astype(FULL)
@@ -1243,94 +1322,99 @@
 
     hn, act, slope, x2 = feed_forward(x1, vec, fc_bias, pack, (1, 3, 7))
     an2, qkv2, mixed2, x3 = attend_forward(
-        place, x2, vec, [pack], planes, (8, 10, 12, 13, 14), length, images, experts, inner
-    )
-    x3, expert_near = tie((x3, expert_near))
-    expert_far = plane_far(expert_near)
-    mn, gate, pick, outgoing, grad_out = dispatch(
-        x3, vec, router_full, route_cols, target_rows, up, experts, slots, (9, 11)
-    )
-
-    def exchange(array):
-        return lax.all_to_all(
-            array.reshape(experts, capacity, width), "expert", split_axis=0, concat_axis=0, tiled=True
-        ).reshape(slots, width)
-
+        place, x2, vec, moe_pieces, planes, (8, 10, 12, 13, 14), length, images, experts, inner
+    )
+    x3, up_slots = tie((x3, up_slots))
+    in_far = plane_far(in_near)
+    out_far = plane_far(out_near)
+    w_in = jnp.concatenate([in_own] + in_near + in_far, axis=0)
+    w_out = jnp.concatenate([out_own] + out_near + out_far, axis=0)
+    mn, gate, pick, outgoing = dispatch(
+        x3, vec, router_full, route_cols, target_rows, experts, slots, (9, 11)
+    )
     arrived = exchange(outgoing)
-    dy = exchange(grad_out)
-    expert_w = jnp.concatenate([expert_own] + expert_near + expert_far, axis=0)
-    e_act, e_slope = hidden_forward(place, arrived, in_bias, expert_w, planes)
-    home = exchange(expert_out_forward(place, e_act, out_bias, expert_w, expert_rows))
-    dh, in_bias_grad, out_bias_grad, back = expert_backward(place, dy, e_slope, expert_w, expert_rows)
+    arrived, an2_far, mixed2_far, w_out = tie((arrived, far(an2), far(mixed2), w_out))
+    e_act, e_slope, dy, out_bias_grad = hidden_forward(
+        place, arrived, in_bias, w_in, up_slots, planes, experts
+    )
+    out_grad = products([[(e_act, dy)]], part=768)
+    out_grad, e_act = tie((out_grad, e_act))
+    expert_out_sum = lax.psum_scatter(out_grad, "fsdp", scatter_dimension=0, tiled=True)
+    hidden_rows = inner // planes
+    result, dots = expert_out_forward(
+        place, e_act, out_bias, w_out, up_slots, hidden_rows, experts
+    )
+    dh, in_bias_grad, back = expert_backward(
+        place, dy, e_slope, w_out, w_in, dots, hidden_rows, experts
+    )
     back = exchange(back)
-    expert_grad = expert_products(arrived, dh, e_act, dy, planes)
-    expert_grad, home = tie((expert_grad, home))
+    expert_grad = expert_products(arrived, dh, in_bias_grad, out_bias_grad, planes)
+    lefts = [far(array) for array in (hn, act, an, mixed)]
+    expert_grad, back, result, expert_out_sum, lefts = tie(
+        (expert_grad, back, result, expert_out_sum, lefts)
+    )
+    hn_far, act_far, an_far, mixed_far = lefts
     expert_sum = lax.psum_scatter(expert_grad, "fsdp", scatter_dimension=0, tiled=True)
-    bias_grads = jnp.concatenate(
-        [in_bias_grad.reshape(planes, -1), out_bias_grad.reshape(planes, -1)], axis=1
-    )
-    bias_parts = [
-        lax.dynamic_index_in_dim(bias_grads, plane ^ mask, 0) for mask in range(planes)
-    ]
-    bias_came = tie([trade(bias_parts[mask], "fsdp", mask) for mask in range(1, planes)])
-    bias_sum = sum_total(bias_parts[0], bias_came)
-
-    output, part, router_grad = combine(
-        x3, home, gate, pick, route_cols, target_cols, up, live_rows, mn, router_full
-    )
-    dx3, gate_sums = return_grad(x3, vec, part, back, target_cols, up, 9)
+    home = exchange(result)
+    dx3, gate_sums, router_grad = return_grad(
+        x3, vec, back, gate, route_cols, target_cols, up, mn, router_full, 9, experts, []
+    )
     dx2, mine2, away2, low_mine2, low_away2, moe_sums = attend_backward(
-        place, dx3, x2, vec, qkv2, [pack], planes, 8, length, images
+        place, dx3, x2, vec, qkv2, moe_pieces, planes, 8, length, images
+    )
+    dx1, mine1, away1, low_mine1, low_away1, feed_sums, fc_bias_grad = feed_backward(
+        place, dx2, x1, vec, slope, pack, 1
+    )
+    away2, low_away2, away1, low_away1, dx1 = tie(
+        (far(away2), far(low_away2), far(away1), far(low_away1), dx1)
     )
     moe_grad = products(
         [
-            [(an2, mine2), (far(an2), far(away2))],
-            [(mixed2, low_mine2), (far(mixed2), far(low_away2))],
+            [(an2, mine2), (an2_far, away2)],
+            [(mixed2, low_mine2), (mixed2_far, low_away2)],
         ]
     )
-    moe_grad, dx2 = tie((moe_grad, dx2))
     moe_parts, moe_got = sum_first(in_blocks(moe_grad))
-    dx1, mine1, away1, low_mine1, low_away1, feed_sums, fc_bias_grad = feed_backward(
-        place, dx2, x1, vec, slope, pack, 1
-    )
-    moe_got, dx1 = tie((moe_got, dx1))
-    moe_came = sum_second(moe_parts, moe_got)
     if (2 * shard_rows) % 16 == 0:
         feed_grad = feed_products(
-            hn, far(hn), mine1, far(away1), act, far(act), low_mine1, far(low_away1),
+            hn, hn_far, mine1, away1, act, act_far, low_mine1, low_away1,
             planes * layers, fold,
         )
     else:
-        in_part = products([[(hn, mine1), (far(hn), far(away1))]])
-        out_part = products([[(act, low_mine1), (far(act), far(low_away1))]], part=768)
+        in_part = products([[(hn, mine1), (hn_far, away1)]])
+        out_part = products([[(act, low_mine1), (act_far, low_away1)]], part=768)
         in_part = in_blocks(in_part)
         in_part = in_part.reshape(in_part.shape[:3] + (fold, -1)).swapaxes(2, 3)
         in_part = in_part.reshape(planes, layers, -1, in_part.shape[-1])
         feed_grad = jnp.concatenate([in_part, in_blocks(out_part)], axis=2)
         feed_grad = feed_grad.reshape(-1, feed_grad.shape[-1])
-    feed_grad, dx1 = tie((feed_grad, dx1))
+    feed_grad, dx1, home, moe_got = tie((feed_grad, dx1, home, moe_got))
     feed_parts, feed_got = sum_first(in_blocks(feed_grad))
+    moe_came = sum_second(moe_parts, moe_got)
     dx0, mine0, away0, low_mine0, low_away0, vectors = attend_backward(
         place, dx1, x0, vec, qkv, dense_pieces, planes, 0, length, images, experts,
         [feed_sums, moe_sums, gate_sums, fc_bias_grad, router_grad],
     )
-    moe_came, feed_got, mine0, expert_sum = tie((moe_came, feed_got, mine0, expert_sum))
+    feed_got, moe_came, mine0, expert_sum = tie((feed_got, moe_came, mine0, expert_sum))
     feed_came = sum_second(feed_parts, feed_got)
     moe_mine, moe_layers = layer_first(sum_total(moe_parts[0], moe_came).astype(LOW))
     dense_grad = products(
         [
-            [(an, mine0), (far(an), far(away0))],
-            [(mixed, low_mine0), (far(mixed), far(low_away0))],
+            [(an, mine0), (an_far, far(away0))],
+            [(mixed, low_mine0), (mixed_far, far(low_away0))],
         ],
         vectors,
     )
+    dense_grad, moe_layers = tie((dense_grad, moe_layers))
     dense_parts, dense_got = sum_first(in_blocks(dense_grad))
-    dense_got, feed_came, moe_layers = tie((dense_got, feed_came, moe_layers))
+    output = output_rows(x3, home, pick, target_cols, live_rows)
+    dense_got, feed_came = tie((dense_got, feed_came))
+    dense_came = sum_second(dense_parts, dense_got)
     feed_mine, feed_layers = layer_first(sum_total(feed_parts[0], feed_came).astype(LOW))
     moe_left, moe_right = core_last(sum_total(moe_mine, moe_layers))
-    dense_came = sum_second(dense_parts, dense_got)
+    dense_came, feed_layers, output = tie((dense_came, feed_layers, output))
+    dense_mine, dense_layers = layer_first(sum_total(dense_parts[0], dense_came).astype(LOW))
     feed_left, feed_right = feed_last(sum_total(feed_mine, feed_layers), fold)
-    dense_mine, dense_layers = layer_first(sum_total(dense_parts[0], dense_came).astype(LOW))
     dense_left, dense_right = core_last(sum_total(dense_mine, dense_layers))
     third = 3 * width // 2
 
@@ -1354,10 +1438,12 @@
     feed_out_sum = jnp.concatenate(
         [feed_left[fold * shard_rows :], feed_right[fold * shard_rows :]], axis=1
     )
+    expert_rows = width // planes
     expert_in_sum = expert_sum[:expert_rows].astype(FULL)[None]
-    expert_out_sum = jnp.concatenate(
-        [expert_sum[expert_rows:, at * width : (at + 1) * width] for at in range(fold)], axis=0
-    ).astype(FULL)[None]
+    expert_out_sum = expert_out_sum.astype(FULL)[None]
+    bias_rows = expert_sum[expert_rows:].astype(FULL)
+    in_bias_sum = lax.dynamic_slice(bias_rows, (0, plane * hidden_part), (1, hidden_part))
+    out_bias_sum = lax.dynamic_slice(bias_rows, (1, plane * expert_rows), (1, expert_rows))
     small_turn = small_sum[:, :15].T
     return (
         trimmed(output),
@@ -1375,9 +1461,9 @@
         moe_proj_sum,
         small_sum[:, 15 : 15 + experts],
         expert_in_sum,
-        bias_sum[:, :hidden_part],
+        in_bias_sum,
         expert_out_sum,
-        bias_sum[:, hidden_part:],
+        out_bias_sum,
     )
 
 

time: 550 us -> 519 us (0.944)
  waiting for transfers between devices: 181 us -> 151 us
  local copies, waits for them, and re-layouts: 58.2 us -> 44.4 us
  starting transfers between devices: 87.7 us -> 95.2 us
    all_gather x1, waiting for transfers between devices: 37.3 us -> 0.01 us  [per_device(): pack = lax.all_gather(later, ('fsdp', 'expert'), axis=0, tiled=True)]
    ppermute x57 -> x66, waiting for transfers between devices: 111 us -> 134 us  [trade(): lax.ppermute(value, axis_name, [(place, place ^ mask) for place in range(...]
    all_to_all x4, waiting for transfers between devices: 32.7 us -> 16.8 us  [exchange(): lax.all_to_all(array.reshape(experts, capacity, width), 'expert', split_a...]
    ppermute x57 -> x66, starting transfers between devices: 59.8 us -> 70.5 us  [trade(): lax.ppermute(value, axis_name, [(place, place ^ mask) for place in range(...]
    unnamed x107 -> x109, local copies, waits for them, and re-layouts: 30.8 us -> 24.1 us
    pallas_call x16 -> x18, Pallas kernels: 178 us -> 182 us  [run_kernel(): pl.pallas_call(kernel, out_shape=list(outs), compiler_params=pltpu.Compil...]
  transfers between devices with their start and end apart: 63 -> 73, of which waited for: 28 -> 29; matrix products, arithmetic and copies ran while one was open for 12% -> 10% of each run, Pallas kernels for 33% -> 32%
where the time goes in v1:
time: 519 us; the launch traced here: 509 us
  Pallas kernels  182 us (35%)
  waiting for transfers between devices  151 us (29%)
  starting transfers between devices  95.2 us (18%)
  local copies, waits for them, and re-layouts  44.4 us (9%)
  other arithmetic  19.9 us (4%)
  between operations  16.1 us (3%)
    pallas_call x18, Pallas kernels, run_kernel(): pl.pallas_call(kernel, out_shape=list(outs), compiler_params=pltpu.Compil...  182 us
    ppermute x66, waiting for transfers between devices, trade(): lax.ppermute(value, axis_name, [(place, place ^ mask) for place in range(...  134 us
    ppermute x66, starting transfers between devices, trade(): lax.ppermute(value, axis_name, [(place, place ^ mask) for place in range(...  70.5 us
    all_to_all x4, starting transfers between devices, exchange(): lax.all_to_all(array.reshape(experts, capacity, width), 'expert', split_a...  24.4 us
    unnamed x109, local copies, waits for them, and re-layouts  24.1 us
    all_to_all x4, waiting for transfers between devices, exchange(): lax.all_to_all(array.reshape(experts, capacity, width), 'expert', split_a...  16.8 us
  transfers between devices with their start and end apart: 73, of which 29 were waited for; matrix products, arithmetic and copies ran while one was open for 10% of the time, Pallas kernels for 32%

profile of v1, /device:TPU:9, one launch (start us, length us, event | category | flops | bytes accessed | tf_op | source)
XLA Modules:
  0.0 509.2 jit_solution(2710666796422893933)
XLA Ops:
  14.9 2.5 collective-permute-start.1
  18.3 1.9 collective-permute-done.3
  20.3 4.4 collective-permute-done.1
  24.7 10.2 %collective-permute-done.2 = bf16[48,1664]{1,0:T(8,128)(2,1)S(1)} collective-permute-done((bf16[48,1664]{1,0:T(8,128)(2,1)S(1)}, bf16[48,1664]{1,0:T(8,128)(2,1)S(1)}, u32[]{:S(2)}, u32[]{:S(2)}) %collective-permute-start.2) | collective-permute-done | bytes 159776 | tf_op jit(solution)/shard_map/ppermute | solution.py:1057
  36.3 4.5 collective-permute-start.8
  43.9 4.8 collective-permute-done.9
  48.8 5.7 %collective-permute-done.8 = bf16[48,1536]{1,0:T(8,128)(2,1)S(1)} collective-permute-done((bf16[48,1536]{1,0:T(8,128)(2,1)S(1)}, bf16[48,1536]{1,0:T(8,128)(2,1)S(1)}, u32[]{:S(2)}, u32[]{:S(2)}) %collective-permute-start.8) | collective-permute-done | bytes 147488 | tf_op jit(solution)/shard_map/ppermute | solution.py:1057
  54.7 4.4 collective-permute-done.5
  64.0 5.1 %collective-permute-done.10 = bf16[96,1664]{1,0:T(8,128)(2,1)S(1)} collective-permute-done((bf16[96,1664]{1,0:T(8,128)(2,1)S(1)}, bf16[96,1664]{1,0:T(8,128)(2,1)S(1)}, u32[]{:S(2)}, u32[]{:S(2)}) %collective-permute-start.10) | collective-permute-done | bytes 319520 | tf_op jit(solution)/shard_map/ppermute | solution.py:1057
  70.6 8.4 %collective-permute-start.12 = (bf16[768,1664]{1,0:T(8,128)(2,1)}, bf16[768,1664]{1,0:T(8,128)(2,1)}, u32[]{:S(2)}, u32[]{:S(2)}) collective-permute-start(bf16[768,1664]{1,0:T(8,128)(2,1)} %constant_dynamic-update-slice_fusion.2.refs_2_.refs_5_), channel_id=1, source_target_pairs={{0,1},{1,0},{2,3},{3,2},{4,5},{5,4},{6,7},{7,6},{8,9},{9,8},{10,11... | collective-permute-start | bytes 7667720 | tf_op jit(solution)/shard_map/ppermute | solution.py:1057
  84.4 3.1 shard_map.340
  88.3 1.9 collective-permute-start.14
  91.1 10.6 %shard_map.341 = (bf16[416,768]{1,0:T(8,128)(2,1)}, bf16[416,2304]{1,0:T(8,128)(2,1)}, bf16[416,768]{1,0:T(8,128)(2,1)}, f32[416,768]{1,0:T(8,128)}, f32[32,768]...) custom-call(s32[2]{0:T(128)} %pad_add_fusion.refs_0_.place_ref, f32[416,768]{1,0:T(8,128)} %bitcast.157, ...), custom_call_target="tpu_custom_call" | custom-call | flops 4400000000 | bytes 11169792 | tf_op jit(solution)/shard_map/pallas_call | solution.py:54
  101.8 5.7 %collective-permute-done.13 = bf16[192,1536]{1,0:T(8,128)(2,1)S(1)} collective-permute-done((bf16[192,1536]{1,0:T(8,128)(2,1)S(1)}, bf16[192,1536]{1,0:T(8,128)(2,1)S(1)}, u32[]{:S(2)}, u32[]{:S(2)}) %collective-permute-start.13) | collective-permute-done | bytes 589856 | tf_op jit(solution)/shard_map/ppermute | solution.py:1057
  110.9 4.9 collective-permute-done.16
  119.9 5.1 %all-to-all-start = ((bf16[8,96,768]{2,1,0:T(8,128)(2,1)}), bf16[8,96,768]{2,1,0:T(8,128)(2,1)}, u32[]{:S(2)}, u32[]{:S(2)}) async-start(bf16[8,96,768]{2,1,0:T(8,128)(2,1)} %bitcast.14), calls=%async_computation | async-start | bytes 2359296 | tf_op jit(solution)/shard_map/all_to_all | solution.py:1303
  134.0 2.4 constant_dynamic-update-slice_fusion.21
  136.4 10.9 %shard_map.342 = (bf16[416,768]{1,0:T(8,128)(2,1)}, bf16[416,3072]{1,0:T(8,128)(2,1)}, bf16[416,3072]{1,0:T(8,128)(2,1)}, f32[416,768]{1,0:T(8,128)}) custom-call(f32[416,768]{1,0:T(8,128)} %get-tuple-element.137.x_ref, f32[32,768]{1,0:T(8,128)} %get-tuple-element.138.vec_ref.refs_2_, f32[1,3072]{1,0:T(1,128)} %get-tuple-element.139.bias_ref, ...), custom_call_target="tpu_custom_call" | custom-call | flops 4400000000 | bytes 27291648 | tf_op jit(solution)/shard_map/pallas_call | solution.py:54
  147.3 10.4 %shard_map.343 = (bf16[416,768]{1,0:T(8,128)(2,1)}, bf16[416,2304]{1,0:T(8,128)(2,1)}, bf16[416,768]{1,0:T(8,128)(2,1)}, f32[416,768]{1,0:T(8,128)}) custom-call(s32[2]{0:T(128)} %pad_add_fusion.refs_0_.place_ref, f32[416,768]{1,0:T(8,128)} %get-tuple-element.141.refs_1_.x_ref, f32[32,768]{1,0:T(8,128)} %get-tuple-element.138.vec_ref.refs_2_, ...), custom_call_target="tpu_custom_call" | custom-call | flops 4400000000 | bytes 10567680 | tf_op jit(solution)/shard_map/pallas_call | solution.py:54
  157.8 4.7 shard_map.344
  162.5 7.5 %all-to-all-start.1 = ((bf16[8,96,768]{2,1,0:T(8,128)(2,1)}), bf16[8,96,768]{2,1,0:T(8,128)(2,1)}, u32[]{:S(2)}, u32[]{:S(2)}) async-start(bf16[8,96,768]{2,1,0:T(8,128)(2,1)} %bitcast.163), calls=%async_computation.1 | async-start | bytes 2359296 | tf_op jit(solution)/shard_map/all_to_all | solution.py:1303
  173.3 9.2 %collective-permute-done.22 = bf16[768,768]{1,0:T(8,128)(2,1)} collective-permute-done((bf16[768,768]{1,0:T(8,128)(2,1)}, bf16[768,768]{1,0:T(8,128)(2,1)}, u32[]{:S(2)}, u32[]{:S(2)}) %collective-permute-start.22) | collective-permute-done | bytes 1179680 | tf_op jit(solution)/shard_map/ppermute | solution.py:1057
  188.9 18.7 %collective-permute-done.23 = bf16[384,768]{1,0:T(8,128)(2,1)S(1)} collective-permute-done((bf16[384,768]{1,0:T(8,128)(2,1)S(1)}, bf16[384,768]{1,0:T(8,128)(2,1)S(1)}, u32[]{:S(2)}, u32[]{:S(2)}) %collective-permute-start.23) | collective-permute-done | bytes 589856 | tf_op jit(solution)/shard_map/ppermute | solution.py:1057
  207.8 2.9 collective-permute-start.19
  213.5 12.5 %shard_map.345 = (bf16[768,3072]{1,0:T(8,128)(2,1)}, bf16[768,3072]{1,0:T(8,128)(2,1)}, bf16[768,768]{1,0:T(8,128)(2,1)}, f32[1,768]{1,0:T(1,128)}) custom-call(s32[2]{0:T(128)} %pad_add_fusion.refs_0_.place_ref, bf16[768,768]{1,0:T(8,128)(2,1)} %bitcast.18.x_ref, f32[1,3072]{1,0:T(1,128)} %bitcast.184, ...), custom_call_target="tpu_custom_call" | custom-call | flops 4400000000 | bytes 17710080 | tf_op jit(solution)/shard_map/pallas_call | solution.py:54
  225.9 7.9 %shard_map.346 = bf16[3072,768]{1,0:T(8,128)(2,1)} custom-call(bf16[768,3072]{1,0:T(8,128)(2,1)} %get-tuple-element.162.refs_0_.act_ref, bf16[768,768]{1,0:T(8,128)(2,1)} %get-tuple-element.158.refs_1_.dy_ref), custom_call_target="tpu_custom_call" | custom-call | flops 2800000000 | bytes 10616832 | tf_op jit(solution)/shard_map/pallas_call | solution.py:54
  234.9 10.4 %shard_map.347 = (bf16[768,768]{1,0:T(8,128)(2,1)}, bf16[128,128]{1,0:T(8,128)(2,1)}) custom-call(s32[2]{0:T(128)} %pad_add_fusion.refs_0_.place_ref, bf16[768,3072]{1,0:T(8,128)(2,1)} %get-tuple-element.162.refs_0_.act_ref, f32[1,768]{1,0:T(1,128)} %reshape.185.bias_ref, bf16[3072,768]{1,0:T(8,128)(2,1)} %copy-done.9, bf16[768,768]{1,0:T(8,128)(2,1)} %bitcast.15.up_ref), custom_call_target="tpu_custom_call" | custom-call | flops 3600000000 | bytes 11832320 | tf_op jit(solution)/shard_map/pallas_call | solution.py:54
  245.2 15.7 %shard_map.348 = (bf16[768,3072]{1,0:T(8,128)(2,1)}, f32[1,3072]{1,0:T(1,128)}, bf16[768,768]{1,0:T(8,128)(2,1)}) custom-call(s32[2]{0:T(128)} %pad_add_fusion.refs_0_.place_ref, bf16[768,768]{1,0:T(8,128)(2,1)} %get-tuple-element.158.refs_1_.dy_ref, bf16[768,3072]{1,0:T(8,128)(2,1)} %get-tuple-element.159.slope_ref, bf16[3072,768]{1,0:T(8,128)(2,1)} %copy-done.9, ...), custom_call_target="tpu_custom_call" | custom-call | flops 6000000000 | bytes 21278720 | tf_op jit(solution)/shard_map/pallas_call | solution.py:54
  261.0 5.0 all-to-all-start.2
  267.0 8.4 %shard_map.349 = bf16[832,3072]{1,0:T(8,128)(2,1)} custom-call(bf16[768,768]{1,0:T(8,128)(2,1)} %bitcast.18.x_ref, bf16[768,3072]{1,0:T(8,128)(2,1)} %get-tuple-element.164.dh_ref, f32[1,3072]{1,0:T(1,128)} %get-tuple-element.165.in_bias_ref, f32[1,768]{1,0:T(1,128)} %get-tuple-element.166.out_bias_ref), custom_call_target="tpu_custom_call" | custom-call | flops 3200000000 | bytes 11025408 | tf_op jit(solution)/shard_map/pallas_call | solution.py:54
  275.4 16.5 %all-to-all-done.2 = bf16[8,96,768]{2,1,0:T(8,128)(2,1)S(1)} async-done(((bf16[8,96,768]{2,1,0:T(8,128)(2,1)}), bf16[8,96,768]{2,1,0:T(8,128)(2,1)S(1)}, u32[]{:S(2)}, u32[]{:S(2)}) %all-to-all-start.2) | async-done | bytes 1179680 | tf_op jit(solution)/shard_map/all_to_all | solution.py:1303
  292.9 7.0 %shard_map.350 = (f32[416,768]{1,0:T(8,128)}, f32[8,768]{1,0:T(8,128)}, f32[768,128]{1,0:T(8,128)}) custom-call(f32[416,768]{1,0:T(8,128)} %get-tuple-element.146.x_ref, f32[32,768]{1,0:T(8,128)} %get-tuple-element.138.vec_ref.refs_2_, bf16[768,768]{1,0:T(8,128)(2,1)} %bitcast.164, f32[416,128]{1,0:T(8,128)} %get-tuple-element.174.gate_ref, ...), custom_call_target="tpu_custom_call" | custom-call | flops 2800000000 | bytes 5945856 | tf_op jit(solution)/shard_map/pallas_call | solution.py:54
  299.9 19.2 %shard_map.351 = (f32[416,768]{1,0:T(8,128)}, bf16[416,1152]{1,0:T(8,128)(2,1)}, bf16[416,1152]{1,0:T(8,128)(2,1)}, bf16[416,384]{1,0:T(8,128)(2,1)}, bf16[416,384]{1,0:T(8,128)(2,1)}, /*index=5*/f32[8,768]{1,0:T(8,128)}) custom-call(s32[2]{0:T(128)} %pad_add_fusion.refs_0_.place_ref, f32[416,768]{1,0:T(8,128)} %get-tuple-element.176.up_ref, ...), custom_call_target="tpu_custom_call" | custom-call | flops 7600000000 | bytes 13148160 | tf_op jit(solution)/shard_map/pallas_call | solution.py:54
  319.1 12.9 %shard_map.352 = (f32[416,768]{1,0:T(8,128)}, bf16[416,1536]{1,0:T(8,128)(2,1)}, bf16[416,1536]{1,0:T(8,128)(2,1)}, bf16[416,384]{1,0:T(8,128)(2,1)}, bf16[416,3...) custom-call(s32[2]{0:T(128)} %pad_add_fusion.refs_0_.place_ref, f32[416,768]{1,0:T(8,128)} %get-tuple-element.178.up_ref, ...), custom_call_target="tpu_custom_call" | custom-call | flops 5200000000 | bytes 28594176 | tf_op jit(solution)/shard_map/pallas_call | solution.py:54
  332.4 6.7 %all-to-all-start.3 = ((bf16[8,96,768]{2,1,0:T(8,128)(2,1)}), bf16[8,96,768]{2,1,0:T(8,128)(2,1)}, u32[]{:S(2)}, u32[]{:S(2)}) async-start(bf16[8,96,768]{2,1,0:T(8,128)(2,1)} %bitcast.21), calls=%async_computation.4 | async-start | bytes 2359296 | tf_op jit(solution)/shard_map/all_to_all | solution.py:1303
  342.9 7.3 %shard_map.354 = bf16[768,1536]{1,0:T(8,128)(2,1)} custom-call(bf16[416,768]{1,0:T(8,128)(2,1)} %get-tuple-element.149.refs_0_, bf16[416,1152]{1,0:T(8,128)(2,1)} %get-tuple-element.192.refs_1_, bf16[416,768]{1,0:T(8,128)(2,1)} %copy-done.33, bf16[416,1152]{1,0:T(8,128)(2,1)} %collective-permute-done.36.refs_3_, ...), custom_call_target="tpu_custom_call" | custom-call | flops 2800000000 | bytes 7471104 | tf_op jit(solution)/shard_map/pallas_call | solution.py:54
  352.8 11.8 %shard_map.353 = bf16[6144,384]{1,0:T(8,128)(2,1)} custom-call(bf16[416,768]{1,0:T(8,128)(2,1)} %get-tuple-element.140.hn_ref, bf16[416,768]{1,0:T(8,128)(2,1)} %collective-permute-done.32.hn_far_ref, bf16[416,1536]{1,0:T(8,128)(2,1)} %get-tuple-element.180.du_ref, bf16[416,1536]{1,0:T(8,128)(2,1)} %copy-done.26, ...), custom_call_target="tpu_custom_call" | custom-call | flops 4400000000 | bytes 14303232 | tf_op jit(solution)/shard_map/pallas_call | solution.py:54
  370.2 18.7 %shard_map.355 = (f32[416,768]{1,0:T(8,128)}, bf16[416,1152]{1,0:T(8,128)(2,1)}, bf16[416,1152]{1,0:T(8,128)(2,1)}, bf16[416,384]{1,0:T(8,128)(2,1)}, bf16[416,384]{1,0:T(8,128)(2,1)}, /*index=5*/f32[768,128]{1,0:T(8,128)}) custom-call(s32[2]{0:T(128)} %pad_add_fusion.refs_0_.place_ref, f32[416,768]{1,0:T(8,128)} %get-tuple-element.201.up_ref, ...), custom_call_target="tpu_custom_call" | custom-call | flops 7600000000 | bytes 14389248 | tf_op jit(solution)/shard_map/pallas_call | solution.py:54
  393.8 3.9 shard_map.357
  400.1 3.3 collective-permute-start.48
  409.6 7.1 %shard_map.356 = bf16[768,1664]{1,0:T(8,128)(2,1)} custom-call(bf16[416,768]{1,0:T(8,128)(2,1)} %get-tuple-element.134.refs_0_, bf16[416,1152]{1,0:T(8,128)(2,1)} %get-tuple-element.210.refs_1_, bf16[416,768]{1,0:T(8,128)(2,1)} %copy-done.30, bf16[416,1152]{1,0:T(8,128)(2,1)} %collective-permute-done.46.refs_3_, ...), custom_call_target="tpu_custom_call" | custom-call | flops 2800000000 | bytes 8060928 | tf_op jit(solution)/shard_map/pallas_call | solution.py:54
  424.8 17.7 %collective-permute-done.51 = bf16[2,48,1664]{2,1,0:T(8,128)(2,1)S(1)} collective-permute-done((bf16[2,48,1664]{2,1,0:T(8,128)(2,1)S(1)}, bf16[2,48,1664]{2,1,0:T(8,128)(2,1)S(1)}, u32[]{:S(2)}, u32[]{:S(2)}) %collective-permute-start.51) | collective-permute-done | bytes 319520 | tf_op jit(solution)/shard_map/ppermute | solution.py:1057
  446.3 2.1 collective-permute-start.57
  450.4 7.2 %collective-permute-done.57 = bf16[384,384]{1,0:T(8,128)(2,1)S(1)} collective-permute-done((bf16[384,384]{1,0:T(8,128)(2,1)S(1)}, bf16[384,384]{1,0:T(8,128)(2,1)S(1)}, u32[]{:S(2)}, u32[]{:S(2)}) %collective-permute-start.57) | collective-permute-done | bytes 294944 | tf_op jit(solution)/shard_map/ppermute | solution.py:1057
  458.4 15.2 %collective-permute-done.59 = bf16[384,384]{1,0:T(8,128)(2,1)S(1)} collective-permute-done((bf16[384,384]{1,0:T(8,128)(2,1)S(1)}, bf16[384,384]{1,0:T(8,128)(2,1)S(1)}, u32[]{:S(2)}, u32[]{:S(2)}) %collective-permute-start.59) | collective-permute-done | bytes 294944 | tf_op jit(solution)/shard_map/ppermute | solution.py:1057
  474.0 3.0 collective-permute-start.64
  483.2 3.3 collective-permute-done.61
  486.5 7.8 %collective-permute-done.62 = bf16[48,1664]{1,0:T(8,128)(2,1)S(1)} collective-permute-done((bf16[48,1664]{1,0:T(8,128)(2,1)S(1)}, bf16[48,1664]{1,0:T(8,128)(2,1)S(1)}, u32[]{:S(2)}, u32[]{:S(2)}) %collective-permute-start.62) | collective-permute-done | bytes 159776 | tf_op jit(solution)/shard_map/ppermute | solution.py:1057
  (345 shorter events, 112.2 us)
Async XLA Ops:
  7.3 129.1 %all-gather.2.cloned.1.call-start = ((), (), s32[]{:S(2)}) async-start(), calls=%async_computation.6 | async-start | bytes 9732096 | tf_op jit(solution)/shard_map/all_gather | solution.py:1278
  17.3 17.5 %collective-permute-start.2 = (bf16[48,1664]{1,0:T(8,128)(2,1)S(1)}, bf16[48,1664]{1,0:T(8,128)(2,1)S(1)}, u32[]{:S(2)}, u32[]{:S(2)}) collective-permute-start(bf16[48,1664]{1,0:T(8,128)(2,1)S(1)} %maximum_select_fusion.7), channel_id=1, source_target_pairs={{0,4},{1,5},{2,6},{3,7},{4,0},{5,1},{6,2},{7,3},{8,12},{9,13},{10,... | collective-permute-start | bytes 479240 | tf_op jit(solution)/shard_map/ppermute | solution.py:1057
  35.1 13.7 %collective-permute-start.7 = (bf16[48,1536]{1,0:T(8,128)(2,1)S(1)}, bf16[48,1536]{1,0:T(8,128)(2,1)S(1)}, u32[]{:S(2)}, u32[]{:S(2)}) collective-permute-start(bf16[48,1536]{1,0:T(8,128)(2,1)S(1)} %maximum_select_fusion.8), channel_id=1, source_target_pairs={{0,6},{1,7},{2,4},{3,5},{4,2},{5,3},{6,0},{7,1},{8,14},{9,15},{10,... | collective-permute-start | bytes 442376 | tf_op jit(solution)/shard_map/ppermute | solution.py:1057
  36.3 18.2 %collective-permute-start.8 = (bf16[48,1536]{1,0:T(8,128)(2,1)S(1)}, bf16[48,1536]{1,0:T(8,128)(2,1)S(1)}, u32[]{:S(2)}, u32[]{:S(2)}) collective-permute-start(bf16[48,1536]{1,0:T(8,128)(2,1)S(1)} %maximum_select_fusion.8), channel_id=1, source_target_pairs={{0,4},{1,5},{2,6},{3,7},{4,0},{5,1},{6,2},{7,3},{8,12},{9,13},{10,... | collective-permute-start | bytes 442376 | tf_op jit(solution)/shard_map/ppermute | solution.py:1057
  40.8 18.3 %collective-permute-start.5 = (bf16[192,1664]{1,0:T(8,128)(2,1)S(1)}, bf16[192,1664]{1,0:T(8,128)(2,1)S(1)}, u32[]{:S(2)}, u32[]{:S(2)}) collective-permute-start(bf16[192,1664]{1,0:T(8,128)(2,1)S(1)} %maximum_select_fusion), channel_id=1, source_target_pairs={{0,8},{8,0},{16,24},{24,16},{1,9},{9,1},{17,25},{25,17},{2,10},{10... | collective-permute-start | bytes 1916936 | tf_op jit(solution)/shard_map/ppermute | solution.py:1057
  41.8 17.4 %collective-permute-start.6 = (bf16[192,1664]{1,0:T(8,128)(2,1)S(1)}, bf16[192,1664]{1,0:T(8,128)(2,1)S(1)}, u32[]{:S(2)}, u32[]{:S(2)}) collective-permute-start(bf16[192,1664]{1,0:T(8,128)(2,1)S(1)} %maximum_select_fusion), channel_id=1, source_target_pairs={{0,16},{8,24},{16,0},{24,8},{1,17},{9,25},{17,1},{25,9},{2,18},{10... | collective-permute-start | bytes 1916936 | tf_op jit(solution)/shard_map/ppermute | solution.py:1057
  59.2 10.0 %collective-permute-start.10 = (bf16[96,1664]{1,0:T(8,128)(2,1)S(1)}, bf16[96,1664]{1,0:T(8,128)(2,1)S(1)}, u32[]{:S(2)}, u32[]{:S(2)}) collective-permute-start(bf16[96,1664]{1,0:T(8,128)(2,1)S(1)} %slice.251), channel_id=1, source_target_pairs={{0,8},{8,0},{16,24},{24,16},{1,9},{9,1},{17,25},{25,17},{2,10},{10... | collective-permute-start | bytes 958472 | tf_op jit(solution)/shard_map/ppermute | solution.py:1057
  70.6 20.5 %collective-permute-start.12 = (bf16[768,1664]{1,0:T(8,128)(2,1)}, bf16[768,1664]{1,0:T(8,128)(2,1)}, u32[]{:S(2)}, u32[]{:S(2)}) collective-permute-start(bf16[768,1664]{1,0:T(8,128)(2,1)} %constant_dynamic-update-slice_fusion.2.refs_2_.refs_5_), channel_id=1, source_target_pairs={{0,1},{1,0},{2,3},{3,2},{4,5},{5,4},{6,7},{7,6},{8,9},{9,8},{10,11... | collective-permute-start | bytes 7667720 | tf_op jit(solution)/shard_map/ppermute | solution.py:1057
  88.1 19.4 %collective-permute-start.13 = (bf16[192,1536]{1,0:T(8,128)(2,1)S(1)}, bf16[192,1536]{1,0:T(8,128)(2,1)S(1)}, u32[]{:S(2)}, u32[]{:S(2)}) collective-permute-start(bf16[192,1536]{1,0:T(8,128)(2,1)S(1)} %maximum_select_fusion.1), channel_id=1, source_target_pairs={{0,8},{8,0},{16,24},{24,16},{1,9},{9,1},{17,25},{25,17},{2,10},{10... | collective-permute-start | bytes 1769480 | tf_op jit(solution)/shard_map/ppermute | solution.py:1057
  88.3 19.2 %collective-permute-start.14 = (bf16[192,1536]{1,0:T(8,128)(2,1)S(1)}, bf16[192,1536]{1,0:T(8,128)(2,1)S(1)}, u32[]{:S(2)}, u32[]{:S(2)}) collective-permute-start(bf16[192,1536]{1,0:T(8,128)(2,1)S(1)} %maximum_select_fusion.1), channel_id=1, source_target_pairs={{0,16},{8,24},{16,0},{24,8},{1,17},{9,25},{17,1},{25,9},{2,18},{10... | collective-permute-start | bytes 1769480 | tf_op jit(solution)/shard_map/ppermute | solution.py:1057
  118.3 29.0 %collective-permute-start.18 = (bf16[768,1536]{1,0:T(8,128)(2,1)}, bf16[768,1536]{1,0:T(8,128)(2,1)}, u32[]{:S(2)}, u32[]{:S(2)}) collective-permute-start(bf16[768,1536]{1,0:T(8,128)(2,1)} %constant_dynamic-update-slice_fusion.7.refs_3_.refs_0_), channel_id=1, source_target_pairs={{0,1},{1,0},{2,3},{3,2},{4,5},{5,4},{6,7},{7,6},{8,9},{9,8},{10,11... | collective-permute-start | bytes 7077896 | tf_op jit(solution)/shard_map/ppermute | solution.py:1057
  119.9 37.9 %all-to-all-start = ((bf16[8,96,768]{2,1,0:T(8,128)(2,1)}), bf16[8,96,768]{2,1,0:T(8,128)(2,1)}, u32[]{:S(2)}, u32[]{:S(2)}) async-start(bf16[8,96,768]{2,1,0:T(8,128)(2,1)} %bitcast.14), calls=%async_computation | async-start | bytes 2359296 | tf_op jit(solution)/shard_map/all_to_all | solution.py:1303
  131.1 41.0 %collective-permute-start.28 = (bf16[192,3072]{1,0:T(8,128)(2,1)}, bf16[192,3072]{1,0:T(8,128)(2,1)S(1)}, u32[]{:S(2)}, u32[]{:S(2)}) collective-permute-start(bf16[192,3072]{1,0:T(8,128)(2,1)} %bitcast.11), channel_id=1, source_target_pairs={{0,8},{8,0},{16,24},{24,16},{1,9},{9,1},{17,25},{25,17},{2,10},{10... | collective-permute-start | bytes 3538952 | tf_op jit(solution)/shard_map/ppermute | solution.py:1057
  131.4 40.2 %collective-permute-start.29 = (bf16[192,3072]{1,0:T(8,128)(2,1)}, bf16[192,3072]{1,0:T(8,128)(2,1)S(1)}, u32[]{:S(2)}, u32[]{:S(2)}) collective-permute-start(bf16[192,3072]{1,0:T(8,128)(2,1)} %bitcast.11), channel_id=1, source_target_pairs={{0,16},{8,24},{16,0},{24,8},{1,17},{9,25},{17,1},{25,9},{2,18},{10... | collective-permute-start | bytes 3538952 | tf_op jit(solution)/shard_map/ppermute | solution.py:1057
  132.6 52.3 %collective-permute-start.21 = (bf16[768,768]{1,0:T(8,128)(2,1)}, bf16[768,768]{1,0:T(8,128)(2,1)S(1)}, u32[]{:S(2)}, u32[]{:S(2)}) collective-permute-start(bf16[768,768]{1,0:T(8,128)(2,1)} %bitcast.160), channel_id=1, source_target_pairs={{0,8},{8,0},{16,24},{24,16},{1,9},{9,1},{17,25},{25,17},{2,10},{10... | collective-permute-start | bytes 3538952 | tf_op jit(solution)/shard_map/ppermute | solution.py:1057
  132.9 49.7 %collective-permute-start.22 = (bf16[768,768]{1,0:T(8,128)(2,1)}, bf16[768,768]{1,0:T(8,128)(2,1)}, u32[]{:S(2)}, u32[]{:S(2)}) collective-permute-start(bf16[768,768]{1,0:T(8,128)(2,1)} %bitcast.161), channel_id=1, source_target_pairs={{0,16},{8,24},{16,0},{24,8},{1,17},{9,25},{17,1},{25,9},{2,18},{10... | collective-permute-start | bytes 3538952 | tf_op jit(solution)/shard_map/ppermute | solution.py:1057
  162.5 51.0 %all-to-all-start.1 = ((bf16[8,96,768]{2,1,0:T(8,128)(2,1)}), bf16[8,96,768]{2,1,0:T(8,128)(2,1)}, u32[]{:S(2)}, u32[]{:S(2)}) async-start(bf16[8,96,768]{2,1,0:T(8,128)(2,1)} %bitcast.163), calls=%async_computation.1 | async-start | bytes 2359296 | tf_op jit(solution)/shard_map/all_to_all | solution.py:1303
  170.0 121.8 %reduce-scatter.3.cloned.1.call-start = ((), (), s32[]{:S(2)}) async-start(), calls=%async_computation.7 | async-start | bytes 5898240 | tf_op jit(solution)/shard_map/reduce_scatter | solution.py:1342
  171.7 39.1 %collective-permute-start.30 = (bf16[96,3072]{1,0:T(8,128)(2,1)S(1)}, bf16[96,3072]{1,0:T(8,128)(2,1)S(1)}, u32[]{:S(2)}, u32[]{:S(2)}) collective-permute-start(bf16[96,3072]{1,0:T(8,128)(2,1)S(1)} %slice.339), channel_id=1, source_target_pairs={{0,8},{8,0},{16,24},{24,16},{1,9},{9,1},{17,25},{25,17},{2,10},{10... | collective-permute-start | bytes 1769480 | tf_op jit(solution)/shard_map/ppermute | solution.py:1057
  172.2 39.6 %collective-permute-start.31 = (bf16[96,3072]{1,0:T(8,128)(2,1)S(1)}, bf16[96,3072]{1,0:T(8,128)(2,1)S(1)}, u32[]{:S(2)}, u32[]{:S(2)}) collective-permute-start(bf16[96,3072]{1,0:T(8,128)(2,1)S(1)} %slice.340), channel_id=1, source_target_pairs={{0,16},{8,24},{16,0},{24,8},{1,17},{9,25},{17,1},{25,9},{2,18},{10... | collective-permute-start | bytes 1769480 | tf_op jit(solution)/shard_map/ppermute | solution.py:1057
  183.7 24.0 %collective-permute-start.23 = (bf16[384,768]{1,0:T(8,128)(2,1)S(1)}, bf16[384,768]{1,0:T(8,128)(2,1)S(1)}, u32[]{:S(2)}, u32[]{:S(2)}) collective-permute-start(bf16[384,768]{1,0:T(8,128)(2,1)S(1)} %slice.336), channel_id=1, source_target_pairs={{0,8},{8,0},{16,24},{24,16},{1,9},{9,1},{17,25},{25,17},{2,10},{10... | collective-permute-start | bytes 1769480 | tf_op jit(solution)/shard_map/ppermute | solution.py:1057
  184.9 22.9 %collective-permute-start.24 = (bf16[384,768]{1,0:T(8,128)(2,1)S(1)}, bf16[384,768]{1,0:T(8,128)(2,1)S(1)}, u32[]{:S(2)}, u32[]{:S(2)}) collective-permute-start(bf16[384,768]{1,0:T(8,128)(2,1)S(1)} %slice.337), channel_id=1, source_target_pairs={{0,16},{8,24},{16,0},{24,8},{1,17},{9,25},{17,1},{25,9},{2,18},{10... | collective-permute-start | bytes 1769480 | tf_op jit(solution)/shard_map/ppermute | solution.py:1057
  234.5 40.9 %collective-permute-start.33 = (bf16[416,3072]{1,0:T(8,128)(2,1)}, bf16[416,3072]{1,0:T(8,128)(2,1)}, u32[]{:S(2)}, u32[]{:S(2)}) collective-permute-start(bf16[416,3072]{1,0:T(8,128)(2,1)} %get-tuple-element.170.act_ref), channel_id=1, source_target_pairs={{0,1},{1,0},{2,3},{3,2},{4,5},{5,4},{6,7},{7,6},{8,9},{9,8},{10,11... | collective-permute-start | bytes 7667720 | tf_op jit(solution)/shard_map/ppermute | solution.py:1057
  261.0 30.9 %all-to-all-start.2 = ((bf16[8,96,768]{2,1,0:T(8,128)(2,1)}), bf16[8,96,768]{2,1,0:T(8,128)(2,1)S(1)}, u32[]{:S(2)}, u32[]{:S(2)}) async-start(bf16[8,96,768]{2,1,0:T(8,128)(2,1)} %bitcast.165), calls=%async_computation.2 | async-start | bytes 2359296 | tf_op jit(solution)/shard_map/all_to_all | solution.py:1303
  266.0 131.7 %reduce-scatter.5.cloned.1.call-start = ((), (), s32[]{:S(2)}) async-start(), calls=%async_computation.8 | async-start | bytes 6389760 | tf_op jit(solution)/shard_map/reduce_scatter | solution.py:1357
  332.0 10.9 %collective-permute-start.38 = (bf16[416,1536]{1,0:T(8,128)(2,1)}, bf16[416,1536]{1,0:T(8,128)(2,1)S(1)}, u32[]{:S(2)}, u32[]{:S(2)}) collective-permute-start(bf16[416,1536]{1,0:T(8,128)(2,1)} %get-tuple-element.183), channel_id=1, source_target_pairs={{0,1},{1,0},{2,3},{3,2},{4,5},{5,4},{6,7},{7,6},{8,9},{9,8},{10,11... | collective-permute-start | bytes 3833864 | tf_op jit(solution)/shard_map/ppermute | solution.py:1057
  332.4 32.5 %all-to-all-start.3 = ((bf16[8,96,768]{2,1,0:T(8,128)(2,1)}), bf16[8,96,768]{2,1,0:T(8,128)(2,1)}, u32[]{:S(2)}, u32[]{:S(2)}) async-start(bf16[8,96,768]{2,1,0:T(8,128)(2,1)} %bitcast.21), calls=%async_computation.4 | async-start | bytes 2359296 | tf_op jit(solution)/shard_map/all_to_all | solution.py:1303
  351.6 13.0 %collective-permute-start.40 = (bf16[2,48,1536]{2,1,0:T(8,128)(2,1)S(1)}, bf16[2,48,1536]{2,1,0:T(8,128)(2,1)S(1)}, u32[]{:S(2)}, u32[]{:S(2)}) collective-permute-start(bf16[2,48,1536]{2,1,0:T(8,128)(2,1)S(1)} %get-tuple-element.310), channel_id=1, source_target_pairs={{0,8},{8,0},{16,24},{24,16},{1,9},{9,1},{17,25},{25,17},{2,10},{10... | collective-permute-start | bytes 884744 | tf_op jit(solution)/shard_map/ppermute | solution.py:1057
  352.7 11.9 %collective-permute-start.41 = (bf16[2,48,1536]{2,1,0:T(8,128)(2,1)S(1)}, bf16[2,48,1536]{2,1,0:T(8,128)(2,1)S(1)}, u32[]{:S(2)}, u32[]{:S(2)}) collective-permute-start(bf16[2,48,1536]{2,1,0:T(8,128)(2,1)S(1)} %get-tuple-element.311), channel_id=1, source_target_pairs={{0,16},{8,24},{16,0},{24,8},{1,17},{9,25},{17,1},{25,9},{2,18},{10... | collective-permute-start | bytes 884744 | tf_op jit(solution)/shard_map/ppermute | solution.py:1057
  365.1 32.6 %collective-permute-start.45 = (bf16[4,48,1536]{2,1,0:T(8,128)(2,1)S(1)}, bf16[4,48,1536]{2,1,0:T(8,128)(2,1)}, u32[]{:S(2)}, u32[]{:S(2)}) collective-permute-start(bf16[4,48,1536]{2,1,0:T(8,128)(2,1)S(1)} %pad_maximum_fusion.5), channel_id=1, source_target_pairs={{0,16},{8,24},{16,0},{24,8},{1,17},{9,25},{17,1},{25,9},{2,18},{10... | collective-permute-start | bytes 1769480 | tf_op jit(solution)/shard_map/ppermute | solution.py:1057
  366.3 31.4 %collective-permute-start.44 = (bf16[4,48,1536]{2,1,0:T(8,128)(2,1)S(1)}, bf16[4,48,1536]{2,1,0:T(8,128)(2,1)}, u32[]{:S(2)}, u32[]{:S(2)}) collective-permute-start(bf16[4,48,1536]{2,1,0:T(8,128)(2,1)S(1)} %pad_maximum_fusion.4), channel_id=1, source_target_pairs={{0,8},{8,0},{16,24},{24,16},{1,9},{9,1},{17,25},{25,17},{2,10},{10... | collective-permute-start | bytes 1769480 | tf_op jit(solution)/shard_map/ppermute | solution.py:1057
  368.7 29.0 %collective-permute-start.42 = (bf16[2,384,384]{2,1,0:T(8,128)(2,1)S(1)}, bf16[2,384,384]{2,1,0:T(8,128)(2,1)}, u32[]{:S(2)}, u32[]{:S(2)}) collective-permute-start(bf16[2,384,384]{2,1,0:T(8,128)(2,1)S(1)} %get-tuple-element.298), channel_id=1, source_target_pairs={{0,8},{8,0},{16,24},{24,16},{1,9},{9,1},{17,25},{25,17},{2,10},{10... | collective-permute-start | bytes 1769480 | tf_op jit(solution)/shard_map/ppermute | solution.py:1057
  369.8 27.9 %collective-permute-start.43 = (bf16[2,384,384]{2,1,0:T(8,128)(2,1)S(1)}, bf16[2,384,384]{2,1,0:T(8,128)(2,1)}, u32[]{:S(2)}, u32[]{:S(2)}) collective-permute-start(bf16[2,384,384]{2,1,0:T(8,128)(2,1)S(1)} %get-tuple-element.299), channel_id=1, source_target_pairs={{0,16},{8,24},{16,0},{24,8},{1,17},{9,25},{17,1},{25,9},{2,18},{10... | collective-permute-start | bytes 1769480 | tf_op jit(solution)/shard_map/ppermute | solution.py:1057
  388.9 20.7 %collective-permute-start.46 = (bf16[416,1152]{1,0:T(8,128)(2,1)}, bf16[416,1152]{1,0:T(8,128)(2,1)}, u32[]{:S(2)}, u32[]{:S(2)}) collective-permute-start(bf16[416,1152]{1,0:T(8,128)(2,1)} %get-tuple-element.212), channel_id=1, source_target_pairs={{0,1},{1,0},{2,3},{3,2},{4,5},{5,4},{6,7},{7,6},{8,9},{9,8},{10,11... | collective-permute-start | bytes 2875400 | tf_op jit(solution)/shard_map/ppermute | solution.py:1057
  397.7 10.8 %collective-permute-start.47 = (bf16[416,384]{1,0:T(8,128)(2,1)}, bf16[416,384]{1,0:T(8,128)(2,1)}, u32[]{:S(2)}, u32[]{:S(2)}) collective-permute-start(bf16[416,384]{1,0:T(8,128)(2,1)} %get-tuple-element.215), channel_id=1, source_target_pairs={{0,1},{1,0},{2,3},{3,2},{4,5},{5,4},{6,7},{7,6},{8,9},{9,8},{10,11... | collective-permute-start | bytes 958472 | tf_op jit(solution)/shard_map/ppermute | solution.py:1057
  400.1 17.8 %collective-permute-start.48 = (bf16[48,1536]{1,0:T(8,128)(2,1)}, bf16[48,1536]{1,0:T(8,128)(2,1)S(1)}, u32[]{:S(2)}, u32[]{:S(2)}) collective-permute-start(bf16[48,1536]{1,0:T(8,128)(2,1)} %get-tuple-element.322), channel_id=1, source_target_pairs={{0,2},{1,3},{2,0},{3,1},{4,6},{5,7},{6,4},{7,5},{8,10},{9,11},{10,... | collective-permute-start | bytes 442376 | tf_op jit(solution)/shard_map/ppermute | solution.py:1057
  403.4 14.5 %collective-permute-start.49 = (bf16[48,1536]{1,0:T(8,128)(2,1)}, bf16[48,1536]{1,0:T(8,128)(2,1)S(1)}, u32[]{:S(2)}, u32[]{:S(2)}) collective-permute-start(bf16[48,1536]{1,0:T(8,128)(2,1)} %get-tuple-element.321), channel_id=1, source_target_pairs={{0,4},{1,5},{2,6},{3,7},{4,0},{5,1},{6,2},{7,3},{8,12},{9,13},{10,... | collective-permute-start | bytes 442376 | tf_op jit(solution)/shard_map/ppermute | solution.py:1057
  403.4 14.5 %collective-permute-start.50 = (bf16[48,1536]{1,0:T(8,128)(2,1)}, bf16[48,1536]{1,0:T(8,128)(2,1)}, u32[]{:S(2)}, u32[]{:S(2)}) collective-permute-start(bf16[48,1536]{1,0:T(8,128)(2,1)} %get-tuple-element.320), channel_id=1, source_target_pairs={{0,6},{1,7},{2,4},{3,5},{4,2},{5,3},{6,0},{7,1},{8,14},{9,15},{10,... | collective-permute-start | bytes 442376 | tf_op jit(solution)/shard_map/ppermute | solution.py:1057
  408.5 34.1 %collective-permute-start.54 = (bf16[4,384,384]{2,1,0:T(8,128)(2,1)S(1)}, bf16[4,384,384]{2,1,0:T(8,128)(2,1)S(1)}, u32[]{:S(2)}, u32[]{:S(2)}) collective-permute-start(bf16[4,384,384]{2,1,0:T(8,128)(2,1)S(1)} %pad_maximum_fusion.1), channel_id=1, source_target_pairs={{0,16},{8,24},{16,0},{24,8},{1,17},{9,25},{17,1},{25,9},{2,18},{10... | collective-permute-start | bytes 3538952 | tf_op jit(solution)/shard_map/ppermute | solution.py:1057
  409.6 33.0 %collective-permute-start.53 = (bf16[4,384,384]{2,1,0:T(8,128)(2,1)S(1)}, bf16[4,384,384]{2,1,0:T(8,128)(2,1)S(1)}, u32[]{:S(2)}, u32[]{:S(2)}) collective-permute-start(bf16[4,384,384]{2,1,0:T(8,128)(2,1)S(1)} %pad_maximum_fusion), channel_id=1, source_target_pairs={{0,8},{8,0},{16,24},{24,16},{1,9},{9,1},{17,25},{25,17},{2,10},{10... | collective-permute-start | bytes 3538952 | tf_op jit(solution)/shard_map/ppermute | solution.py:1057
  421.9 20.6 %collective-permute-start.51 = (bf16[2,48,1664]{2,1,0:T(8,128)(2,1)S(1)}, bf16[2,48,1664]{2,1,0:T(8,128)(2,1)S(1)}, u32[]{:S(2)}, u32[]{:S(2)}) collective-permute-start(bf16[2,48,1664]{2,1,0:T(8,128)(2,1)S(1)} %get-tuple-element.303), channel_id=1, source_target_pairs={{0,8},{8,0},{16,24},{24,16},{1,9},{9,1},{17,25},{25,17},{2,10},{10... | collective-permute-start | bytes 958472 | tf_op jit(solution)/shard_map/ppermute | solution.py:1057
  423.6 18.9 %collective-permute-start.52 = (bf16[2,48,1664]{2,1,0:T(8,128)(2,1)S(1)}, bf16[2,48,1664]{2,1,0:T(8,128)(2,1)S(1)}, u32[]{:S(2)}, u32[]{:S(2)}) collective-permute-start(bf16[2,48,1664]{2,1,0:T(8,128)(2,1)S(1)} %get-tuple-element.305), channel_id=1, source_target_pairs={{0,16},{8,24},{16,0},{24,8},{1,17},{9,25},{17,1},{25,9},{2,18},{10... | collective-permute-start | bytes 958472 | tf_op jit(solution)/shard_map/ppermute | solution.py:1057
  442.8 30.9 %collective-permute-start.56 = (bf16[4,48,1664]{2,1,0:T(8,128)(2,1)S(1)}, bf16[4,48,1664]{2,1,0:T(8,128)(2,1)S(1)}, u32[]{:S(2)}, u32[]{:S(2)}) collective-permute-start(bf16[4,48,1664]{2,1,0:T(8,128)(2,1)S(1)} %pad_maximum_fusion.3), channel_id=1, source_target_pairs={{0,16},{8,24},{16,0},{24,8},{1,17},{9,25},{17,1},{25,9},{2,18},{10... | collective-permute-start | bytes 1916936 | tf_op jit(solution)/shard_map/ppermute | solution.py:1057
  443.4 30.3 %collective-permute-start.55 = (bf16[4,48,1664]{2,1,0:T(8,128)(2,1)S(1)}, bf16[4,48,1664]{2,1,0:T(8,128)(2,1)S(1)}, u32[]{:S(2)}, u32[]{:S(2)}) collective-permute-start(bf16[4,48,1664]{2,1,0:T(8,128)(2,1)S(1)} %pad_maximum_fusion.2), channel_id=1, source_target_pairs={{0,8},{8,0},{16,24},{24,16},{1,9},{9,1},{17,25},{25,17},{2,10},{10... | collective-permute-start | bytes 1916936 | tf_op jit(solution)/shard_map/ppermute | solution.py:1057
  446.3 11.3 %collective-permute-start.57 = (bf16[384,384]{1,0:T(8,128)(2,1)S(1)}, bf16[384,384]{1,0:T(8,128)(2,1)S(1)}, u32[]{:S(2)}, u32[]{:S(2)}) collective-permute-start(bf16[384,384]{1,0:T(8,128)(2,1)S(1)} %get-tuple-element.314), channel_id=1, source_target_pairs={{0,2},{1,3},{2,0},{3,1},{4,6},{5,7},{6,4},{7,5},{8,10},{9,11},{10,... | collective-permute-start | bytes 884744 | tf_op jit(solution)/shard_map/ppermute | solution.py:1057
  448.4 10.0 %collective-permute-start.58 = (bf16[384,384]{1,0:T(8,128)(2,1)S(1)}, bf16[384,384]{1,0:T(8,128)(2,1)S(1)}, u32[]{:S(2)}, u32[]{:S(2)}) collective-permute-start(bf16[384,384]{1,0:T(8,128)(2,1)S(1)} %get-tuple-element.313), channel_id=1, source_target_pairs={{0,4},{1,5},{2,6},{3,7},{4,0},{5,1},{6,2},{7,3},{8,12},{9,13},{10,... | collective-permute-start | bytes 884744 | tf_op jit(solution)/shard_map/ppermute | solution.py:1057
  448.4 25.3 %collective-permute-start.59 = (bf16[384,384]{1,0:T(8,128)(2,1)S(1)}, bf16[384,384]{1,0:T(8,128)(2,1)S(1)}, u32[]{:S(2)}, u32[]{:S(2)}) collective-permute-start(bf16[384,384]{1,0:T(8,128)(2,1)S(1)} %get-tuple-element.312), channel_id=1, source_target_pairs={{0,6},{1,7},{2,4},{3,5},{4,2},{5,3},{6,0},{7,1},{8,14},{9,15},{10,... | collective-permute-start | bytes 884744 | tf_op jit(solution)/shard_map/ppermute | solution.py:1057
  478.8 15.5 %collective-permute-start.62 = (bf16[48,1664]{1,0:T(8,128)(2,1)S(1)}, bf16[48,1664]{1,0:T(8,128)(2,1)S(1)}, u32[]{:S(2)}, u32[]{:S(2)}) collective-permute-start(bf16[48,1664]{1,0:T(8,128)(2,1)S(1)} %get-tuple-element.316), channel_id=1, source_target_pairs={{0,6},{1,7},{2,4},{3,5},{4,2},{5,3},{6,0},{7,1},{8,14},{9,15},{10,... | collective-permute-start | bytes 479240 | tf_op jit(solution)/shard_map/ppermute | solution.py:1057
  (59 other events, 495.7 us)
Sparse Core Ops, SparseCore 0:
  12.5 100.3 all-gather.1
  233.9 56.7 reduce-scatter.2
  293.8 60.3 reduce-scatter.4

commit v2 on v1

--- a/solution.py
+++ b/solution.py
@@ -1284,6 +1284,10 @@
         folded = whole_out.reshape(groups, fold, 48, width).swapaxes(1, 2).reshape(groups, 48, inner)
         pack = jnp.stack([whole_in.reshape(groups, 48, inner), folded], axis=1)
     dense_own = layer_gather(first_half)
+    expert_bias = jnp.concatenate([expert_in_bias[0], expert_out_bias[0]])
+    other_bias = [trade(expert_bias, "fsdp", mask) for mask in range(1, planes)]
+    dense_own, other_bias = tie((dense_own, other_bias))
+    expert_bias = in_order([part[None] for part in [expert_bias] + other_bias], plane).astype(FULL)
     dense_own, moe_half = tie((dense_own, moe_half))
     dense_near = plane_near(dense_own)
     moe_own = layer_gather(moe_half)
@@ -1313,9 +1317,6 @@
     moe_pieces = both_cores(moe_own, moe_near, plane_far(moe_near))
     in_near = plane_near(in_own)
     out_near = plane_near(out_own)
-    expert_bias = jnp.concatenate([expert_in_bias[0], expert_out_bias[0]])
-    other_bias = tie([trade(expert_bias, "fsdp", mask) for mask in range(1, planes)])
-    expert_bias = in_order([part[None] for part in [expert_bias] + other_bias], plane).astype(FULL)
     hidden_part = expert_in_bias.shape[1]
     in_bias = expert_bias[:, :hidden_part].reshape(1, -1)
     out_bias = expert_bias[:, hidden_part:].reshape(1, -1)
@@ -1333,10 +1334,10 @@
         x3, vec, router_full, route_cols, target_rows, experts, slots, (9, 11)
     )
     arrived = exchange(outgoing)
-    arrived, an2_far, mixed2_far, w_out = tie((arrived, far(an2), far(mixed2), w_out))
     e_act, e_slope, dy, out_bias_grad = hidden_forward(
         place, arrived, in_bias, w_in, up_slots, planes, experts
     )
+    e_act, w_out = tie((e_act, w_out))
     out_grad = products([[(e_act, dy)]], part=768)
     out_grad, e_act = tie((out_grad, e_act))
     expert_out_sum = lax.psum_scatter(out_grad, "fsdp", scatter_dimension=0, tiled=True)
@@ -1349,11 +1350,11 @@
     )
     back = exchange(back)
     expert_grad = expert_products(arrived, dh, in_bias_grad, out_bias_grad, planes)
-    lefts = [far(array) for array in (hn, act, an, mixed)]
+    lefts = [far(array) for array in (hn, act, an, mixed, an2, mixed2)]
     expert_grad, back, result, expert_out_sum, lefts = tie(
         (expert_grad, back, result, expert_out_sum, lefts)
     )
-    hn_far, act_far, an_far, mixed_far = lefts
+    hn_far, act_far, an_far, mixed_far, an2_far, mixed2_far = lefts
     expert_sum = lax.psum_scatter(expert_grad, "fsdp", scatter_dimension=0, tiled=True)
     home = exchange(result)
     dx3, gate_sums, router_grad = return_grad(
@@ -1388,14 +1389,14 @@
         in_part = in_part.reshape(planes, layers, -1, in_part.shape[-1])
         feed_grad = jnp.concatenate([in_part, in_blocks(out_part)], axis=2)
         feed_grad = feed_grad.reshape(-1, feed_grad.shape[-1])
-    feed_grad, dx1, home, moe_got = tie((feed_grad, dx1, home, moe_got))
+    feed_grad, dx1, moe_got = tie((feed_grad, dx1, moe_got))
     feed_parts, feed_got = sum_first(in_blocks(feed_grad))
     moe_came = sum_second(moe_parts, moe_got)
     dx0, mine0, away0, low_mine0, low_away0, vectors = attend_backward(
         place, dx1, x0, vec, qkv, dense_pieces, planes, 0, length, images, experts,
         [feed_sums, moe_sums, gate_sums, fc_bias_grad, router_grad],
     )
-    feed_got, moe_came, mine0, expert_sum = tie((feed_got, moe_came, mine0, expert_sum))
+    feed_got, mine0, expert_sum, moe_came = tie((feed_got, mine0, expert_sum, moe_came))
     feed_came = sum_second(feed_parts, feed_got)
     moe_mine, moe_layers = layer_first(sum_total(moe_parts[0], moe_came).astype(LOW))
     dense_grad = products(
@@ -1405,12 +1406,13 @@
         ],
         vectors,
     )
-    dense_grad, moe_layers = tie((dense_grad, moe_layers))
     dense_parts, dense_got = sum_first(in_blocks(dense_grad))
-    output = output_rows(x3, home, pick, target_cols, live_rows)
-    dense_got, feed_came = tie((dense_got, feed_came))
+    dense_got, home, dx0, feed_came, moe_layers, expert_sum, expert_out_sum = tie(
+        (dense_got, home, dx0, feed_came, moe_layers, expert_sum, expert_out_sum)
+    )
     dense_came = sum_second(dense_parts, dense_got)
     feed_mine, feed_layers = layer_first(sum_total(feed_parts[0], feed_came).astype(LOW))
+    output = output_rows(x3, home, pick, target_cols, live_rows)
     moe_left, moe_right = core_last(sum_total(moe_mine, moe_layers))
     dense_came, feed_layers, output = tie((dense_came, feed_layers, output))
     dense_mine, dense_layers = layer_first(sum_total(dense_parts[0], dense_came).astype(LOW))

time: 519 us -> 507 us (0.977)
  waiting for transfers between devices: 151 us -> 138 us
    ppermute x66, waiting for transfers between devices: 134 us -> 124 us  [trade(): lax.ppermute(value, axis_name, [(place, place ^ mask) for place in range(...]
    unnamed x109 -> x115, local copies, waits for them, and re-layouts: 24.1 us -> 25.3 us
  transfers between devices with their start and end apart: 73 -> 73, of which waited for: 29 -> 29; matrix products, arithmetic and copies ran while one was open for 10% -> 11% of each run, Pallas kernels for 32% -> 32%
where the time goes in v2:
time: 507 us; the launch traced here: 497 us
  Pallas kernels  182 us (36%)
  waiting for transfers between devices  138 us (27%)
  starting transfers between devices  91 us (18%)
  local copies, waits for them, and re-layouts  46 us (9%)
  other arithmetic  23.9 us (5%)
  between operations  16.1 us (3%)
    pallas_call x18, Pallas kernels, run_kernel(): pl.pallas_call(kernel, out_shape=list(outs), compiler_params=pltpu.Compil...  182 us
    ppermute x66, waiting for transfers between devices, trade(): lax.ppermute(value, axis_name, [(place, place ^ mask) for place in range(...  124 us
    ppermute x66, starting transfers between devices, trade(): lax.ppermute(value, axis_name, [(place, place ^ mask) for place in range(...  66.5 us
    unnamed x115, local copies, waits for them, and re-layouts  25.3 us
    all_to_all x4, starting transfers between devices, exchange(): lax.all_to_all(array.reshape(experts, capacity, width), 'expert', split_a...  24.2 us
    all_to_all x4, waiting for transfers between devices, exchange(): lax.all_to_all(array.reshape(experts, capacity, width), 'expert', split_a...  14.4 us
  transfers between devices with their start and end apart: 73, of which 29 were waited for; matrix products, arithmetic and copies ran while one was open for 11% of the time, Pallas kernels for 32%

profile of v2, /device:TPU:9, one launch (start us, length us, event | category | flops | bytes accessed | tf_op | source)
XLA Modules:
  0.0 497.1 jit_solution(6556924330314155658)
XLA Ops:
  18.5 2.3 collective-permute-start.1
  20.8 2.6 collective-permute-done.3
  23.4 2.5 collective-permute-start.2
  26.0 13.9 %collective-permute-done.2 = bf16[48,1664]{1,0:T(8,128)(2,1)S(1)} collective-permute-done((bf16[48,1664]{1,0:T(8,128)(2,1)S(1)}, bf16[48,1664]{1,0:T(8,128)(2,1)S(1)}, u32[]{:S(2)}, u32[]{:S(2)}) %collective-permute-start.2) | collective-permute-done | bytes 159776 | tf_op jit(solution)/shard_map/ppermute | solution.py:1057
  40.6 4.3 collective-permute-start.11
  48.3 10.5 %collective-permute-done.12 = bf16[48,1536]{1,0:T(8,128)(2,1)S(1)} collective-permute-done((bf16[48,1536]{1,0:T(8,128)(2,1)S(1)}, bf16[48,1536]{1,0:T(8,128)(2,1)S(1)}, u32[]{:S(2)}, u32[]{:S(2)}) %collective-permute-start.12) | collective-permute-done | bytes 147488 | tf_op jit(solution)/shard_map/ppermute | solution.py:1057
  60.7 7.4 %collective-permute-done.8 = bf16[192,1664]{1,0:T(8,128)(2,1)S(1)} collective-permute-done((bf16[192,1664]{1,0:T(8,128)(2,1)S(1)}, bf16[192,1664]{1,0:T(8,128)(2,1)S(1)}, u32[]{:S(2)}, u32[]{:S(2)}) %collective-permute-start.8) | collective-permute-done | bytes 639008 | tf_op jit(solution)/shard_map/ppermute | solution.py:1057
  73.1 2.4 collective-permute-done.13
  78.6 4.3 collective-permute-start.15
  88.3 3.1 shard_map.340
  95.1 10.6 %shard_map.341 = (bf16[416,768]{1,0:T(8,128)(2,1)}, bf16[416,2304]{1,0:T(8,128)(2,1)}, bf16[416,768]{1,0:T(8,128)(2,1)}, f32[416,768]{1,0:T(8,128)}, f32[32,768]...) custom-call(s32[2]{0:T(128)} %pad_add_fusion.refs_0_.place_ref, f32[416,768]{1,0:T(8,128)} %bitcast.157, ...), custom_call_target="tpu_custom_call" | custom-call | flops 4400000000 | bytes 11169792 | tf_op jit(solution)/shard_map/pallas_call | solution.py:54
  105.7 3.9 collective-permute-done.16
  113.1 4.9 collective-permute-done.19
  122.0 6.0 %all-to-all-start = ((bf16[8,96,768]{2,1,0:T(8,128)(2,1)}), bf16[8,96,768]{2,1,0:T(8,128)(2,1)}, u32[]{:S(2)}, u32[]{:S(2)}) async-start(bf16[8,96,768]{2,1,0:T(8,128)(2,1)} %bitcast.14), calls=%async_computation | async-start | bytes 2359296 | tf_op jit(solution)/shard_map/all_to_all | solution.py:1307
  132.5 2.4 constant_dynamic-update-slice_fusion.16
  134.9 10.9 %shard_map.342 = (bf16[416,768]{1,0:T(8,128)(2,1)}, bf16[416,3072]{1,0:T(8,128)(2,1)}, bf16[416,3072]{1,0:T(8,128)(2,1)}, f32[416,768]{1,0:T(8,128)}) custom-call(f32[416,768]{1,0:T(8,128)} %get-tuple-element.141.x_ref, f32[32,768]{1,0:T(8,128)} %get-tuple-element.142.vec_ref.refs_2_, f32[1,3072]{1,0:T(1,128)} %get-tuple-element.143.bias_ref, ...), custom_call_target="tpu_custom_call" | custom-call | flops 4400000000 | bytes 27291648 | tf_op jit(solution)/shard_map/pallas_call | solution.py:54
  145.8 10.4 %shard_map.343 = (bf16[416,768]{1,0:T(8,128)(2,1)}, bf16[416,2304]{1,0:T(8,128)(2,1)}, bf16[416,768]{1,0:T(8,128)(2,1)}, f32[416,768]{1,0:T(8,128)}) custom-call(s32[2]{0:T(128)} %pad_add_fusion.refs_0_.place_ref, f32[416,768]{1,0:T(8,128)} %get-tuple-element.145.refs_1_.x_ref, f32[32,768]{1,0:T(8,128)} %get-tuple-element.142.vec_ref.refs_2_, ...), custom_call_target="tpu_custom_call" | custom-call | flops 4400000000 | bytes 10567680 | tf_op jit(solution)/shard_map/pallas_call | solution.py:54
  156.3 4.7 shard_map.344
  161.0 6.2 %all-to-all-start.1 = ((bf16[8,96,768]{2,1,0:T(8,128)(2,1)}), bf16[8,96,768]{2,1,0:T(8,128)(2,1)}, u32[]{:S(2)}, u32[]{:S(2)}) async-start(bf16[8,96,768]{2,1,0:T(8,128)(2,1)} %bitcast.160), calls=%async_computation.1 | async-start | bytes 2359296 | tf_op jit(solution)/shard_map/all_to_all | solution.py:1307
  170.5 11.6 %collective-permute-done.23 = bf16[192,3072]{1,0:T(8,128)(2,1)S(1)} collective-permute-done((bf16[192,3072]{1,0:T(8,128)(2,1)}, bf16[192,3072]{1,0:T(8,128)(2,1)S(1)}, u32[]{:S(2)}, u32[]{:S(2)}) %collective-permute-start.23) | collective-permute-done | bytes 1179680 | tf_op jit(solution)/shard_map/ppermute | solution.py:1057
  185.8 2.4 constant_dynamic-update-slice_fusion.15
  189.4 5.4 %collective-permute-done.28 = bf16[384,768]{1,0:T(8,128)(2,1)S(1)} collective-permute-done((bf16[384,768]{1,0:T(8,128)(2,1)S(1)}, bf16[384,768]{1,0:T(8,128)(2,1)S(1)}, u32[]{:S(2)}, u32[]{:S(2)}) %collective-permute-start.28) | collective-permute-done | bytes 589856 | tf_op jit(solution)/shard_map/ppermute | solution.py:1057
  195.0 12.5 %collective-permute-done.24 = bf16[96,3072]{1,0:T(8,128)(2,1)S(1)} collective-permute-done((bf16[96,3072]{1,0:T(8,128)(2,1)S(1)}, bf16[96,3072]{1,0:T(8,128)(2,1)S(1)}, u32[]{:S(2)}, u32[]{:S(2)}) %collective-permute-start.24) | collective-permute-done | bytes 589856 | tf_op jit(solution)/shard_map/ppermute | solution.py:1057
  209.3 12.5 %shard_map.345 = (bf16[768,3072]{1,0:T(8,128)(2,1)}, bf16[768,3072]{1,0:T(8,128)(2,1)}, bf16[768,768]{1,0:T(8,128)(2,1)}, f32[1,768]{1,0:T(1,128)}) custom-call(s32[2]{0:T(128)} %pad_add_fusion.refs_0_.place_ref, bf16[768,768]{1,0:T(8,128)(2,1)} %bitcast.18.x_ref, f32[1,3072]{1,0:T(1,128)} %bitcast.181, ...), custom_call_target="tpu_custom_call" | custom-call | flops 4400000000 | bytes 17710080 | tf_op jit(solution)/shard_map/pallas_call | solution.py:54
  221.8 7.9 %shard_map.346 = bf16[3072,768]{1,0:T(8,128)(2,1)} custom-call(bf16[768,3072]{1,0:T(8,128)(2,1)} %get-tuple-element.164.refs_0_.act_ref, bf16[768,768]{1,0:T(8,128)(2,1)} %get-tuple-element.158.refs_1_.dy_ref), custom_call_target="tpu_custom_call" | custom-call | flops 2800000000 | bytes 10616832 | tf_op jit(solution)/shard_map/pallas_call | solution.py:54
  231.5 10.3 %shard_map.347 = (bf16[768,768]{1,0:T(8,128)(2,1)}, bf16[128,128]{1,0:T(8,128)(2,1)}) custom-call(s32[2]{0:T(128)} %pad_add_fusion.refs_0_.place_ref, bf16[768,3072]{1,0:T(8,128)(2,1)} %get-tuple-element.164.refs_0_.act_ref, f32[1,768]{1,0:T(1,128)} %reshape.185.bias_ref, bf16[3072,768]{1,0:T(8,128)(2,1)} %copy-done.10, bf16[768,768]{1,0:T(8,128)(2,1)} %bitcast.15.up_ref), custom_call_target="tpu_custom_call" | custom-call | flops 3600000000 | bytes 11832320 | tf_op jit(solution)/shard_map/pallas_call | solution.py:54
  241.8 15.7 %shard_map.348 = (bf16[768,3072]{1,0:T(8,128)(2,1)}, f32[1,3072]{1,0:T(1,128)}, bf16[768,768]{1,0:T(8,128)(2,1)}) custom-call(s32[2]{0:T(128)} %pad_add_fusion.refs_0_.place_ref, bf16[768,768]{1,0:T(8,128)(2,1)} %get-tuple-element.158.refs_1_.dy_ref, bf16[768,3072]{1,0:T(8,128)(2,1)} %get-tuple-element.159.slope_ref, bf16[3072,768]{1,0:T(8,128)(2,1)} %copy-done.10, ...), custom_call_target="tpu_custom_call" | custom-call | flops 6000000000 | bytes 21278720 | tf_op jit(solution)/shard_map/pallas_call | solution.py:54
  257.5 5.0 %all-to-all-start.2 = ((bf16[8,96,768]{2,1,0:T(8,128)(2,1)}), bf16[8,96,768]{2,1,0:T(8,128)(2,1)S(1)}, u32[]{:S(2)}, u32[]{:S(2)}) async-start(bf16[8,96,768]{2,1,0:T(8,128)(2,1)} %bitcast.162), calls=%async_computation.2 | async-start | bytes 2359296 | tf_op jit(solution)/shard_map/all_to_all | solution.py:1307
  265.5 8.4 %shard_map.349 = bf16[832,3072]{1,0:T(8,128)(2,1)} custom-call(bf16[768,768]{1,0:T(8,128)(2,1)} %bitcast.18.x_ref, bf16[768,3072]{1,0:T(8,128)(2,1)} %get-tuple-element.166.dh_ref, f32[1,3072]{1,0:T(1,128)} %get-tuple-element.167.in_bias_ref, f32[1,768]{1,0:T(1,128)} %get-tuple-element.168.out_bias_ref), custom_call_target="tpu_custom_call" | custom-call | flops 3200000000 | bytes 11025408 | tf_op jit(solution)/shard_map/pallas_call | solution.py:54
  274.0 14.4 %all-to-all-done.2 = bf16[8,96,768]{2,1,0:T(8,128)(2,1)S(1)} async-done(((bf16[8,96,768]{2,1,0:T(8,128)(2,1)}), bf16[8,96,768]{2,1,0:T(8,128)(2,1)S(1)}, u32[]{:S(2)}, u32[]{:S(2)}) %all-to-all-start.2) | async-done | bytes 1179680 | tf_op jit(solution)/shard_map/all_to_all | solution.py:1307
  289.4 7.0 %shard_map.350 = (f32[416,768]{1,0:T(8,128)}, f32[8,768]{1,0:T(8,128)}, f32[768,128]{1,0:T(8,128)}) custom-call(f32[416,768]{1,0:T(8,128)} %get-tuple-element.150.x_ref, f32[32,768]{1,0:T(8,128)} %get-tuple-element.142.vec_ref.refs_2_, bf16[768,768]{1,0:T(8,128)(2,1)} %bitcast.161, f32[416,128]{1,0:T(8,128)} %get-tuple-element.178.gate_ref, ...), custom_call_target="tpu_custom_call" | custom-call | flops 2800000000 | bytes 5945856 | tf_op jit(solution)/shard_map/pallas_call | solution.py:54
  296.4 19.2 %shard_map.351 = (f32[416,768]{1,0:T(8,128)}, bf16[416,1152]{1,0:T(8,128)(2,1)}, bf16[416,1152]{1,0:T(8,128)(2,1)}, bf16[416,384]{1,0:T(8,128)(2,1)}, bf16[416,384]{1,0:T(8,128)(2,1)}, /*index=5*/f32[8,768]{1,0:T(8,128)}) custom-call(s32[2]{0:T(128)} %pad_add_fusion.refs_0_.place_ref, f32[416,768]{1,0:T(8,128)} %get-tuple-element.180.up_ref, ...), custom_call_target="tpu_custom_call" | custom-call | flops 7600000000 | bytes 13148160 | tf_op jit(solution)/shard_map/pallas_call | solution.py:54
  315.7 12.9 %shard_map.352 = (f32[416,768]{1,0:T(8,128)}, bf16[416,1536]{1,0:T(8,128)(2,1)}, bf16[416,1536]{1,0:T(8,128)(2,1)}, bf16[416,384]{1,0:T(8,128)(2,1)}, bf16[416,3...) custom-call(s32[2]{0:T(128)} %pad_add_fusion.refs_0_.place_ref, f32[416,768]{1,0:T(8,128)} %get-tuple-element.182.up_ref, ...), custom_call_target="tpu_custom_call" | custom-call | flops 5200000000 | bytes 28594176 | tf_op jit(solution)/shard_map/pallas_call | solution.py:54
  329.7 7.0 %all-to-all-start.3 = ((bf16[8,96,768]{2,1,0:T(8,128)(2,1)}), bf16[8,96,768]{2,1,0:T(8,128)(2,1)}, u32[]{:S(2)}, u32[]{:S(2)}) async-start(bf16[8,96,768]{2,1,0:T(8,128)(2,1)} %bitcast.36), calls=%async_computation.5 | async-start | bytes 2359296 | tf_op jit(solution)/shard_map/all_to_all | solution.py:1307
  337.6 6.8 %shard_map.354 = bf16[768,1536]{1,0:T(8,128)(2,1)} custom-call(bf16[416,768]{1,0:T(8,128)(2,1)} %get-tuple-element.174.refs_0_, bf16[416,1152]{1,0:T(8,128)(2,1)} %get-tuple-element.195.refs_1_, bf16[416,768]{1,0:T(8,128)(2,1)} %collective-permute-done.34.refs_2_, bf16[416,1152]{1,0:T(8,128)(2,1)} %copy-done.30, ...), custom_call_target="tpu_custom_call" | custom-call | flops 2800000000 | bytes 7471104 | tf_op jit(solution)/shard_map/pallas_call | solution.py:54
  346.9 11.7 %shard_map.353 = bf16[6144,384]{1,0:T(8,128)(2,1)} custom-call(bf16[416,768]{1,0:T(8,128)(2,1)} %get-tuple-element.144.hn_ref, bf16[416,768]{1,0:T(8,128)(2,1)} %copy-done.35, bf16[416,1536]{1,0:T(8,128)(2,1)} %get-tuple-element.184.du_ref, bf16[416,1536]{1,0:T(8,128)(2,1)} %copy-done.28, bf16[416,3072]{1,0:T(8,128)(2,1)} %get-tuple-element.172.act_ref, ...), custom_call_target="tpu_custom_call" | custom-call | flops 4400000000 | bytes 14303232 | tf_op jit(solution)/shard_map/pallas_call | solution.py:54
  363.9 18.7 %shard_map.355 = (f32[416,768]{1,0:T(8,128)}, bf16[416,1152]{1,0:T(8,128)(2,1)}, bf16[416,1152]{1,0:T(8,128)(2,1)}, bf16[416,384]{1,0:T(8,128)(2,1)}, bf16[416,384]{1,0:T(8,128)(2,1)}, /*index=5*/f32[768,128]{1,0:T(8,128)}) custom-call(s32[2]{0:T(128)} %pad_add_fusion.refs_0_.place_ref, f32[416,768]{1,0:T(8,128)} %get-tuple-element.202.up_ref, ...), custom_call_target="tpu_custom_call" | custom-call | flops 7600000000 | bytes 14389248 | tf_op jit(solution)/shard_map/pallas_call | solution.py:54
  394.8 7.1 %shard_map.356 = bf16[768,1664]{1,0:T(8,128)(2,1)} custom-call(bf16[416,768]{1,0:T(8,128)(2,1)} %get-tuple-element.138.refs_0_, bf16[416,1152]{1,0:T(8,128)(2,1)} %get-tuple-element.213.refs_1_, bf16[416,768]{1,0:T(8,128)(2,1)} %copy-done.34, bf16[416,1152]{1,0:T(8,128)(2,1)} %collective-permute-done.46.refs_3_, ...), custom_call_target="tpu_custom_call" | custom-call | flops 2800000000 | bytes 8060928 | tf_op jit(solution)/shard_map/pallas_call | solution.py:54
  405.3 2.3 collective-permute-start.53
  407.6 3.7 collective-permute-done.53
  413.7 5.4 %collective-permute-done.54 = bf16[48,1536]{1,0:T(8,128)(2,1)S(1)} collective-permute-done((bf16[48,1536]{1,0:T(8,128)(2,1)}, bf16[48,1536]{1,0:T(8,128)(2,1)S(1)}, u32[]{:S(2)}, u32[]{:S(2)}) %collective-permute-start.54) | collective-permute-done | bytes 147488 | tf_op jit(solution)/shard_map/ppermute | solution.py:1057
  419.1 4.2 collective-permute-done.48
  426.2 3.5 collective-permute-start.65
  429.6 2.4 fusion.1
  441.1 3.9 shard_map.357
  449.1 13.0 %collective-permute-done.59 = bf16[384,384]{1,0:T(8,128)(2,1)} collective-permute-done((bf16[384,384]{1,0:T(8,128)(2,1)}, bf16[384,384]{1,0:T(8,128)(2,1)}, u32[]{:S(2)}, u32[]{:S(2)}) %collective-permute-start.59) | collective-permute-done | bytes 294944 | tf_op jit(solution)/shard_map/ppermute | solution.py:1057
  469.5 3.5 collective-permute-done.60
  475.0 7.5 %collective-permute-done.62 = bf16[48,1664]{1,0:T(8,128)(2,1)S(1)} collective-permute-done((bf16[48,1664]{1,0:T(8,128)(2,1)S(1)}, bf16[48,1664]{1,0:T(8,128)(2,1)S(1)}, u32[]{:S(2)}, u32[]{:S(2)}) %collective-permute-start.62) | collective-permute-done | bytes 159776 | tf_op jit(solution)/shard_map/ppermute | solution.py:1057
  (351 shorter events, 121.7 us)
Async XLA Ops:
  7.3 127.6 %all-gather.2.cloned.1.call-start = ((), (), s32[]{:S(2)}) async-start(), calls=%async_computation.6 | async-start | bytes 9732096 | tf_op jit(solution)/shard_map/all_gather | solution.py:1278
  12.5 27.6 %collective-permute-start.4 = (bf16[960]{0:T(1024)(128)(2,1)S(1)}, bf16[960]{0:T(1024)(128)(2,1)S(1)}, u32[]{:S(2)}, u32[]{:S(2)}) collective-permute-start(bf16[960]{0:T(1024)(128)(2,1)S(1)} %pad_maximum_fusion.13), channel_id=1, source_target_pairs={{0,8},{8,0},{16,24},{24,16},{1,9},{9,1},{17,25},{25,17},{2,10},{10... | collective-permute-start | bytes 5768 | tf_op jit(solution)/shard_map/ppermute | solution.py:1057
  13.8 26.3 %collective-permute-start.5 = (bf16[960]{0:T(1024)(128)(2,1)S(1)}, bf16[960]{0:T(1024)(128)(2,1)S(1)}, u32[]{:S(2)}, u32[]{:S(2)}) collective-permute-start(bf16[960]{0:T(1024)(128)(2,1)S(1)} %pad_maximum_fusion.13), channel_id=1, source_target_pairs={{0,16},{8,24},{16,0},{24,8},{1,17},{9,25},{17,1},{25,9},{2,18},{10... | collective-permute-start | bytes 5768 | tf_op jit(solution)/shard_map/ppermute | solution.py:1057
  15.0 25.1 %collective-permute-start.6 = (bf16[960]{0:T(1024)(128)(2,1)S(1)}, bf16[960]{0:T(1024)(128)(2,1)S(1)}, u32[]{:S(2)}, u32[]{:S(2)}) collective-permute-start(bf16[960]{0:T(1024)(128)(2,1)S(1)} %pad_maximum_fusion.13), channel_id=1, source_target_pairs={{0,24},{8,16},{16,8},{24,0},{1,25},{9,17},{17,9},{25,1},{2,26},{10... | collective-permute-start | bytes 5768 | tf_op jit(solution)/shard_map/ppermute | solution.py:1057
  23.4 16.5 %collective-permute-start.2 = (bf16[48,1664]{1,0:T(8,128)(2,1)S(1)}, bf16[48,1664]{1,0:T(8,128)(2,1)S(1)}, u32[]{:S(2)}, u32[]{:S(2)}) collective-permute-start(bf16[48,1664]{1,0:T(8,128)(2,1)S(1)} %maximum_select_fusion.7), channel_id=1, source_target_pairs={{0,4},{1,5},{2,6},{3,7},{4,0},{5,1},{6,2},{7,3},{8,12},{9,13},{10,... | collective-permute-start | bytes 479240 | tf_op jit(solution)/shard_map/ppermute | solution.py:1057
  40.1 18.7 %collective-permute-start.10 = (bf16[48,1536]{1,0:T(8,128)(2,1)S(1)}, bf16[48,1536]{1,0:T(8,128)(2,1)S(1)}, u32[]{:S(2)}, u32[]{:S(2)}) collective-permute-start(bf16[48,1536]{1,0:T(8,128)(2,1)S(1)} %maximum_select_fusion.8), channel_id=1, source_target_pairs={{0,6},{1,7},{2,4},{3,5},{4,2},{5,3},{6,0},{7,1},{8,14},{9,15},{10,... | collective-permute-start | bytes 442376 | tf_op jit(solution)/shard_map/ppermute | solution.py:1057
  40.6 19.9 %collective-permute-start.11 = (bf16[48,1536]{1,0:T(8,128)(2,1)S(1)}, bf16[48,1536]{1,0:T(8,128)(2,1)S(1)}, u32[]{:S(2)}, u32[]{:S(2)}) collective-permute-start(bf16[48,1536]{1,0:T(8,128)(2,1)S(1)} %maximum_select_fusion.8), channel_id=1, source_target_pairs={{0,4},{1,5},{2,6},{3,7},{4,0},{5,1},{6,2},{7,3},{8,12},{9,13},{10,... | collective-permute-start | bytes 442376 | tf_op jit(solution)/shard_map/ppermute | solution.py:1057
  45.0 13.8 %collective-permute-start.12 = (bf16[48,1536]{1,0:T(8,128)(2,1)S(1)}, bf16[48,1536]{1,0:T(8,128)(2,1)S(1)}, u32[]{:S(2)}, u32[]{:S(2)}) collective-permute-start(bf16[48,1536]{1,0:T(8,128)(2,1)S(1)} %maximum_select_fusion.8), channel_id=1, source_target_pairs={{0,2},{1,3},{2,0},{3,1},{4,6},{5,7},{6,4},{7,5},{8,10},{9,11},{10,... | collective-permute-start | bytes 442376 | tf_op jit(solution)/shard_map/ppermute | solution.py:1057
  45.0 23.1 %collective-permute-start.8 = (bf16[192,1664]{1,0:T(8,128)(2,1)S(1)}, bf16[192,1664]{1,0:T(8,128)(2,1)S(1)}, u32[]{:S(2)}, u32[]{:S(2)}) collective-permute-start(bf16[192,1664]{1,0:T(8,128)(2,1)S(1)} %maximum_select_fusion), channel_id=1, source_target_pairs={{0,8},{8,0},{16,24},{24,16},{1,9},{9,1},{17,25},{25,17},{2,10},{10... | collective-permute-start | bytes 1916936 | tf_op jit(solution)/shard_map/ppermute | solution.py:1057
  46.1 22.0 %collective-permute-start.9 = (bf16[192,1664]{1,0:T(8,128)(2,1)S(1)}, bf16[192,1664]{1,0:T(8,128)(2,1)S(1)}, u32[]{:S(2)}, u32[]{:S(2)}) collective-permute-start(bf16[192,1664]{1,0:T(8,128)(2,1)S(1)} %maximum_select_fusion), channel_id=1, source_target_pairs={{0,16},{8,24},{16,0},{24,8},{1,17},{9,25},{17,1},{25,9},{2,18},{10... | collective-permute-start | bytes 1916936 | tf_op jit(solution)/shard_map/ppermute | solution.py:1057
  78.6 16.4 %collective-permute-start.15 = (bf16[768,1664]{1,0:T(8,128)(2,1)}, bf16[768,1664]{1,0:T(8,128)(2,1)}, u32[]{:S(2)}, u32[]{:S(2)}) collective-permute-start(bf16[768,1664]{1,0:T(8,128)(2,1)} %constant_dynamic-update-slice_fusion.2.refs_2_.refs_5_), channel_id=1, source_target_pairs={{0,1},{1,0},{2,3},{3,2},{4,5},{5,4},{6,7},{7,6},{8,9},{9,8},{10,11... | collective-permute-start | bytes 7667720 | tf_op jit(solution)/shard_map/ppermute | solution.py:1057
  92.0 17.6 %collective-permute-start.16 = (bf16[192,1536]{1,0:T(8,128)(2,1)S(1)}, bf16[192,1536]{1,0:T(8,128)(2,1)S(1)}, u32[]{:S(2)}, u32[]{:S(2)}) collective-permute-start(bf16[192,1536]{1,0:T(8,128)(2,1)S(1)} %maximum_select_fusion.1), channel_id=1, source_target_pairs={{0,8},{8,0},{16,24},{24,16},{1,9},{9,1},{17,25},{25,17},{2,10},{10... | collective-permute-start | bytes 1769480 | tf_op jit(solution)/shard_map/ppermute | solution.py:1057
  92.0 17.8 %collective-permute-start.17 = (bf16[192,1536]{1,0:T(8,128)(2,1)S(1)}, bf16[192,1536]{1,0:T(8,128)(2,1)S(1)}, u32[]{:S(2)}, u32[]{:S(2)}) collective-permute-start(bf16[192,1536]{1,0:T(8,128)(2,1)S(1)} %maximum_select_fusion.1), channel_id=1, source_target_pairs={{0,16},{8,24},{16,0},{24,8},{1,17},{9,25},{17,1},{25,9},{2,18},{10... | collective-permute-start | bytes 1769480 | tf_op jit(solution)/shard_map/ppermute | solution.py:1057
  120.3 25.6 %collective-permute-start.21 = (bf16[768,1536]{1,0:T(8,128)(2,1)}, bf16[768,1536]{1,0:T(8,128)(2,1)}, u32[]{:S(2)}, u32[]{:S(2)}) collective-permute-start(bf16[768,1536]{1,0:T(8,128)(2,1)} %constant_dynamic-update-slice_fusion.7.refs_3_.refs_0_), channel_id=1, source_target_pairs={{0,1},{1,0},{2,3},{3,2},{4,5},{5,4},{6,7},{7,6},{8,9},{9,8},{10,11... | collective-permute-start | bytes 7077896 | tf_op jit(solution)/shard_map/ppermute | solution.py:1057
  122.0 34.3 %all-to-all-start = ((bf16[8,96,768]{2,1,0:T(8,128)(2,1)}), bf16[8,96,768]{2,1,0:T(8,128)(2,1)}, u32[]{:S(2)}, u32[]{:S(2)}) async-start(bf16[8,96,768]{2,1,0:T(8,128)(2,1)} %bitcast.14), calls=%async_computation | async-start | bytes 2359296 | tf_op jit(solution)/shard_map/all_to_all | solution.py:1307
  129.5 39.5 %collective-permute-start.26 = (bf16[768,768]{1,0:T(8,128)(2,1)}, bf16[768,768]{1,0:T(8,128)(2,1)S(1)}, u32[]{:S(2)}, u32[]{:S(2)}) collective-permute-start(bf16[768,768]{1,0:T(8,128)(2,1)} %bitcast.12), channel_id=1, source_target_pairs={{0,8},{8,0},{16,24},{24,16},{1,9},{9,1},{17,25},{25,17},{2,10},{10... | collective-permute-start | bytes 3538952 | tf_op jit(solution)/shard_map/ppermute | solution.py:1057
  129.7 39.2 %collective-permute-start.27 = (bf16[768,768]{1,0:T(8,128)(2,1)}, bf16[768,768]{1,0:T(8,128)(2,1)S(1)}, u32[]{:S(2)}, u32[]{:S(2)}) collective-permute-start(bf16[768,768]{1,0:T(8,128)(2,1)} %bitcast.12), channel_id=1, source_target_pairs={{0,16},{8,24},{16,0},{24,8},{1,17},{9,25},{17,1},{25,9},{2,18},{10... | collective-permute-start | bytes 3538952 | tf_op jit(solution)/shard_map/ppermute | solution.py:1057
  131.0 52.6 %collective-permute-start.22 = (bf16[192,3072]{1,0:T(8,128)(2,1)}, bf16[192,3072]{1,0:T(8,128)(2,1)}, u32[]{:S(2)}, u32[]{:S(2)}) collective-permute-start(bf16[192,3072]{1,0:T(8,128)(2,1)} %bitcast.11), channel_id=1, source_target_pairs={{0,8},{8,0},{16,24},{24,16},{1,9},{9,1},{17,25},{25,17},{2,10},{10... | collective-permute-start | bytes 3538952 | tf_op jit(solution)/shard_map/ppermute | solution.py:1057
  132.0 50.1 %collective-permute-start.23 = (bf16[192,3072]{1,0:T(8,128)(2,1)}, bf16[192,3072]{1,0:T(8,128)(2,1)S(1)}, u32[]{:S(2)}, u32[]{:S(2)}) collective-permute-start(bf16[192,3072]{1,0:T(8,128)(2,1)} %bitcast.11), channel_id=1, source_target_pairs={{0,16},{8,24},{16,0},{24,8},{1,17},{9,25},{17,1},{25,9},{2,18},{10... | collective-permute-start | bytes 3538952 | tf_op jit(solution)/shard_map/ppermute | solution.py:1057
  161.0 48.3 %all-to-all-start.1 = ((bf16[8,96,768]{2,1,0:T(8,128)(2,1)}), bf16[8,96,768]{2,1,0:T(8,128)(2,1)}, u32[]{:S(2)}, u32[]{:S(2)}) async-start(bf16[8,96,768]{2,1,0:T(8,128)(2,1)} %bitcast.160), calls=%async_computation.1 | async-start | bytes 2359296 | tf_op jit(solution)/shard_map/all_to_all | solution.py:1307
  167.2 121.2 %reduce-scatter.3.cloned.1.call-start = ((), (), s32[]{:S(2)}) async-start(), calls=%async_computation.7 | async-start | bytes 5898240 | tf_op jit(solution)/shard_map/reduce_scatter | solution.py:1343
  168.9 26.0 %collective-permute-start.28 = (bf16[384,768]{1,0:T(8,128)(2,1)S(1)}, bf16[384,768]{1,0:T(8,128)(2,1)S(1)}, u32[]{:S(2)}, u32[]{:S(2)}) collective-permute-start(bf16[384,768]{1,0:T(8,128)(2,1)S(1)} %slice.339), channel_id=1, source_target_pairs={{0,8},{8,0},{16,24},{24,16},{1,9},{9,1},{17,25},{25,17},{2,10},{10... | collective-permute-start | bytes 1769480 | tf_op jit(solution)/shard_map/ppermute | solution.py:1057
  169.1 25.8 %collective-permute-start.29 = (bf16[384,768]{1,0:T(8,128)(2,1)S(1)}, bf16[384,768]{1,0:T(8,128)(2,1)S(1)}, u32[]{:S(2)}, u32[]{:S(2)}) collective-permute-start(bf16[384,768]{1,0:T(8,128)(2,1)S(1)} %slice.340), channel_id=1, source_target_pairs={{0,16},{8,24},{16,0},{24,8},{1,17},{9,25},{17,1},{25,9},{2,18},{10... | collective-permute-start | bytes 1769480 | tf_op jit(solution)/shard_map/ppermute | solution.py:1057
  182.2 25.3 %collective-permute-start.24 = (bf16[96,3072]{1,0:T(8,128)(2,1)S(1)}, bf16[96,3072]{1,0:T(8,128)(2,1)S(1)}, u32[]{:S(2)}, u32[]{:S(2)}) collective-permute-start(bf16[96,3072]{1,0:T(8,128)(2,1)S(1)} %slice.337), channel_id=1, source_target_pairs={{0,8},{8,0},{16,24},{24,16},{1,9},{9,1},{17,25},{25,17},{2,10},{10... | collective-permute-start | bytes 1769480 | tf_op jit(solution)/shard_map/ppermute | solution.py:1057
  184.7 23.7 %collective-permute-start.25 = (bf16[96,3072]{1,0:T(8,128)(2,1)S(1)}, bf16[96,3072]{1,0:T(8,128)(2,1)S(1)}, u32[]{:S(2)}, u32[]{:S(2)}) collective-permute-start(bf16[96,3072]{1,0:T(8,128)(2,1)S(1)} %slice.338), channel_id=1, source_target_pairs={{0,16},{8,24},{16,0},{24,8},{1,17},{9,25},{17,1},{25,9},{2,18},{10... | collective-permute-start | bytes 1769480 | tf_op jit(solution)/shard_map/ppermute | solution.py:1057
  230.3 43.6 %collective-permute-start.31 = (bf16[416,3072]{1,0:T(8,128)(2,1)}, bf16[416,3072]{1,0:T(8,128)(2,1)}, u32[]{:S(2)}, u32[]{:S(2)}) collective-permute-start(bf16[416,3072]{1,0:T(8,128)(2,1)} %get-tuple-element.172.act_ref), channel_id=1, source_target_pairs={{0,1},{1,0},{2,3},{3,2},{4,5},{5,4},{6,7},{7,6},{8,9},{9,8},{10,11... | collective-permute-start | bytes 7667720 | tf_op jit(solution)/shard_map/ppermute | solution.py:1057
  257.5 30.9 %all-to-all-start.2 = ((bf16[8,96,768]{2,1,0:T(8,128)(2,1)}), bf16[8,96,768]{2,1,0:T(8,128)(2,1)S(1)}, u32[]{:S(2)}, u32[]{:S(2)}) async-start(bf16[8,96,768]{2,1,0:T(8,128)(2,1)} %bitcast.162), calls=%async_computation.2 | async-start | bytes 2359296 | tf_op jit(solution)/shard_map/all_to_all | solution.py:1307
  262.5 123.7 %reduce-scatter.5.cloned.1.call-start = ((), (), s32[]{:S(2)}) async-start(), calls=%async_computation.8 | async-start | bytes 6389760 | tf_op jit(solution)/shard_map/reduce_scatter | solution.py:1358
  263.0 10.9 %collective-permute-start.33 = (bf16[416,768]{1,0:T(8,128)(2,1)S(1)}, bf16[416,768]{1,0:T(8,128)(2,1)}, u32[]{:S(2)}, u32[]{:S(2)}) collective-permute-start(bf16[416,768]{1,0:T(8,128)(2,1)S(1)} %copy-done.32), channel_id=1, source_target_pairs={{0,1},{1,0},{2,3},{3,2},{4,5},{5,4},{6,7},{7,6},{8,9},{9,8},{10,11... | collective-permute-start | bytes 1916936 | tf_op jit(solution)/shard_map/ppermute | solution.py:1057
  329.7 84.0 %all-to-all-start.3 = ((bf16[8,96,768]{2,1,0:T(8,128)(2,1)}), bf16[8,96,768]{2,1,0:T(8,128)(2,1)}, u32[]{:S(2)}, u32[]{:S(2)}) async-start(bf16[8,96,768]{2,1,0:T(8,128)(2,1)} %bitcast.36), calls=%async_computation.5 | async-start | bytes 2359296 | tf_op jit(solution)/shard_map/all_to_all | solution.py:1307
  345.8 12.8 %collective-permute-start.40 = (bf16[2,48,1536]{2,1,0:T(8,128)(2,1)S(1)}, bf16[2,48,1536]{2,1,0:T(8,128)(2,1)S(1)}, u32[]{:S(2)}, u32[]{:S(2)}) collective-permute-start(bf16[2,48,1536]{2,1,0:T(8,128)(2,1)S(1)} %get-tuple-element.316), channel_id=1, source_target_pairs={{0,8},{8,0},{16,24},{24,16},{1,9},{9,1},{17,25},{25,17},{2,10},{10... | collective-permute-start | bytes 884744 | tf_op jit(solution)/shard_map/ppermute | solution.py:1057
  345.8 12.8 %collective-permute-start.41 = (bf16[2,48,1536]{2,1,0:T(8,128)(2,1)S(1)}, bf16[2,48,1536]{2,1,0:T(8,128)(2,1)S(1)}, u32[]{:S(2)}, u32[]{:S(2)}) collective-permute-start(bf16[2,48,1536]{2,1,0:T(8,128)(2,1)S(1)} %get-tuple-element.317), channel_id=1, source_target_pairs={{0,16},{8,24},{16,0},{24,8},{1,17},{9,25},{17,1},{25,9},{2,18},{10... | collective-permute-start | bytes 884744 | tf_op jit(solution)/shard_map/ppermute | solution.py:1057
  358.8 25.9 %collective-permute-start.45 = (bf16[4,48,1536]{2,1,0:T(8,128)(2,1)S(1)}, bf16[4,48,1536]{2,1,0:T(8,128)(2,1)}, u32[]{:S(2)}, u32[]{:S(2)}) collective-permute-start(bf16[4,48,1536]{2,1,0:T(8,128)(2,1)S(1)} %pad_maximum_fusion.5), channel_id=1, source_target_pairs={{0,16},{8,24},{16,0},{24,8},{1,17},{9,25},{17,1},{25,9},{2,18},{10... | collective-permute-start | bytes 1769480 | tf_op jit(solution)/shard_map/ppermute | solution.py:1057
  359.6 25.3 %collective-permute-start.44 = (bf16[4,48,1536]{2,1,0:T(8,128)(2,1)S(1)}, bf16[4,48,1536]{2,1,0:T(8,128)(2,1)}, u32[]{:S(2)}, u32[]{:S(2)}) collective-permute-start(bf16[4,48,1536]{2,1,0:T(8,128)(2,1)S(1)} %pad_maximum_fusion.4), channel_id=1, source_target_pairs={{0,8},{8,0},{16,24},{24,16},{1,9},{9,1},{17,25},{25,17},{2,10},{10... | collective-permute-start | bytes 1769480 | tf_op jit(solution)/shard_map/ppermute | solution.py:1057
  362.8 23.5 %collective-permute-start.42 = (bf16[2,384,384]{2,1,0:T(8,128)(2,1)S(1)}, bf16[2,384,384]{2,1,0:T(8,128)(2,1)}, u32[]{:S(2)}, u32[]{:S(2)}) collective-permute-start(bf16[2,384,384]{2,1,0:T(8,128)(2,1)S(1)} %get-tuple-element.304), channel_id=1, source_target_pairs={{0,8},{8,0},{16,24},{24,16},{1,9},{9,1},{17,25},{25,17},{2,10},{10... | collective-permute-start | bytes 1769480 | tf_op jit(solution)/shard_map/ppermute | solution.py:1057
  363.0 23.2 %collective-permute-start.43 = (bf16[2,384,384]{2,1,0:T(8,128)(2,1)S(1)}, bf16[2,384,384]{2,1,0:T(8,128)(2,1)}, u32[]{:S(2)}, u32[]{:S(2)}) collective-permute-start(bf16[2,384,384]{2,1,0:T(8,128)(2,1)S(1)} %get-tuple-element.305), channel_id=1, source_target_pairs={{0,16},{8,24},{16,0},{24,8},{1,17},{9,25},{17,1},{25,9},{2,18},{10... | collective-permute-start | bytes 1769480 | tf_op jit(solution)/shard_map/ppermute | solution.py:1057
  382.6 12.3 %collective-permute-start.46 = (bf16[416,1152]{1,0:T(8,128)(2,1)}, bf16[416,1152]{1,0:T(8,128)(2,1)}, u32[]{:S(2)}, u32[]{:S(2)}) collective-permute-start(bf16[416,1152]{1,0:T(8,128)(2,1)} %get-tuple-element.215), channel_id=1, source_target_pairs={{0,1},{1,0},{2,3},{3,2},{4,5},{5,4},{6,7},{7,6},{8,9},{9,8},{10,11... | collective-permute-start | bytes 2875400 | tf_op jit(solution)/shard_map/ppermute | solution.py:1057
  389.6 33.8 %collective-permute-start.51 = (bf16[4,384,384]{2,1,0:T(8,128)(2,1)}, bf16[4,384,384]{2,1,0:T(8,128)(2,1)}, u32[]{:S(2)}, u32[]{:S(2)}) collective-permute-start(bf16[4,384,384]{2,1,0:T(8,128)(2,1)} %pad_maximum_fusion.1), channel_id=1, source_target_pairs={{0,16},{8,24},{16,0},{24,8},{1,17},{9,25},{17,1},{25,9},{2,18},{10... | collective-permute-start | bytes 3538952 | tf_op jit(solution)/shard_map/ppermute | solution.py:1057
  391.2 32.1 %collective-permute-start.50 = (bf16[4,384,384]{2,1,0:T(8,128)(2,1)}, bf16[4,384,384]{2,1,0:T(8,128)(2,1)}, u32[]{:S(2)}, u32[]{:S(2)}) collective-permute-start(bf16[4,384,384]{2,1,0:T(8,128)(2,1)} %pad_maximum_fusion), channel_id=1, source_target_pairs={{0,8},{8,0},{16,24},{24,16},{1,9},{9,1},{17,25},{25,17},{2,10},{10... | collective-permute-start | bytes 3538952 | tf_op jit(solution)/shard_map/ppermute | solution.py:1057
  404.3 19.0 %collective-permute-start.48 = (bf16[2,48,1664]{2,1,0:T(8,128)(2,1)}, bf16[2,48,1664]{2,1,0:T(8,128)(2,1)S(1)}, u32[]{:S(2)}, u32[]{:S(2)}) collective-permute-start(bf16[2,48,1664]{2,1,0:T(8,128)(2,1)} %get-tuple-element.309), channel_id=1, source_target_pairs={{0,8},{8,0},{16,24},{24,16},{1,9},{9,1},{17,25},{25,17},{2,10},{10... | collective-permute-start | bytes 958472 | tf_op jit(solution)/shard_map/ppermute | solution.py:1057
  404.5 18.8 %collective-permute-start.49 = (bf16[2,48,1664]{2,1,0:T(8,128)(2,1)}, bf16[2,48,1664]{2,1,0:T(8,128)(2,1)S(1)}, u32[]{:S(2)}, u32[]{:S(2)}) collective-permute-start(bf16[2,48,1664]{2,1,0:T(8,128)(2,1)} %get-tuple-element.311), channel_id=1, source_target_pairs={{0,16},{8,24},{16,0},{24,8},{1,17},{9,25},{17,1},{25,9},{2,18},{10... | collective-permute-start | bytes 958472 | tf_op jit(solution)/shard_map/ppermute | solution.py:1057
  426.2 19.4 %collective-permute-start.65 = (bf16[24,1536]{1,0:T(8,128)(2,1)S(1)}, bf16[24,1536]{1,0:T(8,128)(2,1)S(1)}, u32[]{:S(2)}, u32[]{:S(2)}) collective-permute-start(bf16[24,1536]{1,0:T(8,128)(2,1)S(1)} %dynamic-slice_convert_fusion.1), channel_id=1, source_target_pairs={{0,1},{1,0},{2,3},{3,2},{4,5},{5,4},{6,7},{7,6},{8,9},{9,8},{10,11... | collective-permute-start | bytes 221192 | tf_op jit(solution)/shard_map/ppermute | solution.py:1057
  433.0 15.3 %collective-permute-start.57 = (bf16[384,384]{1,0:T(8,128)(2,1)}, bf16[384,384]{1,0:T(8,128)(2,1)}, u32[]{:S(2)}, u32[]{:S(2)}) collective-permute-start(bf16[384,384]{1,0:T(8,128)(2,1)} %get-tuple-element.320), channel_id=1, source_target_pairs={{0,2},{1,3},{2,0},{3,1},{4,6},{5,7},{6,4},{7,5},{8,10},{9,11},{10,... | collective-permute-start | bytes 884744 | tf_op jit(solution)/shard_map/ppermute | solution.py:1057
  434.7 14.4 %collective-permute-start.58 = (bf16[384,384]{1,0:T(8,128)(2,1)}, bf16[384,384]{1,0:T(8,128)(2,1)}, u32[]{:S(2)}, u32[]{:S(2)}) collective-permute-start(bf16[384,384]{1,0:T(8,128)(2,1)} %get-tuple-element.319), channel_id=1, source_target_pairs={{0,4},{1,5},{2,6},{3,7},{4,0},{5,1},{6,2},{7,3},{8,12},{9,13},{10,... | collective-permute-start | bytes 884744 | tf_op jit(solution)/shard_map/ppermute | solution.py:1057
  435.4 26.6 %collective-permute-start.59 = (bf16[384,384]{1,0:T(8,128)(2,1)}, bf16[384,384]{1,0:T(8,128)(2,1)}, u32[]{:S(2)}, u32[]{:S(2)}) collective-permute-start(bf16[384,384]{1,0:T(8,128)(2,1)} %get-tuple-element.318), channel_id=1, source_target_pairs={{0,6},{1,7},{2,4},{3,5},{4,2},{5,3},{6,0},{7,1},{8,14},{9,15},{10,... | collective-permute-start | bytes 884744 | tf_op jit(solution)/shard_map/ppermute | solution.py:1057
  436.1 26.0 %collective-permute-start.56 = (bf16[4,48,1664]{2,1,0:T(8,128)(2,1)S(1)}, bf16[4,48,1664]{2,1,0:T(8,128)(2,1)S(1)}, u32[]{:S(2)}, u32[]{:S(2)}) collective-permute-start(bf16[4,48,1664]{2,1,0:T(8,128)(2,1)S(1)} %pad_maximum_fusion.3), channel_id=1, source_target_pairs={{0,16},{8,24},{16,0},{24,8},{1,17},{9,25},{17,1},{25,9},{2,18},{10... | collective-permute-start | bytes 1916936 | tf_op jit(solution)/shard_map/ppermute | solution.py:1057
  445.6 16.5 %collective-permute-start.55 = (bf16[4,48,1664]{2,1,0:T(8,128)(2,1)S(1)}, bf16[4,48,1664]{2,1,0:T(8,128)(2,1)S(1)}, u32[]{:S(2)}, u32[]{:S(2)}) collective-permute-start(bf16[4,48,1664]{2,1,0:T(8,128)(2,1)S(1)} %pad_maximum_fusion.2), channel_id=1, source_target_pairs={{0,8},{8,0},{16,24},{24,16},{1,9},{9,1},{17,25},{25,17},{2,10},{10... | collective-permute-start | bytes 1916936 | tf_op jit(solution)/shard_map/ppermute | solution.py:1057
  467.3 15.2 %collective-permute-start.62 = (bf16[48,1664]{1,0:T(8,128)(2,1)S(1)}, bf16[48,1664]{1,0:T(8,128)(2,1)S(1)}, u32[]{:S(2)}, u32[]{:S(2)}) collective-permute-start(bf16[48,1664]{1,0:T(8,128)(2,1)S(1)} %get-tuple-element.322), channel_id=1, source_target_pairs={{0,6},{1,7},{2,4},{3,5},{4,2},{5,3},{6,0},{7,1},{8,14},{9,15},{10,... | collective-permute-start | bytes 479240 | tf_op jit(solution)/shard_map/ppermute | solution.py:1057
  (62 other events, 496.0 us)
Sparse Core Ops, SparseCore 0:
  12.6 100.7 all-gather.1
  229.8 57.7 reduce-scatter.2
  290.6 60.7 reduce-scatter.4

commit v3 on v2

--- a/solution.py
+++ b/solution.py
@@ -1337,9 +1337,8 @@
     e_act, e_slope, dy, out_bias_grad = hidden_forward(
         place, arrived, in_bias, w_in, up_slots, planes, experts
     )
-    e_act, w_out = tie((e_act, w_out))
     out_grad = products([[(e_act, dy)]], part=768)
-    out_grad, e_act = tie((out_grad, e_act))
+    out_grad, e_act, w_out = tie((out_grad, e_act, w_out))
     expert_out_sum = lax.psum_scatter(out_grad, "fsdp", scatter_dimension=0, tiled=True)
     hidden_rows = inner // planes
     result, dots = expert_out_forward(

time: 507 us -> 507 us (level)
  no operation moved by 1% of the time
where the time goes in v3:
time: 507 us; the launch traced here: 497 us
  Pallas kernels  182 us (36%)
  waiting for transfers between devices  138 us (27%)
  starting transfers between devices  91 us (18%)
  local copies, waits for them, and re-layouts  46 us (9%)
  other arithmetic  23.9 us (5%)
  between operations  16.1 us (3%)
    pallas_call x18, Pallas kernels, run_kernel(): pl.pallas_call(kernel, out_shape=list(outs), compiler_params=pltpu.Compil...  182 us
    ppermute x66, waiting for transfers between devices, trade(): lax.ppermute(value, axis_name, [(place, place ^ mask) for place in range(...  124 us
    ppermute x66, starting transfers between devices, trade(): lax.ppermute(value, axis_name, [(place, place ^ mask) for place in range(...  66.5 us
    unnamed x115, local copies, waits for them, and re-layouts  25.3 us
    all_to_all x4, starting transfers between devices, exchange(): lax.all_to_all(array.reshape(experts, capacity, width), 'expert', split_a...  24.2 us
    all_to_all x4, waiting for transfers between devices, exchange(): lax.all_to_all(array.reshape(experts, capacity, width), 'expert', split_a...  14.4 us
  transfers between devices with their start and end apart: 73, of which 29 were waited for; matrix products, arithmetic and copies ran while one was open for 11% of the time, Pallas kernels for 32%

profile of v3, /device:TPU:9, one launch (start us, length us, event | category | flops | bytes accessed | tf_op | source)
XLA Modules:
  0.0 497.1 jit_solution(6556924330314155658)
XLA Ops:
  18.5 2.3 collective-permute-start.1
  20.8 2.6 collective-permute-done.3
  23.4 2.5 collective-permute-start.2
  26.0 13.9 %collective-permute-done.2 = bf16[48,1664]{1,0:T(8,128)(2,1)S(1)} collective-permute-done((bf16[48,1664]{1,0:T(8,128)(2,1)S(1)}, bf16[48,1664]{1,0:T(8,128)(2,1)S(1)}, u32[]{:S(2)}, u32[]{:S(2)}) %collective-permute-start.2) | collective-permute-done | bytes 159776 | tf_op jit(solution)/shard_map/ppermute | solution.py:1057
  40.6 4.3 collective-permute-start.11
  48.3 10.5 %collective-permute-done.12 = bf16[48,1536]{1,0:T(8,128)(2,1)S(1)} collective-permute-done((bf16[48,1536]{1,0:T(8,128)(2,1)S(1)}, bf16[48,1536]{1,0:T(8,128)(2,1)S(1)}, u32[]{:S(2)}, u32[]{:S(2)}) %collective-permute-start.12) | collective-permute-done | bytes 147488 | tf_op jit(solution)/shard_map/ppermute | solution.py:1057
  60.7 7.4 %collective-permute-done.8 = bf16[192,1664]{1,0:T(8,128)(2,1)S(1)} collective-permute-done((bf16[192,1664]{1,0:T(8,128)(2,1)S(1)}, bf16[192,1664]{1,0:T(8,128)(2,1)S(1)}, u32[]{:S(2)}, u32[]{:S(2)}) %collective-permute-start.8) | collective-permute-done | bytes 639008 | tf_op jit(solution)/shard_map/ppermute | solution.py:1057
  73.1 2.4 collective-permute-done.13
  78.6 4.3 collective-permute-start.15
  88.3 3.1 shard_map.340
  95.1 10.6 %shard_map.341 = (bf16[416,768]{1,0:T(8,128)(2,1)}, bf16[416,2304]{1,0:T(8,128)(2,1)}, bf16[416,768]{1,0:T(8,128)(2,1)}, f32[416,768]{1,0:T(8,128)}, f32[32,768]...) custom-call(s32[2]{0:T(128)} %pad_add_fusion.refs_0_.place_ref, f32[416,768]{1,0:T(8,128)} %bitcast.157, ...), custom_call_target="tpu_custom_call" | custom-call | flops 4400000000 | bytes 11169792 | tf_op jit(solution)/shard_map/pallas_call | solution.py:54
  105.7 3.9 collective-permute-done.16
  113.1 4.9 collective-permute-done.19
  122.0 6.0 %all-to-all-start = ((bf16[8,96,768]{2,1,0:T(8,128)(2,1)}), bf16[8,96,768]{2,1,0:T(8,128)(2,1)}, u32[]{:S(2)}, u32[]{:S(2)}) async-start(bf16[8,96,768]{2,1,0:T(8,128)(2,1)} %bitcast.14), calls=%async_computation | async-start | bytes 2359296 | tf_op jit(solution)/shard_map/all_to_all | solution.py:1307
  132.5 2.4 constant_dynamic-update-slice_fusion.16
  134.9 10.9 %shard_map.342 = (bf16[416,768]{1,0:T(8,128)(2,1)}, bf16[416,3072]{1,0:T(8,128)(2,1)}, bf16[416,3072]{1,0:T(8,128)(2,1)}, f32[416,768]{1,0:T(8,128)}) custom-call(f32[416,768]{1,0:T(8,128)} %get-tuple-element.140.x_ref, f32[32,768]{1,0:T(8,128)} %get-tuple-element.141.vec_ref.refs_2_, f32[1,3072]{1,0:T(1,128)} %get-tuple-element.142.bias_ref, ...), custom_call_target="tpu_custom_call" | custom-call | flops 4400000000 | bytes 27291648 | tf_op jit(solution)/shard_map/pallas_call | solution.py:54
  145.8 10.4 %shard_map.343 = (bf16[416,768]{1,0:T(8,128)(2,1)}, bf16[416,2304]{1,0:T(8,128)(2,1)}, bf16[416,768]{1,0:T(8,128)(2,1)}, f32[416,768]{1,0:T(8,128)}) custom-call(s32[2]{0:T(128)} %pad_add_fusion.refs_0_.place_ref, f32[416,768]{1,0:T(8,128)} %get-tuple-element.144.refs_1_.x_ref, f32[32,768]{1,0:T(8,128)} %get-tuple-element.141.vec_ref.refs_2_, ...), custom_call_target="tpu_custom_call" | custom-call | flops 4400000000 | bytes 10567680 | tf_op jit(solution)/shard_map/pallas_call | solution.py:54
  156.3 4.7 shard_map.344
  161.0 6.2 %all-to-all-start.1 = ((bf16[8,96,768]{2,1,0:T(8,128)(2,1)}), bf16[8,96,768]{2,1,0:T(8,128)(2,1)}, u32[]{:S(2)}, u32[]{:S(2)}) async-start(bf16[8,96,768]{2,1,0:T(8,128)(2,1)} %bitcast.160), calls=%async_computation.1 | async-start | bytes 2359296 | tf_op jit(solution)/shard_map/all_to_all | solution.py:1307
  170.5 11.6 %collective-permute-done.23 = bf16[192,3072]{1,0:T(8,128)(2,1)S(1)} collective-permute-done((bf16[192,3072]{1,0:T(8,128)(2,1)}, bf16[192,3072]{1,0:T(8,128)(2,1)S(1)}, u32[]{:S(2)}, u32[]{:S(2)}) %collective-permute-start.23) | collective-permute-done | bytes 1179680 | tf_op jit(solution)/shard_map/ppermute | solution.py:1057
  185.8 2.4 constant_dynamic-update-slice_fusion.15
  189.4 5.4 %collective-permute-done.28 = bf16[384,768]{1,0:T(8,128)(2,1)S(1)} collective-permute-done((bf16[384,768]{1,0:T(8,128)(2,1)S(1)}, bf16[384,768]{1,0:T(8,128)(2,1)S(1)}, u32[]{:S(2)}, u32[]{:S(2)}) %collective-permute-start.28) | collective-permute-done | bytes 589856 | tf_op jit(solution)/shard_map/ppermute | solution.py:1057
  195.0 12.5 %collective-permute-done.24 = bf16[96,3072]{1,0:T(8,128)(2,1)S(1)} collective-permute-done((bf16[96,3072]{1,0:T(8,128)(2,1)S(1)}, bf16[96,3072]{1,0:T(8,128)(2,1)S(1)}, u32[]{:S(2)}, u32[]{:S(2)}) %collective-permute-start.24) | collective-permute-done | bytes 589856 | tf_op jit(solution)/shard_map/ppermute | solution.py:1057
  209.3 12.5 %shard_map.345 = (bf16[768,3072]{1,0:T(8,128)(2,1)}, bf16[768,3072]{1,0:T(8,128)(2,1)}, bf16[768,768]{1,0:T(8,128)(2,1)}, f32[1,768]{1,0:T(1,128)}) custom-call(s32[2]{0:T(128)} %pad_add_fusion.refs_0_.place_ref, bf16[768,768]{1,0:T(8,128)(2,1)} %bitcast.18.x_ref, f32[1,3072]{1,0:T(1,128)} %bitcast.181, ...), custom_call_target="tpu_custom_call" | custom-call | flops 4400000000 | bytes 17710080 | tf_op jit(solution)/shard_map/pallas_call | solution.py:54
  221.8 7.9 %shard_map.346 = bf16[3072,768]{1,0:T(8,128)(2,1)} custom-call(bf16[768,3072]{1,0:T(8,128)(2,1)} %get-tuple-element.162.refs_0_.act_ref, bf16[768,768]{1,0:T(8,128)(2,1)} %get-tuple-element.157.refs_1_.dy_ref), custom_call_target="tpu_custom_call" | custom-call | flops 2800000000 | bytes 10616832 | tf_op jit(solution)/shard_map/pallas_call | solution.py:54
  231.5 10.3 %shard_map.347 = (bf16[768,768]{1,0:T(8,128)(2,1)}, bf16[128,128]{1,0:T(8,128)(2,1)}) custom-call(s32[2]{0:T(128)} %pad_add_fusion.refs_0_.place_ref, bf16[768,3072]{1,0:T(8,128)(2,1)} %get-tuple-element.162.refs_0_.act_ref, f32[1,768]{1,0:T(1,128)} %reshape.185.bias_ref, bf16[3072,768]{1,0:T(8,128)(2,1)} %copy-done.10, bf16[768,768]{1,0:T(8,128)(2,1)} %bitcast.15.up_ref), custom_call_target="tpu_custom_call" | custom-call | flops 3600000000 | bytes 11832320 | tf_op jit(solution)/shard_map/pallas_call | solution.py:54
  241.8 15.7 %shard_map.348 = (bf16[768,3072]{1,0:T(8,128)(2,1)}, f32[1,3072]{1,0:T(1,128)}, bf16[768,768]{1,0:T(8,128)(2,1)}) custom-call(s32[2]{0:T(128)} %pad_add_fusion.refs_0_.place_ref, bf16[768,768]{1,0:T(8,128)(2,1)} %get-tuple-element.157.refs_1_.dy_ref, bf16[768,3072]{1,0:T(8,128)(2,1)} %get-tuple-element.158.slope_ref, bf16[3072,768]{1,0:T(8,128)(2,1)} %copy-done.10, ...), custom_call_target="tpu_custom_call" | custom-call | flops 6000000000 | bytes 21278720 | tf_op jit(solution)/shard_map/pallas_call | solution.py:54
  257.5 5.0 %all-to-all-start.2 = ((bf16[8,96,768]{2,1,0:T(8,128)(2,1)}), bf16[8,96,768]{2,1,0:T(8,128)(2,1)S(1)}, u32[]{:S(2)}, u32[]{:S(2)}) async-start(bf16[8,96,768]{2,1,0:T(8,128)(2,1)} %bitcast.162), calls=%async_computation.2 | async-start | bytes 2359296 | tf_op jit(solution)/shard_map/all_to_all | solution.py:1307
  265.5 8.4 %shard_map.349 = bf16[832,3072]{1,0:T(8,128)(2,1)} custom-call(bf16[768,768]{1,0:T(8,128)(2,1)} %bitcast.18.x_ref, bf16[768,3072]{1,0:T(8,128)(2,1)} %get-tuple-element.164.dh_ref, f32[1,3072]{1,0:T(1,128)} %get-tuple-element.165.in_bias_ref, f32[1,768]{1,0:T(1,128)} %get-tuple-element.166.out_bias_ref), custom_call_target="tpu_custom_call" | custom-call | flops 3200000000 | bytes 11025408 | tf_op jit(solution)/shard_map/pallas_call | solution.py:54
  274.0 14.4 %all-to-all-done.2 = bf16[8,96,768]{2,1,0:T(8,128)(2,1)S(1)} async-done(((bf16[8,96,768]{2,1,0:T(8,128)(2,1)}), bf16[8,96,768]{2,1,0:T(8,128)(2,1)S(1)}, u32[]{:S(2)}, u32[]{:S(2)}) %all-to-all-start.2) | async-done | bytes 1179680 | tf_op jit(solution)/shard_map/all_to_all | solution.py:1307
  289.4 7.0 %shard_map.350 = (f32[416,768]{1,0:T(8,128)}, f32[8,768]{1,0:T(8,128)}, f32[768,128]{1,0:T(8,128)}) custom-call(f32[416,768]{1,0:T(8,128)} %get-tuple-element.149.x_ref, f32[32,768]{1,0:T(8,128)} %get-tuple-element.141.vec_ref.refs_2_, bf16[768,768]{1,0:T(8,128)(2,1)} %bitcast.161, f32[416,128]{1,0:T(8,128)} %get-tuple-element.176.gate_ref, ...), custom_call_target="tpu_custom_call" | custom-call | flops 2800000000 | bytes 5945856 | tf_op jit(solution)/shard_map/pallas_call | solution.py:54
  296.4 19.2 %shard_map.351 = (f32[416,768]{1,0:T(8,128)}, bf16[416,1152]{1,0:T(8,128)(2,1)}, bf16[416,1152]{1,0:T(8,128)(2,1)}, bf16[416,384]{1,0:T(8,128)(2,1)}, bf16[416,384]{1,0:T(8,128)(2,1)}, /*index=5*/f32[8,768]{1,0:T(8,128)}) custom-call(s32[2]{0:T(128)} %pad_add_fusion.refs_0_.place_ref, f32[416,768]{1,0:T(8,128)} %get-tuple-element.178.up_ref, ...), custom_call_target="tpu_custom_call" | custom-call | flops 7600000000 | bytes 13148160 | tf_op jit(solution)/shard_map/pallas_call | solution.py:54
  315.7 12.9 %shard_map.352 = (f32[416,768]{1,0:T(8,128)}, bf16[416,1536]{1,0:T(8,128)(2,1)}, bf16[416,1536]{1,0:T(8,128)(2,1)}, bf16[416,384]{1,0:T(8,128)(2,1)}, bf16[416,3...) custom-call(s32[2]{0:T(128)} %pad_add_fusion.refs_0_.place_ref, f32[416,768]{1,0:T(8,128)} %get-tuple-element.180.up_ref, ...), custom_call_target="tpu_custom_call" | custom-call | flops 5200000000 | bytes 28594176 | tf_op jit(solution)/shard_map/pallas_call | solution.py:54
  329.7 7.0 %all-to-all-start.3 = ((bf16[8,96,768]{2,1,0:T(8,128)(2,1)}), bf16[8,96,768]{2,1,0:T(8,128)(2,1)}, u32[]{:S(2)}, u32[]{:S(2)}) async-start(bf16[8,96,768]{2,1,0:T(8,128)(2,1)} %bitcast.36), calls=%async_computation.5 | async-start | bytes 2359296 | tf_op jit(solution)/shard_map/all_to_all | solution.py:1307
  337.6 6.8 %shard_map.354 = bf16[768,1536]{1,0:T(8,128)(2,1)} custom-call(bf16[416,768]{1,0:T(8,128)(2,1)} %get-tuple-element.172.refs_0_, bf16[416,1152]{1,0:T(8,128)(2,1)} %get-tuple-element.193.refs_1_, bf16[416,768]{1,0:T(8,128)(2,1)} %collective-permute-done.34.refs_2_, bf16[416,1152]{1,0:T(8,128)(2,1)} %copy-done.30, ...), custom_call_target="tpu_custom_call" | custom-call | flops 2800000000 | bytes 7471104 | tf_op jit(solution)/shard_map/pallas_call | solution.py:54
  346.9 11.7 %shard_map.353 = bf16[6144,384]{1,0:T(8,128)(2,1)} custom-call(bf16[416,768]{1,0:T(8,128)(2,1)} %get-tuple-element.143.hn_ref, bf16[416,768]{1,0:T(8,128)(2,1)} %copy-done.35, bf16[416,1536]{1,0:T(8,128)(2,1)} %get-tuple-element.182.du_ref, bf16[416,1536]{1,0:T(8,128)(2,1)} %copy-done.28, bf16[416,3072]{1,0:T(8,128)(2,1)} %get-tuple-element.170.act_ref, ...), custom_call_target="tpu_custom_call" | custom-call | flops 4400000000 | bytes 14303232 | tf_op jit(solution)/shard_map/pallas_call | solution.py:54
  363.9 18.7 %shard_map.355 = (f32[416,768]{1,0:T(8,128)}, bf16[416,1152]{1,0:T(8,128)(2,1)}, bf16[416,1152]{1,0:T(8,128)(2,1)}, bf16[416,384]{1,0:T(8,128)(2,1)}, bf16[416,384]{1,0:T(8,128)(2,1)}, /*index=5*/f32[768,128]{1,0:T(8,128)}) custom-call(s32[2]{0:T(128)} %pad_add_fusion.refs_0_.place_ref, f32[416,768]{1,0:T(8,128)} %get-tuple-element.200.up_ref, ...), custom_call_target="tpu_custom_call" | custom-call | flops 7600000000 | bytes 14389248 | tf_op jit(solution)/shard_map/pallas_call | solution.py:54
  394.8 7.1 %shard_map.356 = bf16[768,1664]{1,0:T(8,128)(2,1)} custom-call(bf16[416,768]{1,0:T(8,128)(2,1)} %get-tuple-element.137.refs_0_, bf16[416,1152]{1,0:T(8,128)(2,1)} %get-tuple-element.211.refs_1_, bf16[416,768]{1,0:T(8,128)(2,1)} %copy-done.34, bf16[416,1152]{1,0:T(8,128)(2,1)} %collective-permute-done.46.refs_3_, ...), custom_call_target="tpu_custom_call" | custom-call | flops 2800000000 | bytes 8060928 | tf_op jit(solution)/shard_map/pallas_call | solution.py:54
  405.3 2.3 collective-permute-start.53
  407.6 3.7 collective-permute-done.53
  413.7 5.4 %collective-permute-done.54 = bf16[48,1536]{1,0:T(8,128)(2,1)S(1)} collective-permute-done((bf16[48,1536]{1,0:T(8,128)(2,1)}, bf16[48,1536]{1,0:T(8,128)(2,1)S(1)}, u32[]{:S(2)}, u32[]{:S(2)}) %collective-permute-start.54) | collective-permute-done | bytes 147488 | tf_op jit(solution)/shard_map/ppermute | solution.py:1057
  419.1 4.2 collective-permute-done.48
  426.2 3.5 collective-permute-start.65
  429.6 2.4 fusion.1
  441.1 3.9 shard_map.357
  449.1 13.0 %collective-permute-done.59 = bf16[384,384]{1,0:T(8,128)(2,1)} collective-permute-done((bf16[384,384]{1,0:T(8,128)(2,1)}, bf16[384,384]{1,0:T(8,128)(2,1)}, u32[]{:S(2)}, u32[]{:S(2)}) %collective-permute-start.59) | collective-permute-done | bytes 294944 | tf_op jit(solution)/shard_map/ppermute | solution.py:1057
  469.5 3.5 collective-permute-done.60
  475.0 7.5 %collective-permute-done.62 = bf16[48,1664]{1,0:T(8,128)(2,1)S(1)} collective-permute-done((bf16[48,1664]{1,0:T(8,128)(2,1)S(1)}, bf16[48,1664]{1,0:T(8,128)(2,1)S(1)}, u32[]{:S(2)}, u32[]{:S(2)}) %collective-permute-start.62) | collective-permute-done | bytes 159776 | tf_op jit(solution)/shard_map/ppermute | solution.py:1057
  (351 shorter events, 121.7 us)
Async XLA Ops:
  7.3 127.6 %all-gather.2.cloned.1.call-start = ((), (), s32[]{:S(2)}) async-start(), calls=%async_computation.6 | async-start | bytes 9732096 | tf_op jit(solution)/shard_map/all_gather | solution.py:1278
  12.5 27.6 %collective-permute-start.4 = (bf16[960]{0:T(1024)(128)(2,1)S(1)}, bf16[960]{0:T(1024)(128)(2,1)S(1)}, u32[]{:S(2)}, u32[]{:S(2)}) collective-permute-start(bf16[960]{0:T(1024)(128)(2,1)S(1)} %pad_maximum_fusion.13), channel_id=1, source_target_pairs={{0,8},{8,0},{16,24},{24,16},{1,9},{9,1},{17,25},{25,17},{2,10},{10... | collective-permute-start | bytes 5768 | tf_op jit(solution)/shard_map/ppermute | solution.py:1057
  13.8 26.3 %collective-permute-start.5 = (bf16[960]{0:T(1024)(128)(2,1)S(1)}, bf16[960]{0:T(1024)(128)(2,1)S(1)}, u32[]{:S(2)}, u32[]{:S(2)}) collective-permute-start(bf16[960]{0:T(1024)(128)(2,1)S(1)} %pad_maximum_fusion.13), channel_id=1, source_target_pairs={{0,16},{8,24},{16,0},{24,8},{1,17},{9,25},{17,1},{25,9},{2,18},{10... | collective-permute-start | bytes 5768 | tf_op jit(solution)/shard_map/ppermute | solution.py:1057
  15.0 25.1 %collective-permute-start.6 = (bf16[960]{0:T(1024)(128)(2,1)S(1)}, bf16[960]{0:T(1024)(128)(2,1)S(1)}, u32[]{:S(2)}, u32[]{:S(2)}) collective-permute-start(bf16[960]{0:T(1024)(128)(2,1)S(1)} %pad_maximum_fusion.13), channel_id=1, source_target_pairs={{0,24},{8,16},{16,8},{24,0},{1,25},{9,17},{17,9},{25,1},{2,26},{10... | collective-permute-start | bytes 5768 | tf_op jit(solution)/shard_map/ppermute | solution.py:1057
  23.4 16.5 %collective-permute-start.2 = (bf16[48,1664]{1,0:T(8,128)(2,1)S(1)}, bf16[48,1664]{1,0:T(8,128)(2,1)S(1)}, u32[]{:S(2)}, u32[]{:S(2)}) collective-permute-start(bf16[48,1664]{1,0:T(8,128)(2,1)S(1)} %maximum_select_fusion.7), channel_id=1, source_target_pairs={{0,4},{1,5},{2,6},{3,7},{4,0},{5,1},{6,2},{7,3},{8,12},{9,13},{10,... | collective-permute-start | bytes 479240 | tf_op jit(solution)/shard_map/ppermute | solution.py:1057
  40.1 18.7 %collective-permute-start.10 = (bf16[48,1536]{1,0:T(8,128)(2,1)S(1)}, bf16[48,1536]{1,0:T(8,128)(2,1)S(1)}, u32[]{:S(2)}, u32[]{:S(2)}) collective-permute-start(bf16[48,1536]{1,0:T(8,128)(2,1)S(1)} %maximum_select_fusion.8), channel_id=1, source_target_pairs={{0,6},{1,7},{2,4},{3,5},{4,2},{5,3},{6,0},{7,1},{8,14},{9,15},{10,... | collective-permute-start | bytes 442376 | tf_op jit(solution)/shard_map/ppermute | solution.py:1057
  40.6 19.9 %collective-permute-start.11 = (bf16[48,1536]{1,0:T(8,128)(2,1)S(1)}, bf16[48,1536]{1,0:T(8,128)(2,1)S(1)}, u32[]{:S(2)}, u32[]{:S(2)}) collective-permute-start(bf16[48,1536]{1,0:T(8,128)(2,1)S(1)} %maximum_select_fusion.8), channel_id=1, source_target_pairs={{0,4},{1,5},{2,6},{3,7},{4,0},{5,1},{6,2},{7,3},{8,12},{9,13},{10,... | collective-permute-start | bytes 442376 | tf_op jit(solution)/shard_map/ppermute | solution.py:1057
  45.0 13.8 %collective-permute-start.12 = (bf16[48,1536]{1,0:T(8,128)(2,1)S(1)}, bf16[48,1536]{1,0:T(8,128)(2,1)S(1)}, u32[]{:S(2)}, u32[]{:S(2)}) collective-permute-start(bf16[48,1536]{1,0:T(8,128)(2,1)S(1)} %maximum_select_fusion.8), channel_id=1, source_target_pairs={{0,2},{1,3},{2,0},{3,1},{4,6},{5,7},{6,4},{7,5},{8,10},{9,11},{10,... | collective-permute-start | bytes 442376 | tf_op jit(solution)/shard_map/ppermute | solution.py:1057
  45.0 23.1 %collective-permute-start.8 = (bf16[192,1664]{1,0:T(8,128)(2,1)S(1)}, bf16[192,1664]{1,0:T(8,128)(2,1)S(1)}, u32[]{:S(2)}, u32[]{:S(2)}) collective-permute-start(bf16[192,1664]{1,0:T(8,128)(2,1)S(1)} %maximum_select_fusion), channel_id=1, source_target_pairs={{0,8},{8,0},{16,24},{24,16},{1,9},{9,1},{17,25},{25,17},{2,10},{10... | collective-permute-start | bytes 1916936 | tf_op jit(solution)/shard_map/ppermute | solution.py:1057
  46.1 22.0 %collective-permute-start.9 = (bf16[192,1664]{1,0:T(8,128)(2,1)S(1)}, bf16[192,1664]{1,0:T(8,128)(2,1)S(1)}, u32[]{:S(2)}, u32[]{:S(2)}) collective-permute-start(bf16[192,1664]{1,0:T(8,128)(2,1)S(1)} %maximum_select_fusion), channel_id=1, source_target_pairs={{0,16},{8,24},{16,0},{24,8},{1,17},{9,25},{17,1},{25,9},{2,18},{10... | collective-permute-start | bytes 1916936 | tf_op jit(solution)/shard_map/ppermute | solution.py:1057
  78.6 16.4 %collective-permute-start.15 = (bf16[768,1664]{1,0:T(8,128)(2,1)}, bf16[768,1664]{1,0:T(8,128)(2,1)}, u32[]{:S(2)}, u32[]{:S(2)}) collective-permute-start(bf16[768,1664]{1,0:T(8,128)(2,1)} %constant_dynamic-update-slice_fusion.2.refs_2_.refs_5_), channel_id=1, source_target_pairs={{0,1},{1,0},{2,3},{3,2},{4,5},{5,4},{6,7},{7,6},{8,9},{9,8},{10,11... | collective-permute-start | bytes 7667720 | tf_op jit(solution)/shard_map/ppermute | solution.py:1057
  92.0 17.6 %collective-permute-start.16 = (bf16[192,1536]{1,0:T(8,128)(2,1)S(1)}, bf16[192,1536]{1,0:T(8,128)(2,1)S(1)}, u32[]{:S(2)}, u32[]{:S(2)}) collective-permute-start(bf16[192,1536]{1,0:T(8,128)(2,1)S(1)} %maximum_select_fusion.1), channel_id=1, source_target_pairs={{0,8},{8,0},{16,24},{24,16},{1,9},{9,1},{17,25},{25,17},{2,10},{10... | collective-permute-start | bytes 1769480 | tf_op jit(solution)/shard_map/ppermute | solution.py:1057
  92.0 17.8 %collective-permute-start.17 = (bf16[192,1536]{1,0:T(8,128)(2,1)S(1)}, bf16[192,1536]{1,0:T(8,128)(2,1)S(1)}, u32[]{:S(2)}, u32[]{:S(2)}) collective-permute-start(bf16[192,1536]{1,0:T(8,128)(2,1)S(1)} %maximum_select_fusion.1), channel_id=1, source_target_pairs={{0,16},{8,24},{16,0},{24,8},{1,17},{9,25},{17,1},{25,9},{2,18},{10... | collective-permute-start | bytes 1769480 | tf_op jit(solution)/shard_map/ppermute | solution.py:1057
  120.3 25.6 %collective-permute-start.21 = (bf16[768,1536]{1,0:T(8,128)(2,1)}, bf16[768,1536]{1,0:T(8,128)(2,1)}, u32[]{:S(2)}, u32[]{:S(2)}) collective-permute-start(bf16[768,1536]{1,0:T(8,128)(2,1)} %constant_dynamic-update-slice_fusion.7.refs_3_.refs_0_), channel_id=1, source_target_pairs={{0,1},{1,0},{2,3},{3,2},{4,5},{5,4},{6,7},{7,6},{8,9},{9,8},{10,11... | collective-permute-start | bytes 7077896 | tf_op jit(solution)/shard_map/ppermute | solution.py:1057
  122.0 34.3 %all-to-all-start = ((bf16[8,96,768]{2,1,0:T(8,128)(2,1)}), bf16[8,96,768]{2,1,0:T(8,128)(2,1)}, u32[]{:S(2)}, u32[]{:S(2)}) async-start(bf16[8,96,768]{2,1,0:T(8,128)(2,1)} %bitcast.14), calls=%async_computation | async-start | bytes 2359296 | tf_op jit(solution)/shard_map/all_to_all | solution.py:1307
  129.5 39.5 %collective-permute-start.26 = (bf16[768,768]{1,0:T(8,128)(2,1)}, bf16[768,768]{1,0:T(8,128)(2,1)S(1)}, u32[]{:S(2)}, u32[]{:S(2)}) collective-permute-start(bf16[768,768]{1,0:T(8,128)(2,1)} %bitcast.12), channel_id=1, source_target_pairs={{0,8},{8,0},{16,24},{24,16},{1,9},{9,1},{17,25},{25,17},{2,10},{10... | collective-permute-start | bytes 3538952 | tf_op jit(solution)/shard_map/ppermute | solution.py:1057
  129.7 39.2 %collective-permute-start.27 = (bf16[768,768]{1,0:T(8,128)(2,1)}, bf16[768,768]{1,0:T(8,128)(2,1)S(1)}, u32[]{:S(2)}, u32[]{:S(2)}) collective-permute-start(bf16[768,768]{1,0:T(8,128)(2,1)} %bitcast.12), channel_id=1, source_target_pairs={{0,16},{8,24},{16,0},{24,8},{1,17},{9,25},{17,1},{25,9},{2,18},{10... | collective-permute-start | bytes 3538952 | tf_op jit(solution)/shard_map/ppermute | solution.py:1057
  131.0 52.6 %collective-permute-start.22 = (bf16[192,3072]{1,0:T(8,128)(2,1)}, bf16[192,3072]{1,0:T(8,128)(2,1)}, u32[]{:S(2)}, u32[]{:S(2)}) collective-permute-start(bf16[192,3072]{1,0:T(8,128)(2,1)} %bitcast.11), channel_id=1, source_target_pairs={{0,8},{8,0},{16,24},{24,16},{1,9},{9,1},{17,25},{25,17},{2,10},{10... | collective-permute-start | bytes 3538952 | tf_op jit(solution)/shard_map/ppermute | solution.py:1057
  132.0 50.1 %collective-permute-start.23 = (bf16[192,3072]{1,0:T(8,128)(2,1)}, bf16[192,3072]{1,0:T(8,128)(2,1)S(1)}, u32[]{:S(2)}, u32[]{:S(2)}) collective-permute-start(bf16[192,3072]{1,0:T(8,128)(2,1)} %bitcast.11), channel_id=1, source_target_pairs={{0,16},{8,24},{16,0},{24,8},{1,17},{9,25},{17,1},{25,9},{2,18},{10... | collective-permute-start | bytes 3538952 | tf_op jit(solution)/shard_map/ppermute | solution.py:1057
  161.0 48.3 %all-to-all-start.1 = ((bf16[8,96,768]{2,1,0:T(8,128)(2,1)}), bf16[8,96,768]{2,1,0:T(8,128)(2,1)}, u32[]{:S(2)}, u32[]{:S(2)}) async-start(bf16[8,96,768]{2,1,0:T(8,128)(2,1)} %bitcast.160), calls=%async_computation.1 | async-start | bytes 2359296 | tf_op jit(solution)/shard_map/all_to_all | solution.py:1307
  167.2 121.2 %reduce-scatter.3.cloned.1.call-start = ((), (), s32[]{:S(2)}) async-start(), calls=%async_computation.7 | async-start | bytes 5898240 | tf_op jit(solution)/shard_map/reduce_scatter | solution.py:1342
  168.9 26.0 %collective-permute-start.28 = (bf16[384,768]{1,0:T(8,128)(2,1)S(1)}, bf16[384,768]{1,0:T(8,128)(2,1)S(1)}, u32[]{:S(2)}, u32[]{:S(2)}) collective-permute-start(bf16[384,768]{1,0:T(8,128)(2,1)S(1)} %slice.339), channel_id=1, source_target_pairs={{0,8},{8,0},{16,24},{24,16},{1,9},{9,1},{17,25},{25,17},{2,10},{10... | collective-permute-start | bytes 1769480 | tf_op jit(solution)/shard_map/ppermute | solution.py:1057
  169.1 25.8 %collective-permute-start.29 = (bf16[384,768]{1,0:T(8,128)(2,1)S(1)}, bf16[384,768]{1,0:T(8,128)(2,1)S(1)}, u32[]{:S(2)}, u32[]{:S(2)}) collective-permute-start(bf16[384,768]{1,0:T(8,128)(2,1)S(1)} %slice.340), channel_id=1, source_target_pairs={{0,16},{8,24},{16,0},{24,8},{1,17},{9,25},{17,1},{25,9},{2,18},{10... | collective-permute-start | bytes 1769480 | tf_op jit(solution)/shard_map/ppermute | solution.py:1057
  182.2 25.3 %collective-permute-start.24 = (bf16[96,3072]{1,0:T(8,128)(2,1)S(1)}, bf16[96,3072]{1,0:T(8,128)(2,1)S(1)}, u32[]{:S(2)}, u32[]{:S(2)}) collective-permute-start(bf16[96,3072]{1,0:T(8,128)(2,1)S(1)} %slice.337), channel_id=1, source_target_pairs={{0,8},{8,0},{16,24},{24,16},{1,9},{9,1},{17,25},{25,17},{2,10},{10... | collective-permute-start | bytes 1769480 | tf_op jit(solution)/shard_map/ppermute | solution.py:1057
  184.7 23.7 %collective-permute-start.25 = (bf16[96,3072]{1,0:T(8,128)(2,1)S(1)}, bf16[96,3072]{1,0:T(8,128)(2,1)S(1)}, u32[]{:S(2)}, u32[]{:S(2)}) collective-permute-start(bf16[96,3072]{1,0:T(8,128)(2,1)S(1)} %slice.338), channel_id=1, source_target_pairs={{0,16},{8,24},{16,0},{24,8},{1,17},{9,25},{17,1},{25,9},{2,18},{10... | collective-permute-start | bytes 1769480 | tf_op jit(solution)/shard_map/ppermute | solution.py:1057
  230.3 43.6 %collective-permute-start.31 = (bf16[416,3072]{1,0:T(8,128)(2,1)}, bf16[416,3072]{1,0:T(8,128)(2,1)}, u32[]{:S(2)}, u32[]{:S(2)}) collective-permute-start(bf16[416,3072]{1,0:T(8,128)(2,1)} %get-tuple-element.170.act_ref), channel_id=1, source_target_pairs={{0,1},{1,0},{2,3},{3,2},{4,5},{5,4},{6,7},{7,6},{8,9},{9,8},{10,11... | collective-permute-start | bytes 7667720 | tf_op jit(solution)/shard_map/ppermute | solution.py:1057
  257.5 30.9 %all-to-all-start.2 = ((bf16[8,96,768]{2,1,0:T(8,128)(2,1)}), bf16[8,96,768]{2,1,0:T(8,128)(2,1)S(1)}, u32[]{:S(2)}, u32[]{:S(2)}) async-start(bf16[8,96,768]{2,1,0:T(8,128)(2,1)} %bitcast.162), calls=%async_computation.2 | async-start | bytes 2359296 | tf_op jit(solution)/shard_map/all_to_all | solution.py:1307
  262.5 123.7 %reduce-scatter.5.cloned.1.call-start = ((), (), s32[]{:S(2)}) async-start(), calls=%async_computation.8 | async-start | bytes 6389760 | tf_op jit(solution)/shard_map/reduce_scatter | solution.py:1357
  263.0 10.9 %collective-permute-start.33 = (bf16[416,768]{1,0:T(8,128)(2,1)S(1)}, bf16[416,768]{1,0:T(8,128)(2,1)}, u32[]{:S(2)}, u32[]{:S(2)}) collective-permute-start(bf16[416,768]{1,0:T(8,128)(2,1)S(1)} %copy-done.32), channel_id=1, source_target_pairs={{0,1},{1,0},{2,3},{3,2},{4,5},{5,4},{6,7},{7,6},{8,9},{9,8},{10,11... | collective-permute-start | bytes 1916936 | tf_op jit(solution)/shard_map/ppermute | solution.py:1057
  329.7 84.0 %all-to-all-start.3 = ((bf16[8,96,768]{2,1,0:T(8,128)(2,1)}), bf16[8,96,768]{2,1,0:T(8,128)(2,1)}, u32[]{:S(2)}, u32[]{:S(2)}) async-start(bf16[8,96,768]{2,1,0:T(8,128)(2,1)} %bitcast.36), calls=%async_computation.5 | async-start | bytes 2359296 | tf_op jit(solution)/shard_map/all_to_all | solution.py:1307
  345.8 12.8 %collective-permute-start.40 = (bf16[2,48,1536]{2,1,0:T(8,128)(2,1)S(1)}, bf16[2,48,1536]{2,1,0:T(8,128)(2,1)S(1)}, u32[]{:S(2)}, u32[]{:S(2)}) collective-permute-start(bf16[2,48,1536]{2,1,0:T(8,128)(2,1)S(1)} %get-tuple-element.314), channel_id=1, source_target_pairs={{0,8},{8,0},{16,24},{24,16},{1,9},{9,1},{17,25},{25,17},{2,10},{10... | collective-permute-start | bytes 884744 | tf_op jit(solution)/shard_map/ppermute | solution.py:1057
  345.8 12.8 %collective-permute-start.41 = (bf16[2,48,1536]{2,1,0:T(8,128)(2,1)S(1)}, bf16[2,48,1536]{2,1,0:T(8,128)(2,1)S(1)}, u32[]{:S(2)}, u32[]{:S(2)}) collective-permute-start(bf16[2,48,1536]{2,1,0:T(8,128)(2,1)S(1)} %get-tuple-element.315), channel_id=1, source_target_pairs={{0,16},{8,24},{16,0},{24,8},{1,17},{9,25},{17,1},{25,9},{2,18},{10... | collective-permute-start | bytes 884744 | tf_op jit(solution)/shard_map/ppermute | solution.py:1057
  358.8 25.9 %collective-permute-start.45 = (bf16[4,48,1536]{2,1,0:T(8,128)(2,1)S(1)}, bf16[4,48,1536]{2,1,0:T(8,128)(2,1)}, u32[]{:S(2)}, u32[]{:S(2)}) collective-permute-start(bf16[4,48,1536]{2,1,0:T(8,128)(2,1)S(1)} %pad_maximum_fusion.5), channel_id=1, source_target_pairs={{0,16},{8,24},{16,0},{24,8},{1,17},{9,25},{17,1},{25,9},{2,18},{10... | collective-permute-start | bytes 1769480 | tf_op jit(solution)/shard_map/ppermute | solution.py:1057
  359.6 25.3 %collective-permute-start.44 = (bf16[4,48,1536]{2,1,0:T(8,128)(2,1)S(1)}, bf16[4,48,1536]{2,1,0:T(8,128)(2,1)}, u32[]{:S(2)}, u32[]{:S(2)}) collective-permute-start(bf16[4,48,1536]{2,1,0:T(8,128)(2,1)S(1)} %pad_maximum_fusion.4), channel_id=1, source_target_pairs={{0,8},{8,0},{16,24},{24,16},{1,9},{9,1},{17,25},{25,17},{2,10},{10... | collective-permute-start | bytes 1769480 | tf_op jit(solution)/shard_map/ppermute | solution.py:1057
  362.8 23.5 %collective-permute-start.42 = (bf16[2,384,384]{2,1,0:T(8,128)(2,1)S(1)}, bf16[2,384,384]{2,1,0:T(8,128)(2,1)}, u32[]{:S(2)}, u32[]{:S(2)}) collective-permute-start(bf16[2,384,384]{2,1,0:T(8,128)(2,1)S(1)} %get-tuple-element.302), channel_id=1, source_target_pairs={{0,8},{8,0},{16,24},{24,16},{1,9},{9,1},{17,25},{25,17},{2,10},{10... | collective-permute-start | bytes 1769480 | tf_op jit(solution)/shard_map/ppermute | solution.py:1057
  363.0 23.2 %collective-permute-start.43 = (bf16[2,384,384]{2,1,0:T(8,128)(2,1)S(1)}, bf16[2,384,384]{2,1,0:T(8,128)(2,1)}, u32[]{:S(2)}, u32[]{:S(2)}) collective-permute-start(bf16[2,384,384]{2,1,0:T(8,128)(2,1)S(1)} %get-tuple-element.303), channel_id=1, source_target_pairs={{0,16},{8,24},{16,0},{24,8},{1,17},{9,25},{17,1},{25,9},{2,18},{10... | collective-permute-start | bytes 1769480 | tf_op jit(solution)/shard_map/ppermute | solution.py:1057
  382.6 12.3 %collective-permute-start.46 = (bf16[416,1152]{1,0:T(8,128)(2,1)}, bf16[416,1152]{1,0:T(8,128)(2,1)}, u32[]{:S(2)}, u32[]{:S(2)}) collective-permute-start(bf16[416,1152]{1,0:T(8,128)(2,1)} %get-tuple-element.213), channel_id=1, source_target_pairs={{0,1},{1,0},{2,3},{3,2},{4,5},{5,4},{6,7},{7,6},{8,9},{9,8},{10,11... | collective-permute-start | bytes 2875400 | tf_op jit(solution)/shard_map/ppermute | solution.py:1057
  389.6 33.8 %collective-permute-start.51 = (bf16[4,384,384]{2,1,0:T(8,128)(2,1)}, bf16[4,384,384]{2,1,0:T(8,128)(2,1)}, u32[]{:S(2)}, u32[]{:S(2)}) collective-permute-start(bf16[4,384,384]{2,1,0:T(8,128)(2,1)} %pad_maximum_fusion.1), channel_id=1, source_target_pairs={{0,16},{8,24},{16,0},{24,8},{1,17},{9,25},{17,1},{25,9},{2,18},{10... | collective-permute-start | bytes 3538952 | tf_op jit(solution)/shard_map/ppermute | solution.py:1057
  391.2 32.1 %collective-permute-start.50 = (bf16[4,384,384]{2,1,0:T(8,128)(2,1)}, bf16[4,384,384]{2,1,0:T(8,128)(2,1)}, u32[]{:S(2)}, u32[]{:S(2)}) collective-permute-start(bf16[4,384,384]{2,1,0:T(8,128)(2,1)} %pad_maximum_fusion), channel_id=1, source_target_pairs={{0,8},{8,0},{16,24},{24,16},{1,9},{9,1},{17,25},{25,17},{2,10},{10... | collective-permute-start | bytes 3538952 | tf_op jit(solution)/shard_map/ppermute | solution.py:1057
  404.3 19.0 %collective-permute-start.48 = (bf16[2,48,1664]{2,1,0:T(8,128)(2,1)}, bf16[2,48,1664]{2,1,0:T(8,128)(2,1)S(1)}, u32[]{:S(2)}, u32[]{:S(2)}) collective-permute-start(bf16[2,48,1664]{2,1,0:T(8,128)(2,1)} %get-tuple-element.307), channel_id=1, source_target_pairs={{0,8},{8,0},{16,24},{24,16},{1,9},{9,1},{17,25},{25,17},{2,10},{10... | collective-permute-start | bytes 958472 | tf_op jit(solution)/shard_map/ppermute | solution.py:1057
  404.5 18.8 %collective-permute-start.49 = (bf16[2,48,1664]{2,1,0:T(8,128)(2,1)}, bf16[2,48,1664]{2,1,0:T(8,128)(2,1)S(1)}, u32[]{:S(2)}, u32[]{:S(2)}) collective-permute-start(bf16[2,48,1664]{2,1,0:T(8,128)(2,1)} %get-tuple-element.309), channel_id=1, source_target_pairs={{0,16},{8,24},{16,0},{24,8},{1,17},{9,25},{17,1},{25,9},{2,18},{10... | collective-permute-start | bytes 958472 | tf_op jit(solution)/shard_map/ppermute | solution.py:1057
  426.2 19.4 %collective-permute-start.65 = (bf16[24,1536]{1,0:T(8,128)(2,1)S(1)}, bf16[24,1536]{1,0:T(8,128)(2,1)S(1)}, u32[]{:S(2)}, u32[]{:S(2)}) collective-permute-start(bf16[24,1536]{1,0:T(8,128)(2,1)S(1)} %dynamic-slice_convert_fusion.1), channel_id=1, source_target_pairs={{0,1},{1,0},{2,3},{3,2},{4,5},{5,4},{6,7},{7,6},{8,9},{9,8},{10,11... | collective-permute-start | bytes 221192 | tf_op jit(solution)/shard_map/ppermute | solution.py:1057
  433.0 15.3 %collective-permute-start.57 = (bf16[384,384]{1,0:T(8,128)(2,1)}, bf16[384,384]{1,0:T(8,128)(2,1)}, u32[]{:S(2)}, u32[]{:S(2)}) collective-permute-start(bf16[384,384]{1,0:T(8,128)(2,1)} %get-tuple-element.318), channel_id=1, source_target_pairs={{0,2},{1,3},{2,0},{3,1},{4,6},{5,7},{6,4},{7,5},{8,10},{9,11},{10,... | collective-permute-start | bytes 884744 | tf_op jit(solution)/shard_map/ppermute | solution.py:1057
  434.7 14.4 %collective-permute-start.58 = (bf16[384,384]{1,0:T(8,128)(2,1)}, bf16[384,384]{1,0:T(8,128)(2,1)}, u32[]{:S(2)}, u32[]{:S(2)}) collective-permute-start(bf16[384,384]{1,0:T(8,128)(2,1)} %get-tuple-element.317), channel_id=1, source_target_pairs={{0,4},{1,5},{2,6},{3,7},{4,0},{5,1},{6,2},{7,3},{8,12},{9,13},{10,... | collective-permute-start | bytes 884744 | tf_op jit(solution)/shard_map/ppermute | solution.py:1057
  435.4 26.6 %collective-permute-start.59 = (bf16[384,384]{1,0:T(8,128)(2,1)}, bf16[384,384]{1,0:T(8,128)(2,1)}, u32[]{:S(2)}, u32[]{:S(2)}) collective-permute-start(bf16[384,384]{1,0:T(8,128)(2,1)} %get-tuple-element.316), channel_id=1, source_target_pairs={{0,6},{1,7},{2,4},{3,5},{4,2},{5,3},{6,0},{7,1},{8,14},{9,15},{10,... | collective-permute-start | bytes 884744 | tf_op jit(solution)/shard_map/ppermute | solution.py:1057
  436.1 26.0 %collective-permute-start.56 = (bf16[4,48,1664]{2,1,0:T(8,128)(2,1)S(1)}, bf16[4,48,1664]{2,1,0:T(8,128)(2,1)S(1)}, u32[]{:S(2)}, u32[]{:S(2)}) collective-permute-start(bf16[4,48,1664]{2,1,0:T(8,128)(2,1)S(1)} %pad_maximum_fusion.3), channel_id=1, source_target_pairs={{0,16},{8,24},{16,0},{24,8},{1,17},{9,25},{17,1},{25,9},{2,18},{10... | collective-permute-start | bytes 1916936 | tf_op jit(solution)/shard_map/ppermute | solution.py:1057
  445.6 16.5 %collective-permute-start.55 = (bf16[4,48,1664]{2,1,0:T(8,128)(2,1)S(1)}, bf16[4,48,1664]{2,1,0:T(8,128)(2,1)S(1)}, u32[]{:S(2)}, u32[]{:S(2)}) collective-permute-start(bf16[4,48,1664]{2,1,0:T(8,128)(2,1)S(1)} %pad_maximum_fusion.2), channel_id=1, source_target_pairs={{0,8},{8,0},{16,24},{24,16},{1,9},{9,1},{17,25},{25,17},{2,10},{10... | collective-permute-start | bytes 1916936 | tf_op jit(solution)/shard_map/ppermute | solution.py:1057
  467.3 15.2 %collective-permute-start.62 = (bf16[48,1664]{1,0:T(8,128)(2,1)S(1)}, bf16[48,1664]{1,0:T(8,128)(2,1)S(1)}, u32[]{:S(2)}, u32[]{:S(2)}) collective-permute-start(bf16[48,1664]{1,0:T(8,128)(2,1)S(1)} %get-tuple-element.320), channel_id=1, source_target_pairs={{0,6},{1,7},{2,4},{3,5},{4,2},{5,3},{6,0},{7,1},{8,14},{9,15},{10,... | collective-permute-start | bytes 479240 | tf_op jit(solution)/shard_map/ppermute | solution.py:1057
  (62 other events, 496.0 us)
Sparse Core Ops, SparseCore 0:
  12.6 100.7 all-gather.1
  229.8 57.7 reduce-scatter.2
  290.6 60.7 reduce-scatter.4
